TPU v7x, 32 devices: a whole 2x2x4 slice. The times are simulated.
32 devices in a mesh: ctx: 4 (over y, x), fsdp: 8 (over z, core).
Axes of the slice: x: 2, y: 2, z: 4, core: 2. Of those that a mesh axis runs over, the one named last changes fastest.
Arguments:
- tokens: bfloat16 [16384, 2048], P(('ctx', 'fsdp')), may hold values from -6 to 6
- cotangent: float32 [16384, 2048], P(('ctx', 'fsdp')), may hold values from -6 to 6
- lengths: int32 [8, 2], P('fsdp'), may hold values from 8 to 8, as said below
- span_place: int32 [8, 16], P('fsdp'), may hold values from 0 to 15, as said below
- ln1_gain: float32 [2048], P('fsdp'), may hold values from 0.1 to 1.9
- ln1_shift: float32 [2048], P('fsdp'), may hold values from -2.5 to 2.5
- qkv_weight: float32 [2048, 6144], P('fsdp'), may hold values from -0.125 to 0.125
- q_bias: float32 [2048], P('fsdp'), may hold values from -2.5 to 2.5
- v_bias: float32 [2048], P('fsdp'), may hold values from -2.5 to 2.5
- out_weight: float32 [2048, 2048], P('fsdp'), may hold values from -0.5 to 0.5
- out_bias: float32 [2048], P('fsdp'), may hold values from -2.5 to 2.5
- ln2_gain: float32 [2048], P('fsdp'), may hold values from 0.1 to 1.9
- ln2_shift: float32 [2048], P('fsdp'), may hold values from -2.5 to 2.5
- up_weight: float32 [2048, 8192], P('fsdp'), may hold values from -0.125 to 0.125
- up_bias: float32 [8192], P('fsdp'), may hold values from -3 to 3
- down_weight: float32 [8192, 2048], P('fsdp'), may hold values from -0.0625 to 0.0625
- down_bias: float32 [2048], P('fsdp'), may hold values from -2.5 to 2.5
Outputs:
- mixed: float32 [16384, 2048], P(('ctx', 'fsdp'))
- input_grad: float32 [16384, 2048], P(('ctx', 'fsdp'))
- ln1_gain_grad: float32 [2048], P('fsdp')
- ln1_shift_grad: float32 [2048], P('fsdp')
- qkv_weight_grad: float32 [2048, 6144], P('fsdp')
- q_bias_grad: float32 [2048], P('fsdp')
- v_bias_grad: float32 [2048], P('fsdp')
- out_weight_grad: float32 [2048, 2048], P('fsdp')
- out_bias_grad: float32 [2048], P('fsdp')
- ln2_gain_grad: float32 [2048], P('fsdp')
- ln2_shift_grad: float32 [2048], P('fsdp')
- up_weight_grad: float32 [2048, 8192], P('fsdp')
- up_bias_grad: float32 [8192], P('fsdp')
- down_weight_grad: float32 [8192, 2048], P('fsdp')
- down_bias_grad: float32 [2048], P('fsdp')
Inputs may be any that keep to these rules, and one draw needn't show every extreme that they name: Each row holds two lengths in blocks, each 8 or more, that sum to 16; the first is at least as long as the second; in some row the first is exactly 8. `span_place`: each row is a permutation of the 16 blocks of a group.
All inputs are finite; a program needn't handle non-finite values.
Results may differ from a plain program's by a relative error of at most 0.02.
Values may be sent and summed in bfloat16 or wider, within the bound.
A program may use at most 512 MiB of HBM per device.

v0:
```python
import math

import jax
import jax.numpy as jnp
from jax import lax
from jax.sharding import PartitionSpec as P

HEADS = 16
SPAN = 128


norm_eps = 1e-05
gelu_coef = 0.7978845608028654


def layer_norm(values, gain, shift):
    center = values - jnp.mean(values, axis=-1, keepdims=True)
    spread = jnp.mean(center * center, axis=-1, keepdims=True)
    return center * lax.rsqrt(spread + norm_eps) * gain + shift


def gelu_tanh(values):
    return (
        0.5 * values * (1.0 + jnp.tanh(gelu_coef * (values + 0.044715 * values * values * values)))
    )


def head_slopes():
    return 2.0 ** (-8.0 * (jnp.arange(HEADS, dtype=jnp.float32) + 1.0) / HEADS)


def token_places(place_row, len_row, first, count):
    index = first + jnp.arange(count, dtype=jnp.int32)
    span_index = index // SPAN
    table = jnp.arange(place_row.shape[0], dtype=jnp.int32)
    placed = jnp.sum(
        jnp.where(span_index[:, None] == table[None, :], place_row[None, :], 0), axis=1
    )
    packed = placed * SPAN + index % SPAN
    starts = (jnp.cumsum(len_row) - len_row) * SPAN
    member = jnp.sum((packed[:, None] >= starts[None, :]).astype(jnp.int32), axis=1)
    return (packed, member)


def attention_scores(queries, keys, query_places, key_places):
    query_pos, query_seq = query_places
    key_pos, key_seq = key_places
    scale = 1.0 / math.sqrt(queries.shape[2])
    scores = jnp.einsum("qhd,khd->hqk", queries, keys, preferred_element_type=jnp.float32) * scale
    gap = (query_pos[:, None] - key_pos[None, :]).astype(jnp.float32)
    scores = scores - head_slopes()[:, None, None] * gap[None, :, :]
    allowed = (query_seq[:, None] == key_seq[None, :]) & (key_pos[None, :] <= query_pos[:, None])
    return jnp.where(allowed[None, :, :], scores, -1e30)


def product(left, right):
    return jnp.dot(left, right, preferred_element_type=jnp.float32)


def per_device(
    tokens,
    cotangent,
    lengths,
    span_place,
    ln1_gain,
    ln1_shift,
    qkv_weight,
    q_bias,
    v_bias,
    out_weight,
    out_bias,
    ln2_gain,
    ln2_shift,
    up_weight,
    up_bias,
    down_weight,
    down_bias,
):
    rows, width = tokens.shape
    cycle_size = lax.axis_size("ctx")
    cycle_rank = lax.axis_index("ctx")
    group_rows = rows * cycle_size
    head_width = width // HEADS
    scale = 1.0 / math.sqrt(head_width)
    half = jnp.bfloat16
    single = jnp.float32
    attn_shards = (
        ln1_gain.astype(half),
        ln1_shift.astype(half),
        qkv_weight.astype(half),
        q_bias.astype(half),
        v_bias.astype(half),
        out_weight.astype(half),
        out_bias.astype(half),
    )
    mlp_shards = (
        ln2_gain.astype(half),
        ln2_shift.astype(half),
        up_weight.astype(half),
        up_bias.astype(half),
        down_weight.astype(half),
        down_bias.astype(half),
    )
    attn_set = (
        lax.all_gather(attn_shards[0], "fsdp", axis=0, tiled=True),
        lax.all_gather(attn_shards[1], "fsdp", axis=0, tiled=True),
        lax.all_gather(attn_shards[2], "fsdp", axis=0, tiled=True),
        lax.all_gather(attn_shards[3], "fsdp", axis=0, tiled=True),
        lax.all_gather(attn_shards[4], "fsdp", axis=0, tiled=True),
        lax.all_gather(attn_shards[5], "fsdp", axis=0, tiled=True),
        lax.all_gather(attn_shards[6], "fsdp", axis=0, tiled=True),
    )
    gain_one, shift_one, joint_weight, query_bias, value_bias, proj_weight, proj_bias = attn_set
    query_places = token_places(span_place[0], lengths[0], cycle_rank * rows, rows)
    key_places = token_places(span_place[0], lengths[0], 0, group_rows)
    start = tokens.astype(single)
    hidden_one, norm_one_back = jax.vjp(
        layer_norm, start, gain_one.astype(single), shift_one.astype(single)
    )
    input_one = hidden_one.astype(half)
    blank = jnp.zeros_like(query_bias)
    joint_bias = jnp.concatenate([query_bias, blank, value_bias]).astype(single)
    joined = (product(input_one, joint_weight) + joint_bias).astype(half)
    queries = joined[:, :width].reshape(rows, HEADS, head_width)
    keys_own = joined[:, width : 2 * width]
    values_own = joined[:, 2 * width :]
    keys_all, values_all = (
        lax.all_gather(keys_own, "ctx", axis=0, tiled=True),
        lax.all_gather(values_own, "ctx", axis=0, tiled=True),
    )
    keys_all = keys_all.reshape(group_rows, HEADS, head_width)
    values_all = values_all.reshape(group_rows, HEADS, head_width)
    scores = attention_scores(queries, keys_all, query_places, key_places)
    row_top = jnp.max(scores, axis=2, keepdims=True)
    weights = jnp.exp(scores - row_top)
    total = jnp.sum(weights, axis=2, keepdims=True)
    probs_low = (weights / total).astype(half)
    attended = jnp.einsum("hqk,khd->qhd", probs_low, values_all, preferred_element_type=single)
    attended_low = attended.reshape(rows, width).astype(half)
    middle = start + product(attended_low, proj_weight) + proj_bias.astype(single)
    mlp_set = (
        lax.all_gather(mlp_shards[0], "fsdp", axis=0, tiled=True),
        lax.all_gather(mlp_shards[1], "fsdp", axis=0, tiled=True),
        lax.all_gather(mlp_shards[2], "fsdp", axis=0, tiled=True),
        lax.all_gather(mlp_shards[3], "fsdp", axis=0, tiled=True),
        lax.all_gather(mlp_shards[4], "fsdp", axis=0, tiled=True),
        lax.all_gather(mlp_shards[5], "fsdp", axis=0, tiled=True),
    )
    gain_two, shift_two, raise_weight, raise_bias, lower_weight, lower_bias = mlp_set
    hidden_two, norm_two_back = jax.vjp(
        layer_norm, middle, gain_two.astype(single), shift_two.astype(single)
    )
    input_two = hidden_two.astype(half)
    upward = product(input_two, raise_weight) + raise_bias.astype(single)
    activated, gelu_back = jax.vjp(gelu_tanh, upward)
    activated_low = activated.astype(half)
    mixed = middle + product(activated_low, lower_weight) + lower_bias.astype(single)
    back_mlp = (
        lax.all_gather(mlp_shards[0], "fsdp", axis=0, tiled=True),
        lax.all_gather(mlp_shards[1], "fsdp", axis=0, tiled=True),
        lax.all_gather(mlp_shards[2], "fsdp", axis=0, tiled=True),
        lax.all_gather(mlp_shards[3], "fsdp", axis=0, tiled=True),
        lax.all_gather(mlp_shards[4], "fsdp", axis=0, tiled=True),
        lax.all_gather(mlp_shards[5], "fsdp", axis=0, tiled=True),
    )
    raise_back = back_mlp[2]
    lower_back = back_mlp[4]
    grad_out_low = cotangent.astype(half)
    down_bias_grad = jnp.sum(grad_out_low.astype(single), axis=0)
    grad_act = product(grad_out_low, lower_back.T)
    (grad_up,) = gelu_back(grad_act)
    grad_up_low = grad_up.astype(half)
    up_bias_grad = jnp.sum(grad_up_low.astype(single), axis=0)
    grad_hidden_two = product(grad_up_low, raise_back.T)
    grad_inner, gain_two_grad, shift_two_grad = norm_two_back(grad_hidden_two)
    grad_middle = cotangent + grad_inner
    down_grad = product(activated_low.T, grad_out_low)
    up_grad = product(input_two.T, grad_up_low)
    mlp_grads = (
        lax.psum_scatter(
            gain_two_grad.astype(jnp.bfloat16), "fsdp", scatter_dimension=0, tiled=True
        ).astype(jnp.float32),
        lax.psum_scatter(
            shift_two_grad.astype(jnp.bfloat16), "fsdp", scatter_dimension=0, tiled=True
        ).astype(jnp.float32),
        lax.psum_scatter(
            up_grad.astype(jnp.bfloat16), "fsdp", scatter_dimension=0, tiled=True
        ).astype(jnp.float32),
        lax.psum_scatter(
            up_bias_grad.astype(jnp.bfloat16), "fsdp", scatter_dimension=0, tiled=True
        ).astype(jnp.float32),
        lax.psum_scatter(
            down_grad.astype(jnp.bfloat16), "fsdp", scatter_dimension=0, tiled=True
        ).astype(jnp.float32),
        lax.psum_scatter(
            down_bias_grad.astype(jnp.bfloat16), "fsdp", scatter_dimension=0, tiled=True
        ).astype(jnp.float32),
    )
    mlp_grads = (
        lax.psum(mlp_grads[0].astype(jnp.bfloat16), "ctx").astype(jnp.float32),
        lax.psum(mlp_grads[1].astype(jnp.bfloat16), "ctx").astype(jnp.float32),
        lax.psum(mlp_grads[2].astype(jnp.bfloat16), "ctx").astype(jnp.float32),
        lax.psum(mlp_grads[3].astype(jnp.bfloat16), "ctx").astype(jnp.float32),
        lax.psum(mlp_grads[4].astype(jnp.bfloat16), "ctx").astype(jnp.float32),
        lax.psum(mlp_grads[5].astype(jnp.bfloat16), "ctx").astype(jnp.float32),
    )
    back_attn = (
        lax.all_gather(attn_shards[0], "fsdp", axis=0, tiled=True),
        lax.all_gather(attn_shards[1], "fsdp", axis=0, tiled=True),
        lax.all_gather(attn_shards[2], "fsdp", axis=0, tiled=True),
        lax.all_gather(attn_shards[3], "fsdp", axis=0, tiled=True),
        lax.all_gather(attn_shards[4], "fsdp", axis=0, tiled=True),
        lax.all_gather(attn_shards[5], "fsdp", axis=0, tiled=True),
        lax.all_gather(attn_shards[6], "fsdp", axis=0, tiled=True),
    )
    joint_back = back_attn[2]
    proj_back = back_attn[5]
    grad_branch_low = grad_middle.astype(half)
    out_bias_grad = jnp.sum(grad_branch_low.astype(single), axis=0)
    grad_att_low = (
        product(grad_branch_low, proj_back.T).astype(half).reshape(rows, HEADS, head_width)
    )
    scores = attention_scores(queries, keys_all, query_places, key_places)
    probs = jnp.exp(scores - row_top) / total
    probs_again = probs.astype(half)
    grad_probs = jnp.einsum("qhd,khd->hqk", grad_att_low, values_all, preferred_element_type=single)
    center = jnp.sum(probs * grad_probs, axis=2, keepdims=True)
    grad_scores = (probs * (grad_probs - center)).astype(half)
    grad_queries = (
        jnp.einsum("hqk,khd->qhd", grad_scores, keys_all, preferred_element_type=single) * scale
    )
    grad_keys_all = (
        jnp.einsum("hqk,qhd->khd", grad_scores, queries, preferred_element_type=single) * scale
    )
    grad_values_all = jnp.einsum(
        "hqk,qhd->khd", probs_again, grad_att_low, preferred_element_type=single
    )
    grad_keys, grad_values = (
        lax.psum_scatter(
            grad_keys_all.reshape(group_rows, width).astype(jnp.bfloat16),
            "ctx",
            scatter_dimension=0,
            tiled=True,
        ).astype(jnp.float32),
        lax.psum_scatter(
            grad_values_all.reshape(group_rows, width).astype(jnp.bfloat16),
            "ctx",
            scatter_dimension=0,
            tiled=True,
        ).astype(jnp.float32),
    )
    grad_joined = jnp.concatenate(
        [grad_queries.reshape(rows, width), grad_keys, grad_values], axis=1
    ).astype(half)
    column_sums = jnp.sum(grad_joined.astype(single), axis=0)
    query_bias_grad = column_sums[:width]
    value_bias_grad = column_sums[2 * width :]
    grad_hidden_one = product(grad_joined, joint_back.T)
    grad_start, gain_one_grad, shift_one_grad = norm_one_back(grad_hidden_one)
    input_grad = grad_middle + grad_start
    joint_grad = product(input_one.T, grad_joined)
    out_grad = product(attended_low.T, grad_branch_low)
    attn_grads = (
        lax.psum_scatter(
            gain_one_grad.astype(jnp.bfloat16), "fsdp", scatter_dimension=0, tiled=True
        ).astype(jnp.float32),
        lax.psum_scatter(
            shift_one_grad.astype(jnp.bfloat16), "fsdp", scatter_dimension=0, tiled=True
        ).astype(jnp.float32),
        lax.psum_scatter(
            joint_grad.astype(jnp.bfloat16), "fsdp", scatter_dimension=0, tiled=True
        ).astype(jnp.float32),
        lax.psum_scatter(
            query_bias_grad.astype(jnp.bfloat16), "fsdp", scatter_dimension=0, tiled=True
        ).astype(jnp.float32),
        lax.psum_scatter(
            value_bias_grad.astype(jnp.bfloat16), "fsdp", scatter_dimension=0, tiled=True
        ).astype(jnp.float32),
        lax.psum_scatter(
            out_grad.astype(jnp.bfloat16), "fsdp", scatter_dimension=0, tiled=True
        ).astype(jnp.float32),
        lax.psum_scatter(
            out_bias_grad.astype(jnp.bfloat16), "fsdp", scatter_dimension=0, tiled=True
        ).astype(jnp.float32),
    )
    attn_grads = (
        lax.psum(attn_grads[0].astype(jnp.bfloat16), "ctx").astype(jnp.float32),
        lax.psum(attn_grads[1].astype(jnp.bfloat16), "ctx").astype(jnp.float32),
        lax.psum(attn_grads[2].astype(jnp.bfloat16), "ctx").astype(jnp.float32),
        lax.psum(attn_grads[3].astype(jnp.bfloat16), "ctx").astype(jnp.float32),
        lax.psum(attn_grads[4].astype(jnp.bfloat16), "ctx").astype(jnp.float32),
        lax.psum(attn_grads[5].astype(jnp.bfloat16), "ctx").astype(jnp.float32),
        lax.psum(attn_grads[6].astype(jnp.bfloat16), "ctx").astype(jnp.float32),
    )
    return (
        mixed,
        input_grad,
        attn_grads[0],
        attn_grads[1],
        attn_grads[2],
        attn_grads[3],
        attn_grads[4],
        attn_grads[5],
        attn_grads[6],
        mlp_grads[0],
        mlp_grads[1],
        mlp_grads[2],
        mlp_grads[3],
        mlp_grads[4],
        mlp_grads[5],
    )


def solution(mesh):
    in_specs = (
        P(("ctx", "fsdp"), None),
        P(("ctx", "fsdp"), None),
        P("fsdp", None),
        P("fsdp", None),
        P("fsdp"),
        P("fsdp"),
        P("fsdp", None),
        P("fsdp"),
        P("fsdp"),
        P("fsdp", None),
        P("fsdp"),
        P("fsdp"),
        P("fsdp"),
        P("fsdp", None),
        P("fsdp"),
        P("fsdp", None),
        P("fsdp"),
    )
    out_specs = (
        P(("ctx", "fsdp"), None),
        P(("ctx", "fsdp"), None),
        P("fsdp"),
        P("fsdp"),
        P("fsdp", None),
        P("fsdp"),
        P("fsdp"),
        P("fsdp", None),
        P("fsdp"),
        P("fsdp"),
        P("fsdp"),
        P("fsdp", None),
        P("fsdp"),
        P("fsdp", None),
        P("fsdp"),
    )
    return jax.shard_map(
        per_device, mesh=mesh, in_specs=in_specs, out_specs=out_specs, check_vma=False
    )
```

profile of v0, /device:TPU:0, one launch (start us, length us, event | category | flops | bytes accessed | tf_op | source)
XLA Modules:
  0.0 2668.8 jit_solution(463993376815542760)
XLA Ops:
  12.5 13.4 all-gather.3
  34.8 14.2 all-gather.1
  49.0 13.6 all-gather
  64.3 170.9 %all-gather.15.cloned.1.call-done = bf16[2048,6144]{1,0:T(8,128)(2,1)} async-done(((bf16[256,6144]{1,0:T(8,128)(2,1)}), bf16[2048,6144]{1,0:T(8,128)(2,1)}) %all-gather.15.cloned.1.call-update) | async-done | bytes 25165840 | tf_op jit(solution)/shard_map/all_gather | solution.py:107
  235.2 18.2 add_convert_fusion
  300.7 12.7 all_gather.61
  321.1 21.2 all-gather.19.cloned.1.call-done
  354.6 40.3 %fusion.80 = (f32[16,512]{1,0:T(8,128)S(1)}, f32[16,512,2048]{2,1,0:T(8,128)}) fusion(f32[512,2048]{1,0:T(8,128)} %subtract_convert_fusion, f32[16]{0:T(128)S(1)} %multiply_power_fusion, pred[512,2048]{1,0:T(8,128)(4,1)S(1)} %compare_and_fusion, bf16[512,16,128]{0,2,1:T(8,128)(2,1)S(1)} %bitcast.77, bf16[2048,16,128]{0,2,1:T(8,128)(2,1)} %bitcast.74), kind=kOutput, calls=%fused_computation.130 | convolution fusion | flops 4395632640 | bytes 82870336 | tf_op jit(solution)/shard_map/sub | solution.py:135
  394.9 37.5 %all-gather.17.cloned.1.call-done = bf16[2048,2048]{1,0:T(8,128)(2,1)} async-done(((bf16[512,2048]{1,0:T(8,128)(2,1)}), bf16[2048,2048]{1,0:T(8,128)(2,1)}) %all-gather.17.cloned.1.call-update) | async-done | bytes 8388624 | tf_op jit(solution)/shard_map/all_gather | solution.py:129
  432.4 29.1 %fusion.39 = bf16[16,128,512]{2,1,0:T(8,128)(2,1)} fusion(f32[16,512,2048]{2,1,0:T(8,128)} %get-tuple-element.55, f32[16,512]{1,0:T(8,128)S(1)} %get-tuple-element.54, bf16[2048,2048]{1,0:T(8,128)(2,1)} %all-gather.17.cloned.1.call-done), kind=kOutput, calls=%fused_computation.69 | convolution fusion | flops 4329570304 | bytes 77627392 | tf_op jit(solution)/shard_map/hqk,khd->qhd/dot_general | solution.py:138
  461.4 54.5 %all-gather.21.cloned.1.call-done = bf16[2048,2048]{1,0:T(8,128)(2,1)} async-done(((bf16[256,2048]{1,0:T(8,128)(2,1)}), bf16[2048,2048]{1,0:T(8,128)(2,1)}) %all-gather.21.cloned.1.call-update) | async-done | bytes 8388624 | tf_op jit(solution)/shard_map/all_gather | solution.py:110
  526.4 278.7 %all-gather.23.cloned.1.call-done = bf16[2048,8192]{1,0:T(8,128)(2,1)} async-done(((bf16[256,8192]{1,0:T(8,128)(2,1)}), bf16[2048,8192]{1,0:T(8,128)(2,1)}) %all-gather.23.cloned.1.call-update) | async-done | bytes 33554448 | tf_op jit(solution)/shard_map/all_gather | solution.py:144
  805.1 43.0 %fusion.73 = f32[512,8192]{1,0:T(8,128)} fusion(bf16[2048,8192]{1,0:T(8,128)(2,1)} %all-gather.23.cloned.1.call-done, f32[512,2048]{1,0:T(8,128)} %copy-done.4, f32[2048]{0:T(1024)S(1)} %bitcast.100, f32[2048]{0:T(1024)S(1)} %bitcast.90, f32[512]{0:T(512)S(1)} %fusion.59, f32[512]{0:T(512)S(1)} %broadcast_multiply_fusion), kind=kOutput, calls=%fused_computation.124 | convolution fusion | flops 17185112064 | bytes 54546432 | tf_op jit(solution)/shard_map/dot_general | solution.py:57
  848.1 245.9 %all-gather.25.cloned.1.call-done = bf16[8192,2048]{1,0:T(8,128)(2,1)} async-done(((bf16[1024,2048]{1,0:T(8,128)(2,1)}), bf16[8192,2048]{1,0:T(8,128)(2,1)}) %all-gather.25.cloned.1.call-update) | async-done | bytes 33554448 | tf_op jit(solution)/shard_map/all_gather | solution.py:146
  1094.0 38.1 %fusion.82 = (bf16[8192]{0:T(1024)(128)(2,1)}, bf16[512,8192]{1,0:T(8,128)(2,1)}) fusion(bf16[8192,2048]{1,0:T(8,128)(2,1)} %all-gather.25.cloned.1.call-done, f32[512,2048]{1,0:T(8,128)} %param.18, f32[512,8192]{1,0:T(8,128)} %fusion.73, f32[8192]{0:T(1024)S(1)} %copy-done.20), kind=kOutput, calls=%fused_computation.132 | convolution fusion | flops 17289961472 | bytes 62963712 | tf_op jit(solution)/shard_map/dot_general | solution.py:57
  1132.1 26.9 %multiply_reduce_fusion.1 = (bf16[2048]{0:T(1024)(128)(2,1)}, f32[512]{0:T(512)S(1)}, bf16[2048]{0:T(1024)(128)(2,1)}, f32[512,2048]{1,0:T(8,128)}) fusion(f32[512,2048]{1,0:T(8,128)} %copy-done.4, f32[512]{0:T(512)S(1)} %fusion.59, f32[512]{0:T(512)S(1)} %broadcast_multiply_fusion, f32[2048]{0:T(1024)S(1)} %bitcast.91, ...), kind=kOutput, calls=%fused_computation.58 | convolution fusion | flops 17188253696 | bytes 50354176 | tf_op jit(solution)/shard_map/dot_general | solution.py:57
  1178.2 26.4 fusion.28
  1204.7 49.2 %multiply_reduce_fusion = (f32[16,512]{1,0:T(8,128)S(1)}, f32[16,512,2048]{2,1,0:T(8,128)}) fusion(f32[16,512,2048]{2,1,0:T(8,128)} %get-tuple-element.55, f32[16,512]{1,0:T(8,128)S(1)} %get-tuple-element.54, bf16[512,16,128]{0,2,1:T(8,128)(2,1)S(1)} %bitcast.84, bf16[2048,2048]{1,0:T(8,128)(2,1)} %all-gather.17.cloned.1.call-done), kind=kOutput, calls=%fused_computation.2 | convolution fusion | flops 4345290752 | bytes 144769024 | tf_op jit(solution)/shard_map/qhd,khd->hqk/dot_general | solution.py:226
  1254.0 54.5 %multiply_convert_fusion = bf16[16,512,2048]{2,1,0:T(8,128)(2,1)} fusion(f32[16,512,2048]{2,1,0:T(8,128)} %get-tuple-element.60, f32[16,512]{1,0:T(8,128)S(1)} %get-tuple-element.59, f32[16,512,2048]{2,1,0:T(8,128)} %get-tuple-element.55, f32[16,512]{1,0:T(8,128)S(1)} %get-tuple-element.54), kind=kLoop, calls=%fused_computation.1 | loop fusion | flops 67108864 | bytes 167837696 | tf_op jit(solution)/shard_map/convert_element_type | solution.py:228
  1308.5 16.5 multiply_convert_fusion.1
  1335.7 29.0 %convolution_convert_fusion = bf16[8192,2048]{1,0:T(8,128)(2,1)} fusion(f32[512,2048]{1,0:T(8,128)} %param.18, f32[512,8192]{1,0:T(8,128)} %fusion.73, f32[8192]{0:T(1024)S(1)} %copy-done.21), kind=kOutput, calls=%fused_computation.12 | convolution fusion | flops 17239638016 | bytes 54558720 | tf_op jit(solution)/shard_map/dot_general | solution.py:57
  1365.5 25.5 convolution_convert_fusion.1
  1391.0 18.8 multiply_convert_fusion.3
  1409.9 20.4 convolution_convert_fusion.2
  1430.5 71.4 %reduce-scatter.13.cloned.1.call-done = bf16[256,2048]{1,0:T(8,128)(2,1)} async-done(((bf16[2048,2048]{1,0:T(8,128)(2,1)}), bf16[256,2048]{1,0:T(8,128)(2,1)}) %reduce-scatter.13.cloned.1.call-update) | async-done | bytes 1048592 | tf_op jit(solution)/shard_map/reduce_scatter | solution.py:279
  1501.9 326.2 %reduce-scatter.17.cloned.1.call-done = bf16[1024,2048]{1,0:T(8,128)(2,1)} async-done(((bf16[8192,2048]{1,0:T(8,128)(2,1)}), bf16[1024,2048]{1,0:T(8,128)(2,1)}) %reduce-scatter.17.cloned.1.call-update) | async-done | bytes 4194320 | tf_op jit(solution)/shard_map/reduce_scatter | solution.py:192
  1828.0 326.4 %reduce-scatter.15.cloned.1.call-done = bf16[256,8192]{1,0:T(8,128)(2,1)} async-done(((bf16[2048,8192]{1,0:T(8,128)(2,1)}), bf16[256,8192]{1,0:T(8,128)(2,1)}) %reduce-scatter.15.cloned.1.call-update) | async-done | bytes 4194320 | tf_op jit(solution)/shard_map/reduce_scatter | solution.py:186
  2154.4 247.8 %reduce-scatter.11.cloned.1.call-done = bf16[256,6144]{1,0:T(8,128)(2,1)} async-done(((bf16[2048,6144]{1,0:T(8,128)(2,1)}), bf16[256,6144]{1,0:T(8,128)(2,1)}) %reduce-scatter.11.cloned.1.call-update) | async-done | bytes 3145744 | tf_op jit(solution)/shard_map/reduce_scatter | solution.py:270
  2413.9 29.3 %add_add_fusion.4 = f32[512,2048]{1,0:T(8,128)} fusion(f32[512,2048]{1,0:T(8,128)} %copy-done.4, bf16[8192,2048]{1,0:T(8,128)(2,1)} %all-gather.25.cloned.1.call-done, f32[2048]{0:T(1024)S(1)} %bitcast.103, f32[512,8192]{1,0:T(8,128)} %fusion.73, f32[8192]{0:T(1024)S(1)} %copy-done.21), kind=kOutput, calls=%fused_computation.63 | convolution fusion | flops 17223909376 | bytes 58761216 | tf_op jit(solution)/shard_map/dot_general | solution.py:57
  2443.2 23.2 fusion.74
  2473.5 27.3 %all-reduce.9 = (bf16[2048]{0:T(1024)(128)(2,1)S(1)}, bf16[2048]{0:T(1024)(128)(2,1)S(1)}, bf16[2048]{0:T(1024)(128)(2,1)S(1)}, bf16[2048]{0:T(1024)(128)(2,1)S(...) all-reduce(bf16[2048]{0:T(1024)(128)(2,1)S(1)} %get-tuple-element.1, ...), channel_id=4, replica_groups=mesh['ctx'=4,'fsdp'=8] {'fsdp'}, use_global_device_ids=true, to_apply=%region_19.20.clone | all-reduce | flops 24576 | bytes 98304
  2524.7 121.9 %all-reduce.14.cloned.1.call-done = (bf16[256,6144]{1,0:T(8,128)(2,1)}, bf16[256,2048]{1,0:T(8,128)(2,1)}, bf16[256,8192]{1,0:T(8,128)(2,1)}, bf16[1024,2048]{1,0:T(8,128)(2,1)}) async-done(((bf16[256,6144]{1,0:T(8,128)(2,1)}, bf16[256,2048]{1,0:T(8,128)(2,1)}, bf16[256,8192]{1,0:T(8,128)(2,1)}, bf16[1024,2048]{1,0:T(8,128)(2,1)}), (bf16[256,6144]{1,0:T(8,128)(2,1)}, bf16[256,2048]{1,0:T(8,128)(2,1)}, ...) | async-done | bytes 12582928 | tf_op jit(solution)/shard_map/psum | solution.py:289
  (238 shorter events, 180.3 us)
Async XLA Ops:
  7.2 55.4 %copy-start.1 = (bf16[512,2048]{1,0:T(8,128)(2,1)S(1)}, bf16[512,2048]{1,0:T(8,128)(2,1)}, u32[]{:S(2)}) copy-start(bf16[512,2048]{1,0:T(8,128)(2,1)} %param.17) | copy-start | bytes 6291460
  7.2 228.0 %all-gather.15.cloned.1.call-start = ((), (), s32[]{:S(2)}) async-start(), calls=%async_computation.6 | async-start | bytes 28311552 | tf_op jit(solution)/shard_map/all_gather | solution.py:107
  12.3 329.9 %all-gather.19.cloned.1.call-start = ((), (), s32[]{:S(2)}) async-start(), calls=%async_computation.8 | async-start | bytes 10485760 | tf_op jit(solution)/shard_map/all_gather | solution.py:128
  49.0 204.4 %copy-start.37 = (f32[8,1,256]{2,1,0:T(1,128)}, f32[8,1,256]{2,1,0:T(1,128)S(1)}, u32[]{:S(2)}) copy-start(f32[8,1,256]{2,1,0:T(1,128)S(1)} %convert_element_type.312) | copy-start | bytes 24580
  62.6 190.9 %copy-start.16 = (f32[8,1,256]{2,1,0:T(1,128)}, f32[8,1,256]{2,1,0:T(1,128)S(1)}, u32[]{:S(2)}) copy-start(f32[8,1,256]{2,1,0:T(1,128)S(1)} %convert_element_type.311) | copy-start | bytes 24580
  63.0 190.5 %copy-start.22 = (f32[512]{0:T(512)}, f32[512]{0:T(512)S(1)}, u32[]{:S(2)}) copy-start(f32[512]{0:T(512)S(1)} %broadcast_multiply_fusion.1) | copy-start | bytes 6148
  64.3 189.2 %copy-start.26 = (f32[512]{0:T(512)}, f32[512]{0:T(512)S(1)}, u32[]{:S(2)}) copy-start(f32[512]{0:T(512)S(1)} %fusion.58) | copy-start | bytes 6148
  256.4 176.0 %all-gather.17.cloned.1.call-start = ((), (), s32[]{:S(2)}) async-start(), calls=%async_computation.7 | async-start | bytes 10485760 | tf_op jit(solution)/shard_map/all_gather | solution.py:129
  257.1 258.8 %all-gather.21.cloned.1.call-start = ((), (), s32[]{:S(2)}) async-start(), calls=%async_computation.9 | async-start | bytes 9437184 | tf_op jit(solution)/shard_map/all_gather | solution.py:110
  259.1 546.0 %all-gather.23.cloned.1.call-start = ((), (), s32[]{:S(2)}) async-start(), calls=%async_computation.10 | async-start | bytes 37748736 | tf_op jit(solution)/shard_map/all_gather | solution.py:144
  266.0 828.0 %all-gather.25.cloned.1.call-start = ((), (), s32[]{:S(2)}) async-start(), calls=%async_computation.11 | async-start | bytes 37748736 | tf_op jit(solution)/shard_map/all_gather | solution.py:146
  272.2 41.9 %copy-start.53 = (s32[1,2]{1,0:T(1,128)S(1)}, s32[1,2]{1,0:T(1,128)}, u32[]{:S(2)}) copy-start(s32[1,2]{1,0:T(1,128)} %param.19) | copy-start | bytes 28
  272.2 42.1 %copy-start.44 = (s32[1,16]{1,0:T(1,128)S(1)}, s32[1,16]{1,0:T(1,128)}, u32[]{:S(2)}) copy-start(s32[1,16]{1,0:T(1,128)} %param.20) | copy-start | bytes 196
  272.2 1137.6 %reduce-scatter.9.cloned.1.call-start = ((), (), s32[]{:S(2)}) async-start(), calls=%async_computation.13 | async-start | bytes 10485760 | tf_op jit(solution)/shard_map/reduce_scatter | solution.py:245
  281.9 523.2 %copy-start.39 = (f32[8,1,256]{2,1,0:T(1,128)}, f32[8,1,256]{2,1,0:T(1,128)S(1)}, u32[]{:S(2)}) copy-start(f32[8,1,256]{2,1,0:T(1,128)S(1)} %convert_element_type.315) | copy-start | bytes 24580
  291.8 867.3 %copy-start.18 = (f32[8,1,256]{2,1,0:T(1,128)}, f32[8,1,256]{2,1,0:T(1,128)S(1)}, u32[]{:S(2)}) copy-start(f32[8,1,256]{2,1,0:T(1,128)S(1)} %convert_element_type.314) | copy-start | bytes 24580
  321.1 33.5 %copy-start.8 = (bf16[512,2048]{0,1:T(8,128)(2,1)}, bf16[512,2048]{0,1:T(8,128)(2,1)S(1)}, u32[]{:S(2)}) copy-start(bf16[512,2048]{0,1:T(8,128)(2,1)S(1)} %copy.64) | copy-start | bytes 6291460
  432.3 83.5 %copy-start.2 = (bf16[512,2048]{1,0:T(8,128)(2,1)S(1)}, bf16[512,2048]{1,0:T(8,128)(2,1)}, u32[]{:S(2)}) copy-start(bf16[512,2048]{1,0:T(8,128)(2,1)} %param.17) | copy-start | bytes 6291460
  523.7 635.4 %copy-start.24 = (f32[512]{0:T(512)}, f32[512]{0:T(512)S(1)}, u32[]{:S(2)}) copy-start(f32[512]{0:T(512)S(1)} %broadcast_multiply_fusion) | copy-start | bytes 6148
  526.4 632.7 %copy-start.35 = (f32[512]{0:T(512)}, f32[512]{0:T(512)S(1)}, u32[]{:S(2)}) copy-start(f32[512]{0:T(512)S(1)} %fusion.59) | copy-start | bytes 6148
  805.1 288.9 %copy-start.20 = (f32[8192]{0:T(1024)S(1)}, f32[8192]{0:T(1024)}, u32[]{:S(2)}) copy-start(f32[8192]{0:T(1024)} %convert_element_type.273) | copy-start | bytes 98308
  1132.1 27.0 %copy-start.5 = (f32[512,2048]{1,0:T(8,128)S(1)}, f32[512,2048]{1,0:T(8,128)}, u32[]{:S(2)}) copy-start(f32[512,2048]{1,0:T(8,128)} %copy-done.4) | copy-start | bytes 12582916
  1204.7 205.2 %reduce-scatter.7.cloned.1.call-start = ((), (), s32[]{:S(2)}) async-start(), calls=%async_computation.12 | async-start | bytes 10485760 | tf_op jit(solution)/shard_map/reduce_scatter | solution.py:239
  1254.0 54.5 %copy-start.9 = (bf16[512,2048]{0,1:T(8,128)(2,1)S(1)}, bf16[512,2048]{0,1:T(8,128)(2,1)}, u32[]{:S(2)}) copy-start(bf16[512,2048]{0,1:T(8,128)(2,1)} %copy-done.8) | copy-start | bytes 6291460
  1325.0 176.8 %reduce-scatter.13.cloned.1.call-start = ((), (), s32[]{:S(2)}) async-start(), calls=%async_computation.15 | async-start | bytes 9437184 | tf_op jit(solution)/shard_map/reduce_scatter | solution.py:279
  1335.0 493.0 %reduce-scatter.17.cloned.1.call-start = ((), (), s32[]{:S(2)}) async-start(), calls=%async_computation.17 | async-start | bytes 37748736 | tf_op jit(solution)/shard_map/reduce_scatter | solution.py:192
  1364.8 789.6 %reduce-scatter.15.cloned.1.call-start = ((), (), s32[]{:S(2)}) async-start(), calls=%async_computation.16 | async-start | bytes 37748736 | tf_op jit(solution)/shard_map/reduce_scatter | solution.py:186
  1390.9 19.0 copy-start.3
  1391.0 1011.2 %reduce-scatter.11.cloned.1.call-start = ((), (), s32[]{:S(2)}) async-start(), calls=%async_computation.14 | async-start | bytes 28311552 | tf_op jit(solution)/shard_map/reduce_scatter | solution.py:270
  1430.4 1216.1 %all-reduce.14.cloned.1.call-start = ((), (), s32[]{:S(2)}) async-start(), calls=%async_computation.18 | async-start | bytes 25165824 | tf_op jit(solution)/shard_map/psum | solution.py:289
  2443.2 23.2 copy-start.31
  2471.4 46.2 %copy-start.29 = (f32[512]{0:T(512)S(1)}, f32[512]{0:T(512)}, u32[]{:S(2)}) copy-start(f32[512]{0:T(512)} %copy-done.28) | copy-start | bytes 6148
  (36 other events, 147.7 us)
Sparse Core Ops, SparseCore 0:
  12.4 222.7 all-gather.14
  256.5 85.7 all-gather.18
  344.7 87.5 all-gather.16
  433.8 82.0 all-gather.20
  517.9 287.1 all-gather.22
  807.1 286.8 all-gather.24
  1204.8 84.5 reduce-scatter.8
  1325.2 84.6 reduce-scatter.6
  1412.2 89.5 reduce-scatter.12
  1504.1 323.8 reduce-scatter.16
  1830.5 323.8 reduce-scatter.14
  2156.6 245.5 reduce-scatter.10
  2406.1 240.3 all-reduce.13
where the time goes:
time: 2680 us; the launch traced here: 2670 us
  waiting for transfers between devices  1900 us (71%)
  matrix products  459 us (17%)
  blocking collectives  138 us (5%)
  other arithmetic  120 us (4%)
  local copies, waits for them, and re-layouts  31.4 us (1%)
    reduce_scatter x1, waiting for transfers between devices, per_device(): lax.psum_scatter(up_grad.astype(jnp.bfloat16), 'fsdp', scatter_dimension=...  326 us
    reduce_scatter x1, waiting for transfers between devices, per_device(): lax.psum_scatter(down_grad.astype(jnp.bfloat16), 'fsdp', scatter_dimensio...  326 us
    dot_general x12, matrix products, product(): return jnp.dot(left, right, preferred_element_type=jnp.float32)  279 us
    all_gather x1, waiting for transfers between devices, per_device(): lax.all_gather(mlp_shards[2], 'fsdp', axis=0, tiled=True)  279 us
    reduce_scatter x1, waiting for transfers between devices, per_device(): lax.psum_scatter(joint_grad.astype(jnp.bfloat16), 'fsdp', scatter_dimensi...  248 us
    all_gather x1, waiting for transfers between devices, per_device(): lax.all_gather(mlp_shards[4], 'fsdp', axis=0, tiled=True)  246 us
    all_gather x1, waiting for transfers between devices, per_device(): lax.all_gather(attn_shards[2], 'fsdp', axis=0, tiled=True)  171 us
    psum x1, waiting for transfers between devices, per_device(): lax.psum(attn_grads[2].astype(jnp.bfloat16), 'ctx').astype(jnp.float32)  122 us
  transfers between devices with their start and end apart: 13, of which 12 were waited for; matrix products, arithmetic and copies ran while one was open for 17% of the time, Pallas kernels for 0%

commit v1 on v0

v1 whole, which is shorter than its diff:
```python
import functools
import math

import jax
import jax.numpy as jnp
from jax import lax
from jax.experimental import pallas as pl
from jax.experimental.pallas import tpu as pltpu
from jax.sharding import PartitionSpec as P

HEADS = 16
SPAN = 128
SEQ_BLOCKS = 8

norm_eps = 1e-05
gelu_coef = 0.7978845608028654
LOG2E = 1.4426950408889634

half = jnp.bfloat16
single = jnp.float32


def dot_nn(a, b):
    return lax.dot_general(a, b, (((1,), (0,)), ((), ())), preferred_element_type=single)


def dot_nt(a, b):
    return lax.dot_general(a, b, (((1,), (1,)), ((), ())), preferred_element_type=single)


def dot_tn(a, b):
    return lax.dot_general(a, b, (((0,), (0,)), ((), ())), preferred_element_type=single)


def norm_parts(values):
    center = values - jnp.mean(values, axis=-1, keepdims=True)
    spread = jnp.mean(center * center, axis=-1, keepdims=True)
    inv = lax.rsqrt(spread + norm_eps)
    return center * inv, inv


def norm_back(normed, inv, gain, grad):
    dn = grad * gain
    return inv * (
        dn
        - jnp.mean(dn, axis=-1, keepdims=True)
        - normed * jnp.mean(dn * normed, axis=-1, keepdims=True)
    )


def gelu_both(v):
    t = jnp.tanh(gelu_coef * (v + 0.044715 * v * v * v))
    value = 0.5 * v * (1.0 + t)
    slope = 0.5 * (1.0 + t) + 0.5 * v * (1.0 - t * t) * gelu_coef * (1.0 + 3 * 0.044715 * v * v)
    return value, slope


def swap(x, mask):
    n = lax.axis_size("ctx")
    return lax.ppermute(x, "ctx", [(i, i ^ mask) for i in range(n)])


def gather_ctx(x):
    n = x.shape[0] // 2
    count = lax.axis_size("ctx")
    if count != 4:
        c = lax.axis_index("ctx")
        whole = lax.all_gather(x, "ctx", axis=0)
        parts = [lax.dynamic_index_in_dim(whole, c ^ j, 0, keepdims=False) for j in range(count)]
        return [(p[:n], p[n:]) for p in parts]
    lo, hi = x[:n], x[n:]
    x_lo = swap(lo, 1)
    y_hi = swap(hi, 2)
    x_hi = swap(hi, 1)
    y_lo = swap(lo, 2)
    d_lo = swap(x_lo, 2)
    d_hi = swap(y_hi, 1)
    return [(lo, hi), (x_lo, x_hi), (y_lo, y_hi), (d_lo, d_hi)]


def scatter_ctx(pieces):
    if len(pieces) != 4:
        c = lax.axis_index("ctx")
        ordered = xor_order([p.astype(half) for p in pieces], c)
        whole = jnp.concatenate(ordered, axis=0)
        return lax.psum_scatter(whole, "ctx", scatter_dimension=0, tiled=True).astype(single)
    p0, p1, p2, p3 = pieces
    n = p0.shape[0] // 2
    from_x = swap(p3[:n], 1)
    from_y = swap(p3[n:], 2)
    p2_lo = (p2[:n].astype(single) + from_x.astype(single)).astype(half)
    p1_hi = (p1[n:].astype(single) + from_y.astype(single)).astype(half)
    x_lo = swap(p1[:n], 1)
    y_hi = swap(p2[n:], 2)
    x_hi = swap(p1_hi, 1)
    y_lo = swap(p2_lo, 2)
    lo = p0[:n].astype(single) + x_lo.astype(single) + y_lo.astype(single)
    hi = p0[n:].astype(single) + x_hi.astype(single) + y_hi.astype(single)
    return jnp.concatenate([lo, hi], axis=0)


def xor_order(items, c):
    bit = 1
    while bit < len(items):
        on = (c & bit) == bit
        items = [jnp.where(on, items[i ^ bit], items[i]) for i in range(len(items))]
        bit *= 2
    return items


TILE = 256


def attn_scores(q_refs, k_refs, i, scale, slope):
    q = jnp.concatenate([q_refs[2 * i][...], q_refs[2 * i + 1][...]], axis=0)
    k = jnp.concatenate([r[...] for r in k_refs[: 2 * i + 2]], axis=0)
    n = TILE * (i + 1)
    col = lax.broadcasted_iota(jnp.int32, (1, n), 1) - (n - 1)
    s = dot_nt(q, k) * (scale * LOG2E) + (slope * LOG2E) * col.astype(single)
    row_at = lax.broadcasted_iota(jnp.int32, (TILE, TILE), 0)
    col_at = lax.broadcasted_iota(jnp.int32, (TILE, TILE), 1)
    last = jnp.where(col_at <= row_at, s[:, n - TILE :], -1e30)
    s = last if i == 0 else jnp.concatenate([s[:, : n - TILE], last], axis=1)
    e = jnp.exp2(s - jnp.max(s, axis=1, keepdims=True))
    return q, k, e, 1.0 / jnp.sum(e, axis=1, keepdims=True)


def attn_fwd_kernel(scale, inv_ref, slope_ref, *refs):
    q_refs, k_refs, v_refs = refs[:8], refs[8:16], refs[16:24]
    o_ref = refs[24]
    slope = slope_ref[pl.program_id(1)]
    for i in range(4):
        q, k, e, r = attn_scores(q_refs, k_refs, i, scale, slope)
        v = jnp.concatenate([x[...] for x in v_refs[: 2 * i + 2]], axis=0)
        o = dot_nn((e * r).astype(half), v)
        o_ref[TILE * i : TILE * (i + 1), :] = o.astype(half)


def attn_bwd_kernel(scale, inv_ref, slope_ref, *refs):
    q_refs, k_refs, v_refs, g_refs = refs[:8], refs[8:16], refs[16:24], refs[24:32]
    dq_ref, dk_ref, dv_ref, dk_acc, dv_acc = refs[32:]
    slope = slope_ref[pl.program_id(1)]
    for i in (3, 2, 1, 0):
        q, k, e, r = attn_scores(q_refs, k_refs, i, scale, slope)
        n = TILE * (i + 1)
        v = jnp.concatenate([x[...] for x in v_refs[: 2 * i + 2]], axis=0)
        g = jnp.concatenate([g_refs[2 * i][...], g_refs[2 * i + 1][...]], axis=0)
        p = e * r
        dp = dot_nt(g, v)
        delta = jnp.sum(p * dp, axis=1, keepdims=True)
        ds = (p * (dp - delta)).astype(half)
        pb = p.astype(half)
        dq_ref[TILE * i : TILE * (i + 1), :] = (dot_nn(ds, k) * scale).astype(half)
        dk = dot_tn(ds, q)
        dv = dot_tn(pb, g)
        if i == 3:
            dk_acc[...] = dk
            dv_acc[...] = dv
        else:
            dk_acc[:n, :] += dk
            dv_acc[:n, :] += dv
    dk_ref[...] = (dk_acc[...] * scale).astype(half)
    dv_ref[...] = dv_acc[...].astype(half)


def block_specs(offset):
    def one(j):
        return pl.BlockSpec(
            (SPAN, 128), lambda s, h, inv, slope: (inv[s * SEQ_BLOCKS + j], offset + h)
        )

    return [one(j) for j in range(SEQ_BLOCKS)]


def attn_forward(joined, inv, slopes, heads, scale):
    rows = joined.shape[0]
    specs = block_specs(0) + block_specs(heads) + block_specs(2 * heads)
    out = pl.BlockSpec((rows // 2, 128), lambda s, h, inv, slope: (s, h))
    return pl.pallas_call(
        functools.partial(attn_fwd_kernel, scale),
        grid_spec=pltpu.PrefetchScalarGridSpec(
            num_scalar_prefetch=2, grid=(2, heads), in_specs=specs, out_specs=out
        ),
        out_shape=jax.ShapeDtypeStruct((rows, heads * 128), half),
        compiler_params=pltpu.CompilerParams(vmem_limit_bytes=48 * 1024 * 1024),
        cost_estimate=pl.CostEstimate(
            flops=20 * 10**9, bytes_accessed=rows * heads * 128 * 8, transcendentals=0
        ),
        name="attn_forward",
    )(inv, slopes, *([joined] * 24))


def attn_backward(joined, grad, inv, slopes, heads, scale):
    rows = joined.shape[0]
    specs = block_specs(0) + block_specs(heads) + block_specs(2 * heads) + block_specs(0)
    out = pl.BlockSpec((rows // 2, 128), lambda s, h, inv, slope: (s, h))
    shape = jax.ShapeDtypeStruct((rows, heads * 128), half)
    return pl.pallas_call(
        functools.partial(attn_bwd_kernel, scale),
        grid_spec=pltpu.PrefetchScalarGridSpec(
            num_scalar_prefetch=2,
            grid=(2, heads),
            in_specs=specs,
            out_specs=[out] * 3,
            scratch_shapes=[pltpu.VMEM((rows // 2, 128), single)] * 2,
        ),
        out_shape=[shape] * 3,
        compiler_params=pltpu.CompilerParams(vmem_limit_bytes=48 * 1024 * 1024),
        cost_estimate=pl.CostEstimate(
            flops=40 * 10**9, bytes_accessed=rows * heads * 128 * 14, transcendentals=0
        ),
        name="attn_backward",
    )(inv, slopes, *([joined] * 24), *([grad] * 8))


def per_device(
    tokens,
    cotangent,
    lengths,
    span_place,
    ln1_gain,
    ln1_shift,
    qkv_weight,
    q_bias,
    v_bias,
    out_weight,
    out_bias,
    ln2_gain,
    ln2_shift,
    up_weight,
    up_bias,
    down_weight,
    down_bias,
):
    rows, width = tokens.shape
    CTX = lax.axis_size("ctx")
    c = lax.axis_index("ctx")
    f = lax.axis_index("fsdp")
    nf = lax.axis_size("fsdp")
    wide = up_weight.shape[1]
    part = width // CTX
    heads = HEADS // CTX
    scale = 1.0 / math.sqrt(width // HEADS)
    shard = width // nf
    fpart = wide // nf // CTX
    wpart = wide // CTX

    def pick(x, axis):
        return lax.dynamic_index_in_dim(x, c, axis, keepdims=False)

    def gather_f(x):
        return lax.all_gather(x, "fsdp", axis=0, tiled=True)

    qkv_own = pick(qkv_weight.reshape(shard, 3, CTX, part), 2).reshape(shard, 3 * part)
    up_own = pick(up_weight.reshape(shard, nf, CTX, fpart), 2).reshape(shard, wpart)
    down_own = pick(down_weight.reshape(CTX, fpart, width), 0)
    w_qkv = gather_f(qkv_own.astype(half))
    small = jnp.concatenate(
        [ln1_gain, ln1_shift, q_bias, v_bias, out_bias, ln2_gain, ln2_shift, down_bias, up_bias]
    ).astype(half)
    small_all = lax.all_gather(small, "fsdp", axis=0).astype(single)

    def vector(k):
        return small_all[:, k * shard : (k + 1) * shard].reshape(width)

    gain1, shift1, bias_q, bias_v, bias_o, gain2, shift2, bias_d = [vector(k) for k in range(8)]
    bias_u = pick(small_all[:, 8 * shard :].reshape(nf, CTX, fpart), 1).reshape(wpart)
    bias_qkv = jnp.concatenate(
        [pick(bias_q.reshape(CTX, part), 0), jnp.zeros((part,), single), pick(bias_v.reshape(CTX, part), 0)]
    )
    w_out = gather_f(out_weight.astype(half))
    w_down = gather_f(down_own.astype(half))
    w_up = gather_f(up_own.astype(half))

    per = rows // SPAN
    table = jnp.arange(CTX * per, dtype=jnp.int32)
    source = ((table // per) ^ c) * per + table % per
    place = jnp.sum(jnp.where(source[:, None] == table[None, :], span_place[0][None, :], 0), axis=1)
    inv = jnp.sum(jnp.where(place[None, :] == table[:, None], table[None, :], 0), axis=1)
    slopes = 2.0 ** (-8.0 * ((c * heads + jnp.arange(heads)).astype(single) + 1.0) / HEADS)

    def to_rows(x):
        return jnp.concatenate(
            [lax.dynamic_slice_in_dim(x, place[r] * SPAN, SPAN, axis=0) for r in range(CTX * per)]
        )

    def join(pieces):
        return jnp.concatenate([h for p in pieces for h in p], axis=0)

    tok_all = join(gather_ctx(tokens))
    normed1, _ = norm_parts(tok_all.astype(single))
    a1 = (normed1 * gain1 + shift1).astype(half)
    joined = (dot_nn(a1, w_qkv) + bias_qkv).astype(half)
    attended = to_rows(attn_forward(joined, inv, slopes, heads, scale))

    def pieces_of(x):
        return [x[j * rows : (j + 1) * rows] for j in range(CTX)]

    mine = pieces_of(attended)
    mine = [mine[0]] + [swap(mine[j], j) for j in range(1, CTX)]
    ob = jnp.concatenate(xor_order(mine, c), axis=1)
    y1 = tokens.astype(single) + dot_nn(ob, w_out) + bias_o

    normed2, inv2 = norm_parts(y1)
    a2_pieces = gather_ctx((normed2 * gain2 + shift2).astype(half))
    dz2_own = cotangent.astype(half)
    dz2_pieces = gather_ctx(dz2_own)
    a2_pieces = [jnp.concatenate(p, axis=0) for p in a2_pieces]
    dz2_pieces = [jnp.concatenate(p, axis=0) for p in dz2_pieces]
    gb, du, dh2, mix = [], [], [None] * CTX, [None] * CTX
    for j in range(CTX):
        dgb = dot_nt(dz2_pieces[j], w_down).astype(half).astype(single)
        value, slope = gelu_both(dot_nn(a2_pieces[j], w_up) + bias_u)
        gb.append(value.astype(half))
        du.append((dgb * slope).astype(half))
    for j in reversed(range(CTX)):
        dh2[j] = dot_nt(du[j], w_up)
        if j:
            dh2[j] = dh2[j].astype(half)
    for j in reversed(range(CTX)):
        mix[j] = dot_nn(gb[j], w_down)
        if j:
            mix[j] = mix[j].astype(half)
    dh2 = scatter_ctx(dh2)
    mixed = y1 + scatter_ctx(mix) + bias_d
    gb = jnp.concatenate(gb, axis=0)
    du = jnp.concatenate(du, axis=0)
    a2 = jnp.concatenate(a2_pieces, axis=0)
    dz2 = jnp.concatenate(dz2_pieces, axis=0)
    down_grad = dot_tn(gb, dz2).astype(half)
    up_grad = dot_tn(a2, du).astype(half)
    up_bias_grad = jnp.sum(du.astype(single), axis=0)
    down_bias_grad = jnp.sum(dz2_own.astype(single), axis=0)
    gain2_grad = jnp.sum(dh2 * normed2, axis=0)
    shift2_grad = jnp.sum(dh2, axis=0)
    dy1 = cotangent + norm_back(normed2, inv2, gain2, dh2)

    dz1 = dy1.astype(half)
    out_bias_grad = jnp.sum(dz1.astype(single), axis=0)
    out_grad = dot_tn(ob, dz1).astype(half)
    dattn = dot_nt(dz1, w_out).astype(half)
    dattn = xor_order([dattn[:, s * part : (s + 1) * part] for s in range(CTX)], c)
    dattn = jnp.concatenate([dattn[0]] + [swap(dattn[j], j) for j in range(1, CTX)], axis=0)
    dqkv = jnp.concatenate(attn_backward(joined, dattn, inv, slopes, heads, scale), axis=1)
    dqkv = to_rows(dqkv)
    dh1 = [dot_nt(p, w_qkv) for p in pieces_of(dqkv)]
    dh1 = scatter_ctx(dh1[:1] + [p.astype(half) for p in dh1[1:]])
    qkv_grad = dot_tn(a1, dqkv).astype(half)
    sums = jnp.sum(dqkv.astype(single), axis=0)
    normed1_own, inv1_own = norm_parts(tokens.astype(single))
    gain1_grad = jnp.sum(dh1 * normed1_own, axis=0)
    shift1_grad = jnp.sum(dh1, axis=0)
    input_grad = dy1 + norm_back(normed1_own, inv1_own, gain1, dh1)

    def scatter_f(x):
        return lax.psum_scatter(x, "fsdp", scatter_dimension=0, tiled=True)

    def everywhere(x):
        pieces = [jnp.concatenate(p, axis=0) for p in gather_ctx(x)]
        return xor_order([p.astype(single) for p in pieces], c)

    down_out = jnp.concatenate(everywhere(scatter_f(down_grad)), axis=0)
    up_out = everywhere(scatter_f(up_grad))
    up_out = jnp.stack([p.reshape(shard, nf, fpart) for p in up_out], axis=2).reshape(shard, wide)
    out_part = scatter_f(out_grad)
    bit = 1
    while bit < CTX:
        out_part = out_part.astype(half)
        out_part = out_part.astype(single) + swap(out_part, bit).astype(single)
        bit *= 2
    out_out = out_part
    qkv_out = everywhere(scatter_f(qkv_grad))
    qkv_out = jnp.stack([p.reshape(shard, 3, part) for p in qkv_out], axis=2)
    qkv_out = qkv_out.reshape(shard, 3 * width)

    def spread(x, inner):
        x = x.reshape(-1, 1, inner)
        mask = (jnp.arange(CTX) == c)[None, :, None]
        return jnp.where(mask, x, 0.0).reshape(-1)

    early = [out_bias_grad, gain2_grad, shift2_grad, down_bias_grad, spread(up_bias_grad, fpart)]
    late = [gain1_grad, shift1_grad, spread(sums[:part], part), spread(sums[2 * part :], part)]

    def reduced(items):
        sizes = [x.shape[0] // nf for x in items]
        x = jnp.concatenate([x.reshape(nf, -1) for x in items], axis=1)
        x = lax.psum(x, ("ctx", "fsdp"))
        x = lax.dynamic_index_in_dim(x, f, 0, keepdims=False)
        out, at = [], 0
        for n in sizes:
            out.append(x[at : at + n])
            at += n
        return out

    out_bias_out, gain2_out, shift2_out, down_bias_out, up_bias_out = reduced(early)
    gain1_out, shift1_out, q_bias_out, v_bias_out = reduced(late)
    return (
        mixed,
        input_grad,
        gain1_out,
        shift1_out,
        qkv_out,
        q_bias_out,
        v_bias_out,
        out_out,
        out_bias_out,
        gain2_out,
        shift2_out,
        up_out,
        up_bias_out,
        down_out,
        down_bias_out,
    )


def solution(mesh):
    rows, flat = P(("ctx", "fsdp"), None), P("fsdp")
    mat = P("fsdp", None)
    in_specs = (
        rows,
        rows,
        mat,
        mat,
        flat,
        flat,
        mat,
        flat,
        flat,
        mat,
        flat,
        flat,
        flat,
        mat,
        flat,
        mat,
        flat,
    )
    out_specs = (
        rows,
        rows,
        flat,
        flat,
        mat,
        flat,
        flat,
        mat,
        flat,
        flat,
        flat,
        mat,
        flat,
        mat,
        flat,
    )
    return jax.shard_map(
        per_device, mesh=mesh, in_specs=in_specs, out_specs=out_specs, check_vma=False
    )
```

time: 2680 us -> 1220 us (0.46)
  waiting for transfers between devices: 1900 us -> 435 us
  matrix products: 459 us -> 281 us
  local copies, waits for them, and re-layouts: 31.4 us -> 175 us
  blocking collectives: 138 us -> 57.7 us
  starting transfers between devices: 0.54 us -> 73.4 us
  Pallas kernels: 0 us -> 59 us
    reduce_scatter x6 -> x4, waiting for transfers between devices: 972 us -> 74.2 us  [scatter_f(): return lax.psum_scatter(x, 'fsdp', scatter_dimension=0, tiled=True)]
    all_gather x6 -> x4, waiting for transfers between devices: 809 us -> 106 us  [gather_f(): return lax.all_gather(x, 'fsdp', axis=0, tiled=True)]
    ppermute x0 -> x62, waiting for transfers between devices: none -> 254 us  [swap(): return lax.ppermute(x, 'ctx', [(i, i ^ mask) for i in range(n)])]
    dot_general x17 -> x27, matrix products: 419 us -> 281 us  [the longest x13 113 us: dot_nt(): lax.dot_general(a, b, (((1,), (1,)), ((), ())), preferred_element_type=si...]
    psum x1, waiting for transfers between devices: 122 us -> 0.01 us  [reduced(): x = lax.psum(x, ('ctx', 'fsdp'))]
    convert_element_type x36 -> x8, other arithmetic: 97 us -> 10.8 us  [the longest x3 4.83 us: scatter_ctx(): p2_lo = (p2[:n].astype(single) + from_x.astype(single)).astype(half)]
    all_gather x9 -> x1, blocking collectives: 99.6 us -> 17.4 us  [per_device(): small_all = lax.all_gather(small, 'fsdp', axis=0).astype(single)]
    unnamed x130 -> x304, local copies, waits for them, and re-layouts: 10.3 us -> 87.5 us
  transfers between devices with their start and end apart: 13 -> 71, of which waited for: 12 -> 28; matrix products, arithmetic and copies ran while one was open for 17% -> 43% of each run, Pallas kernels for 0% -> 5%
where the time goes in v1:
time: 1220 us; the launch traced here: 1210 us
  waiting for transfers between devices  435 us (36%)
  matrix products  281 us (23%)
  local copies, waits for them, and re-layouts  175 us (14%)
  other arithmetic  101 us (8%)
  starting transfers between devices  73.4 us (6%)
  Pallas kernels  59 us (5%)
  blocking collectives  57.7 us (5%)
  between operations  26.6 us (2%)
    ppermute x62, waiting for transfers between devices, swap(): return lax.ppermute(x, 'ctx', [(i, i ^ mask) for i in range(n)])  254 us
    dot_general x13, matrix products, dot_nt(): lax.dot_general(a, b, (((1,), (1,)), ((), ())), preferred_element_type=si...  113 us
    all_gather x4, waiting for transfers between devices, gather_f(): return lax.all_gather(x, 'fsdp', axis=0, tiled=True)  106 us
    dot_general x10, matrix products, dot_nn(): lax.dot_general(a, b, (((1,), (0,)), ((), ())), preferred_element_type=si...  97.6 us
    unnamed x304, local copies, waits for them, and re-layouts  87.5 us
    reduce_scatter x4, waiting for transfers between devices, scatter_f(): return lax.psum_scatter(x, 'fsdp', scatter_dimension=0, tiled=True)  74.2 us
    ppermute x62, starting transfers between devices, swap(): return lax.ppermute(x, 'ctx', [(i, i ^ mask) for i in range(n)])  73 us
    dot_general x4, matrix products, dot_tn(): lax.dot_general(a, b, (((0,), (0,)), ((), ())), preferred_element_type=si...  71 us
  transfers between devices with their start and end apart: 71, of which 28 were waited for; matrix products, arithmetic and copies ran while one was open for 43% of the time, Pallas kernels for 5%

profile of v1, /device:TPU:0, one launch (start us, length us, event | category | flops | bytes accessed | tf_op | source)
XLA Modules:
  0.0 1207.9 jit_solution(4925745065841918242)
XLA Ops:
  35.7 17.4 %all-gather.1 = bf16[8,1,3072]{2,1,0:T(2,128)(2,1)S(1)} all-gather(bf16[1,1,3072]{2,1,0:T(2,128)(2,1)S(1)} %bitcast.188), channel_id=1, replica_groups=mesh['ctx'=4,'fsdp'=8] {'fsdp'}, dimensions={0}, use_global_device_ids=true | all-gather | bytes 55296 | tf_op jit(solution)/shard_map/all_gather | solution.py:261
  61.2 16.7 %collective-permute-done = bf16[256,2048]{1,0:T(8,128)(2,1)} collective-permute-done((bf16[256,2048]{1,0:T(8,128)(2,1)}, bf16[256,2048]{1,0:T(8,128)(2,1)}, u32[]{:S(2)}, u32[]{:S(2)}) %collective-permute-start) | collective-permute-done | bytes 1048608 | tf_op jit(solution)/shard_map/ppermute | solution.py:60
  121.9 19.7 %add_convert_fusion.refs_0_.refs_1_.refs_2_.refs_3_.refs_4_.refs_5_.refs_6_.refs_7_.refs_8_.refs_9_.refs_10_.refs_11_.refs_12_.refs_13_.refs_14_.refs_15_.refs_16_.refs_17_.refs_18_.refs_19_.refs_20_.refs_21_.refs_22_.refs_23_ = bf16[2048,1536]{1,0:T(8,128)(2,1)} fusion(bf16[2048,1536]{0,1:T(8,128)(2,1)} %all-gather.7.cloned.1.call-done, ...), kind=kOutput, calls=%fused_computation.10 | convolution fusion | flops 12916359168 | bytes 21010432 | tf_op jit(solution)/shard_map/dot_general | solution.py:24
  141.6 23.6 %attn_forward.1 = bf16[2048,512]{1,0:T(8,128)(2,1)S(1)} custom-call(s32[16]{0:T(128)S(1)} %select_reduce_fusion.inv_ref, f32[4]{0:T(128)S(1)} %multiply_power_fusion.slope_ref, ...), custom_call_target="tpu_custom_call" | custom-call | flops 20000000000 | bytes 8388608 | tf_op jit(solution)/shard_map/attn_forward/pallas_call | solution.py:179
  213.9 34.8 %all-gather.11.cloned.1.call-done = bf16[2048,2048]{0,1:T(8,128)(2,1)} async-done(((bf16[256,2048]{0,1:T(8,128)(2,1)}), bf16[2048,2048]{0,1:T(8,128)(2,1)}) %all-gather.11.cloned.1.call-update) | async-done | bytes 8388624 | tf_op jit(solution)/shard_map/all_gather | solution.py:252
  248.7 10.7 fusion.215
  259.4 71.1 %all-gather.13.cloned.1.call-done = bf16[1,2048,2048]{2,1,0:T(8,128)(2,1)} async-done(((bf16[1,256,2048]{2,1,0:T(8,128)(2,1)}), bf16[1,2048,2048]{2,1,0:T(8,128)(2,1)}) %all-gather.13.cloned.1.call-update) | async-done | bytes 8388624 | tf_op jit(solution)/shard_map/all_gather | solution.py:252
  330.5 11.0 fusion.57
  359.5 59.7 %collective-permute-done.9 = bf16[256,2048]{1,0:T(8,128)(2,1)S(1)} collective-permute-done((bf16[256,2048]{1,0:T(8,128)(2,1)}, bf16[256,2048]{1,0:T(8,128)(2,1)S(1)}, u32[]{:S(2)}, u32[]{:S(2)}) %collective-permute-start.9) | collective-permute-done | bytes 1048608 | tf_op jit(solution)/shard_map/ppermute | solution.py:60
  420.7 10.6 fusion.67
  446.0 10.2 fusion.117
  466.2 15.4 %multiply_convert_fusion.2 = (bf16[512,2048]{1,0:T(8,128)(2,1)}, bf16[512,2048]{1,0:T(8,128)(2,1)}, bf16[512,2048]{1,0:T(8,128)(2,1)}, bf16[512,2048]{1,0:T(8,128)(2,1)}, f32[512,2048]{1,0:T(8,128)}) fusion(f32[2048]{0:T(1024)S(1)} %bitcast.195, f32[512,2048]{1,0:T(8,128)} %copy-done.104, f32[512,2048]{1,0:T(8,128)} %fusion.117, f32[512,2048]{1,0:T(8,128)} %fusion.215, ...), kind=kOutput, calls=%fused_computation.105 | convolution fusion | flops 4341104640 | bytes 35659776 | tf_op jit(solution)/shard_map/dot_general | solution.py:24
  493.3 10.6 fusion.72
  536.4 11.8 fusion.62
  573.4 13.3 %collective-permute-done.18 = bf16[256,2048]{1,0:T(8,128)(2,1)} collective-permute-done((bf16[256,2048]{1,0:T(8,128)(2,1)}, bf16[256,2048]{1,0:T(8,128)(2,1)}, u32[]{:S(2)}, u32[]{:S(2)}) %collective-permute-start.18) | collective-permute-done | bytes 1048608 | tf_op jit(solution)/shard_map/ppermute | solution.py:60
  592.4 16.6 %collective-permute-done.29 = bf16[256,2048]{1,0:T(8,128)(2,1)S(1)} collective-permute-done((bf16[256,2048]{1,0:T(8,128)(2,1)S(1)}, bf16[256,2048]{1,0:T(8,128)(2,1)S(1)}, u32[]{:S(2)}, u32[]{:S(2)}) %collective-permute-start.29) | collective-permute-done | bytes 1048608 | tf_op jit(solution)/shard_map/ppermute | solution.py:60
  618.7 16.3 %collective-permute-done.11 = bf16[256,2048]{1,0:T(8,128)(2,1)} collective-permute-done((bf16[256,2048]{1,0:T(8,128)(2,1)}, bf16[256,2048]{1,0:T(8,128)(2,1)}, u32[]{:S(2)}, u32[]{:S(2)}) %collective-permute-start.11) | collective-permute-done | bytes 1048608 | tf_op jit(solution)/shard_map/ppermute | solution.py:60
  635.0 14.4 %collective-permute-done.17 = bf16[256,2048]{1,0:T(8,128)(2,1)} collective-permute-done((bf16[256,2048]{1,0:T(8,128)(2,1)}, bf16[256,2048]{1,0:T(8,128)(2,1)}, u32[]{:S(2)}, u32[]{:S(2)}) %collective-permute-start.17) | collective-permute-done | bytes 1048608 | tf_op jit(solution)/shard_map/ppermute | solution.py:60
  676.6 11.0 collective-permute-done.33
  694.9 35.4 %attn_backward.1 = (bf16[2048,512]{1,0:T(8,128)(2,1)S(1)}, bf16[2048,512]{1,0:T(8,128)(2,1)S(1)}, bf16[2048,512]{1,0:T(8,128)(2,1)}) custom-call(s32[16]{0:T(128)S(1)} %select_reduce_fusion.inv_ref, f32[4]{0:T(128)S(1)} %multiply_power_fusion.slope_ref, ...), custom_call_target="tpu_custom_call" | custom-call | flops 40000000000 | bytes 14680064 | tf_op jit(solution)/shard_map/attn_backward/pallas_call | solution.py:198
  747.1 15.8 %convolution_convert_fusion.2 = bf16[2048,1536]{1,0:T(8,128)(2,1)} fusion(bf16[2048,1536]{1,0:T(8,128)(2,1)S(1)} %get-tuple-element.86, bf16[2048,2048]{1,0:T(8,128)(2,1)S(1)} %bitcast.154, f32[2048]{0:T(1024)S(1)} %bitcast.192, f32[2048]{0:T(1024)S(1)} %bitcast.182, f32[2048]{0:T(1024)S(1)} %copy-done.88, f32[2048]{0:T(1024)S(1)} %copy-done.79), kind=kOutput, calls=%fused_computation.41 | convolution fusion | flops 12913213440 | bytes 21004288 | tf_op jit(solution)/shard_map/dot_general | solution.py:32
  776.6 22.9 %fusion.30 = bf16[2048,2048]{1,0:T(8,128)(2,1)} fusion(bf16[2048,2048]{1,0:T(8,128)(2,1)} %constant_dynamic-update-slice_fusion.47, bf16[512,2048]{1,0:T(8,128)(2,1)S(1)} %copy-done.112, bf16[512,2048]{1,0:T(8,128)(2,1)S(1)} %copy-done.111, bf16[512,2048]{1,0:T(8,128)(2,1)S(1)} %copy-done.109, bf16[512,2048]{1,0:T(8,128)(2,1)S(1)} %copy-done.107), kind=kOutput, calls=%fused_computation.38 | convolution fusion | flops 17217617920 | bytes 25165824 | tf_op jit(solution)/shard_map/dot_general | solution.py:32
  810.5 22.5 %convolution_convert_fusion = bf16[2048,2048]{1,0:T(8,128)(2,1)} fusion(bf16[2048,2048]{1,0:T(8,128)(2,1)} %constant_dynamic-update-slice_fusion.40, bf16[512,2048]{1,0:T(8,128)(2,1)S(1)} %copy-done.27, bf16[512,2048]{1,0:T(8,128)(2,1)S(1)} %copy-done.25, bf16[512,2048]{1,0:T(8,128)(2,1)S(1)} %copy-done.29, bf16[512,2048]{1,0:T(8,128)(2,1)S(1)} %copy-done.23), kind=kOutput, calls=%fused_computation.39 | convolution fusion | flops 17217617920 | bytes 25165824 | tf_op jit(solution)/shard_map/dot_general | solution.py:32
  887.5 14.7 %collective-permute-done.39 = bf16[256,2048]{1,0:T(8,128)(2,1)S(1)} collective-permute-done((bf16[256,2048]{1,0:T(8,128)(2,1)}, bf16[256,2048]{1,0:T(8,128)(2,1)S(1)}, u32[]{:S(2)}, u32[]{:S(2)}) %collective-permute-start.39) | collective-permute-done | bytes 1048608 | tf_op jit(solution)/shard_map/ppermute | solution.py:60
  906.8 17.8 %collective-permute-done.41 = bf16[256,2048]{1,0:T(8,128)(2,1)S(1)} collective-permute-done((bf16[256,2048]{1,0:T(8,128)(2,1)S(1)}, bf16[256,2048]{1,0:T(8,128)(2,1)S(1)}, u32[]{:S(2)}, u32[]{:S(2)}) %collective-permute-start.41) | collective-permute-done | bytes 1048608 | tf_op jit(solution)/shard_map/ppermute | solution.py:60
  924.6 14.0 %collective-permute-done.38 = bf16[256,2048]{1,0:T(8,128)(2,1)S(1)} collective-permute-done((bf16[256,2048]{1,0:T(8,128)(2,1)S(1)}, bf16[256,2048]{1,0:T(8,128)(2,1)S(1)}, u32[]{:S(2)}, u32[]{:S(2)}) %collective-permute-start.38) | collective-permute-done | bytes 1048608 | tf_op jit(solution)/shard_map/ppermute | solution.py:60
  955.6 40.3 %psum.14 = f32[8,1024]{1,0:T(8,128)S(1)} all-reduce(f32[8,1024]{1,0:T(8,128)S(1)} %pad_maximum_fusion.24), channel_id=1, replica_groups=mesh['ctx'=4,'fsdp'=8] {'ctx','fsdp'}, use_global_device_ids=true, to_apply=%region_16.17 | all-reduce | flops 8192 | bytes 65536 | tf_op jit(solution)/shard_map/psum | solution.py:387
  1005.2 43.4 %reduce-scatter.9.cloned.1.call-done = bf16[256,2048]{1,0:T(8,128)(2,1)} async-done(((bf16[2048,2048]{1,0:T(8,128)(2,1)}), bf16[256,2048]{1,0:T(8,128)(2,1)}) %reduce-scatter.9.cloned.1.call-update) | async-done | bytes 1048592 | tf_op jit(solution)/shard_map/reduce_scatter | solution.py:356
  1108.7 30.8 %reduce-scatter.7.cloned.1.call-done = bf16[256,2048]{1,0:T(8,128)(2,1)} async-done(((bf16[2048,2048]{1,0:T(8,128)(2,1)}), bf16[256,2048]{1,0:T(8,128)(2,1)}) %reduce-scatter.7.cloned.1.call-update) | async-done | bytes 1048592 | tf_op jit(solution)/shard_map/reduce_scatter | solution.py:356
  1149.7 12.7 %collective-permute-done.48 = bf16[256,2048]{1,0:T(8,128)(2,1)S(1)} collective-permute-done((bf16[256,2048]{1,0:T(8,128)(2,1)}, bf16[256,2048]{1,0:T(8,128)(2,1)S(1)}, u32[]{:S(2)}, u32[]{:S(2)}) %collective-permute-start.48) | collective-permute-done | bytes 1048608 | tf_op jit(solution)/shard_map/ppermute | solution.py:60
  1168.4 12.1 %copy.63 = f32[256,8,4,256]{3,2,1,0:T(4,128)} copy(f32[256,8,4,256]{3,1,0,2:T(8,128)} %pad_maximum_fusion.1) | data formatting | bytes 16777216 | tf_op jit(solution)/shard_map/stack | solution.py:364
  1180.5 10.7 reshape.394
  (590 shorter events, 493.5 us)
Async XLA Ops:
  7.2 114.7 %all-gather.7.cloned.1.call-start = ((), (), s32[]{:S(2)}) async-start(), calls=%async_computation.4 | async-start | bytes 7077888 | tf_op jit(solution)/shard_map/all_gather | solution.py:252
  14.8 184.5 %all-gather.9.cloned.1.call-start = ((), (), s32[]{:S(2)}) async-start(), calls=%async_computation.5 | async-start | bytes 9437184 | tf_op jit(solution)/shard_map/all_gather | solution.py:252
  16.0 232.7 %all-gather.11.cloned.1.call-start = ((), (), s32[]{:S(2)}) async-start(), calls=%async_computation.6 | async-start | bytes 9437184 | tf_op jit(solution)/shard_map/all_gather | solution.py:252
  25.9 304.5 %all-gather.13.cloned.1.call-start = ((), (), s32[]{:S(2)}) async-start(), calls=%async_computation.12 | async-start | bytes 9437184 | tf_op jit(solution)/shard_map/all_gather | solution.py:252
  27.5 61.2 %collective-permute-start.3 = (bf16[256,2048]{1,0:T(8,128)(2,1)}, bf16[256,2048]{1,0:T(8,128)(2,1)S(1)}, u32[]{:S(2)}, u32[]{:S(2)}) collective-permute-start(bf16[256,2048]{1,0:T(8,128)(2,1)} %get-tuple-element.170), channel_id=1, source_target_pairs={{0,16},{8,24},{16,0},{24,8},{1,17},{9,25},{17,1},{25,9},{2,18},{10... | collective-permute-start | bytes 3145736 | tf_op jit(solution)/shard_map/ppermute | solution.py:60
  30.5 62.4 %collective-permute-start.1 = (bf16[256,2048]{1,0:T(8,128)(2,1)}, bf16[256,2048]{1,0:T(8,128)(2,1)}, u32[]{:S(2)}, u32[]{:S(2)}) collective-permute-start(bf16[256,2048]{1,0:T(8,128)(2,1)} %get-tuple-element.170), channel_id=1, source_target_pairs={{0,8},{8,0},{16,24},{24,16},{1,9},{9,1},{17,25},{25,17},{2,10},{10... | collective-permute-start | bytes 3145736 | tf_op jit(solution)/shard_map/ppermute | solution.py:60
  32.0 63.5 %collective-permute-start.2 = (bf16[256,2048]{1,0:T(8,128)(2,1)}, bf16[256,2048]{1,0:T(8,128)(2,1)}, u32[]{:S(2)}, u32[]{:S(2)}) collective-permute-start(bf16[256,2048]{1,0:T(8,128)(2,1)} %get-tuple-element.171), channel_id=1, source_target_pairs={{0,16},{8,24},{16,0},{24,8},{1,17},{9,25},{17,1},{25,9},{2,18},{10... | collective-permute-start | bytes 3145736 | tf_op jit(solution)/shard_map/ppermute | solution.py:60
  35.3 812.3 %all-reduce.2.cloned.1.call-start = ((), (), s32[]{:S(2)}) async-start(), calls=%async_computation.9 | async-start | bytes 131072 | tf_op jit(solution)/shard_map/psum | solution.py:387
  173.6 185.3 %collective-permute-start.24 = (bf16[256,2048]{1,0:T(8,128)(2,1)}, bf16[256,2048]{1,0:T(8,128)(2,1)}, u32[]{:S(2)}, u32[]{:S(2)}) collective-permute-start(bf16[256,2048]{1,0:T(8,128)(2,1)} %get-tuple-element.145), channel_id=1, source_target_pairs={{0,16},{8,24},{16,0},{24,8},{1,17},{9,25},{17,1},{25,9},{2,18},{10... | collective-permute-start | bytes 3145736 | tf_op jit(solution)/shard_map/ppermute | solution.py:60
  175.0 173.0 %collective-permute-start.21 = (bf16[256,2048]{1,0:T(8,128)(2,1)}, bf16[256,2048]{1,0:T(8,128)(2,1)}, u32[]{:S(2)}, u32[]{:S(2)}) collective-permute-start(bf16[256,2048]{1,0:T(8,128)(2,1)} %get-tuple-element.145), channel_id=1, source_target_pairs={{0,8},{8,0},{16,24},{24,16},{1,9},{9,1},{17,25},{25,17},{2,10},{10... | collective-permute-start | bytes 3145736 | tf_op jit(solution)/shard_map/ppermute | solution.py:60
  189.3 160.3 %collective-permute-start.25 = (bf16[256,2048]{1,0:T(8,128)(2,1)}, bf16[256,2048]{1,0:T(8,128)(2,1)}, u32[]{:S(2)}, u32[]{:S(2)}) collective-permute-start(bf16[256,2048]{1,0:T(8,128)(2,1)} %get-tuple-element.146), channel_id=1, source_target_pairs={{0,16},{8,24},{16,0},{24,8},{1,17},{9,25},{17,1},{25,9},{2,18},{10... | collective-permute-start | bytes 3145736 | tf_op jit(solution)/shard_map/ppermute | solution.py:60
  211.9 139.1 %collective-permute-start.12 = (bf16[256,2048]{1,0:T(8,128)(2,1)}, bf16[256,2048]{1,0:T(8,128)(2,1)S(1)}, u32[]{:S(2)}, u32[]{:S(2)}) collective-permute-start(bf16[256,2048]{1,0:T(8,128)(2,1)} %get-tuple-element.149), channel_id=1, source_target_pairs={{0,16},{8,24},{16,0},{24,8},{1,17},{9,25},{17,1},{25,9},{2,18},{10... | collective-permute-start | bytes 3145736 | tf_op jit(solution)/shard_map/ppermute | solution.py:60
  212.6 139.0 %collective-permute-start.13 = (bf16[256,2048]{1,0:T(8,128)(2,1)}, bf16[256,2048]{1,0:T(8,128)(2,1)}, u32[]{:S(2)}, u32[]{:S(2)}) collective-permute-start(bf16[256,2048]{1,0:T(8,128)(2,1)} %get-tuple-element.150), channel_id=1, source_target_pairs={{0,16},{8,24},{16,0},{24,8},{1,17},{9,25},{17,1},{25,9},{2,18},{10... | collective-permute-start | bytes 3145736 | tf_op jit(solution)/shard_map/ppermute | solution.py:60
  348.0 188.4 %collective-permute-start.22 = (bf16[256,2048]{1,0:T(8,128)(2,1)}, bf16[256,2048]{1,0:T(8,128)(2,1)}, u32[]{:S(2)}, u32[]{:S(2)}) collective-permute-start(bf16[256,2048]{1,0:T(8,128)(2,1)} %get-tuple-element.146), channel_id=1, source_target_pairs={{0,8},{8,0},{16,24},{24,16},{1,9},{9,1},{17,25},{25,17},{2,10},{10... | collective-permute-start | bytes 3145736 | tf_op jit(solution)/shard_map/ppermute | solution.py:60
  349.5 143.8 %collective-permute-start.26 = (bf16[256,2048]{1,0:T(8,128)(2,1)}, bf16[256,2048]{1,0:T(8,128)(2,1)S(1)}, u32[]{:S(2)}, u32[]{:S(2)}) collective-permute-start(bf16[256,2048]{1,0:T(8,128)(2,1)} %collective-permute-done.21), channel_id=1, source_target_pairs={{0,16},{8,24},{16,0},{24,8},{1,17},{9,25},{17,1},{25,9},{2,18},{10... | collective-permute-start | bytes 3145736 | tf_op jit(solution)/shard_map/ppermute | solution.py:60
  351.0 142.3 %collective-permute-start.27 = (bf16[256,2048]{1,0:T(8,128)(2,1)}, bf16[256,2048]{1,0:T(8,128)(2,1)}, u32[]{:S(2)}, u32[]{:S(2)}) collective-permute-start(bf16[256,2048]{1,0:T(8,128)(2,1)} %collective-permute-done.25), channel_id=1, source_target_pairs={{0,8},{8,0},{16,24},{24,16},{1,9},{9,1},{17,25},{25,17},{2,10},{10... | collective-permute-start | bytes 3145736 | tf_op jit(solution)/shard_map/ppermute | solution.py:60
  351.6 67.6 %collective-permute-start.9 = (bf16[256,2048]{1,0:T(8,128)(2,1)}, bf16[256,2048]{1,0:T(8,128)(2,1)S(1)}, u32[]{:S(2)}, u32[]{:S(2)}) collective-permute-start(bf16[256,2048]{1,0:T(8,128)(2,1)} %get-tuple-element.149), channel_id=1, source_target_pairs={{0,8},{8,0},{16,24},{24,16},{1,9},{9,1},{17,25},{25,17},{2,10},{10... | collective-permute-start | bytes 3145736 | tf_op jit(solution)/shard_map/ppermute | solution.py:60
  358.9 85.6 %collective-permute-start.15 = (bf16[256,2048]{1,0:T(8,128)(2,1)}, bf16[256,2048]{1,0:T(8,128)(2,1)S(1)}, u32[]{:S(2)}, u32[]{:S(2)}) collective-permute-start(bf16[256,2048]{1,0:T(8,128)(2,1)} %collective-permute-done.13), channel_id=1, source_target_pairs={{0,8},{8,0},{16,24},{24,16},{1,9},{9,1},{17,25},{25,17},{2,10},{10... | collective-permute-start | bytes 3145736 | tf_op jit(solution)/shard_map/ppermute | solution.py:60
  444.5 145.8 %collective-permute-start.32 = (bf16[256,2048]{1,0:T(8,128)(2,1)}, bf16[256,2048]{1,0:T(8,128)(2,1)S(1)}, u32[]{:S(2)}, u32[]{:S(2)}) collective-permute-start(bf16[256,2048]{1,0:T(8,128)(2,1)} %slice.426), channel_id=1, source_target_pairs={{0,16},{8,24},{16,0},{24,8},{1,17},{9,25},{17,1},{25,9},{2,18},{10... | collective-permute-start | bytes 3145736 | tf_op jit(solution)/shard_map/ppermute | solution.py:60
  491.7 78.1 %collective-permute-start.16 = (bf16[256,2048]{1,0:T(8,128)(2,1)}, bf16[256,2048]{1,0:T(8,128)(2,1)}, u32[]{:S(2)}, u32[]{:S(2)}) collective-permute-start(bf16[256,2048]{1,0:T(8,128)(2,1)} %get-tuple-element.147), channel_id=1, source_target_pairs={{0,8},{8,0},{16,24},{24,16},{1,9},{9,1},{17,25},{25,17},{2,10},{10... | collective-permute-start | bytes 3145736 | tf_op jit(solution)/shard_map/ppermute | solution.py:60
  591.0 58.4 %collective-permute-start.17 = (bf16[256,2048]{1,0:T(8,128)(2,1)}, bf16[256,2048]{1,0:T(8,128)(2,1)}, u32[]{:S(2)}, u32[]{:S(2)}) collective-permute-start(bf16[256,2048]{1,0:T(8,128)(2,1)} %add_convert_fusion.8), channel_id=1, source_target_pairs={{0,16},{8,24},{16,0},{24,8},{1,17},{9,25},{17,1},{25,9},{2,18},{10... | collective-permute-start | bytes 3145736 | tf_op jit(solution)/shard_map/ppermute | solution.py:60
  676.6 266.8 %reduce-scatter.5.cloned.1.call-start = ((), (), s32[]{:S(2)}) async-start(), calls=%async_computation.7 | async-start | bytes 7077888 | tf_op jit(solution)/shard_map/reduce_scatter | solution.py:356
  762.9 238.0 %reduce-scatter.11.cloned.1.call-start = ((), (), s32[]{:S(2)}) async-start(), calls=%async_computation.11 | async-start | bytes 9437184 | tf_op jit(solution)/shard_map/reduce_scatter | solution.py:356
  799.5 249.0 %reduce-scatter.9.cloned.1.call-start = ((), (), s32[]{:S(2)}) async-start(), calls=%async_computation.10 | async-start | bytes 9437184 | tf_op jit(solution)/shard_map/reduce_scatter | solution.py:356
  833.0 306.4 %reduce-scatter.7.cloned.1.call-start = ((), (), s32[]{:S(2)}) async-start(), calls=%async_computation.8 | async-start | bytes 9437184 | tf_op jit(solution)/shard_map/reduce_scatter | solution.py:356
  945.4 54.5 %collective-permute-start.42 = (bf16[128,1536]{1,0:T(8,128)(2,1)}, bf16[128,1536]{1,0:T(8,128)(2,1)S(1)}, u32[]{:S(2)}, u32[]{:S(2)}) collective-permute-start(bf16[128,1536]{1,0:T(8,128)(2,1)} %get-tuple-element.176), channel_id=1, source_target_pairs={{0,8},{8,0},{16,24},{24,16},{1,9},{9,1},{17,25},{25,17},{2,10},{10... | collective-permute-start | bytes 1179656 | tf_op jit(solution)/shard_map/ppermute | solution.py:60
  946.9 53.9 %collective-permute-start.44 = (bf16[128,1536]{1,0:T(8,128)(2,1)}, bf16[128,1536]{1,0:T(8,128)(2,1)S(1)}, u32[]{:S(2)}, u32[]{:S(2)}) collective-permute-start(bf16[128,1536]{1,0:T(8,128)(2,1)} %get-tuple-element.177), channel_id=1, source_target_pairs={{0,16},{8,24},{16,0},{24,8},{1,17},{9,25},{17,1},{25,9},{2,18},{10... | collective-permute-start | bytes 1179656 | tf_op jit(solution)/shard_map/ppermute | solution.py:60
  996.6 54.3 %collective-permute-start.46 = (bf16[128,1536]{1,0:T(8,128)(2,1)}, bf16[128,1536]{1,0:T(8,128)(2,1)S(1)}, u32[]{:S(2)}, u32[]{:S(2)}) collective-permute-start(bf16[128,1536]{1,0:T(8,128)(2,1)} %get-tuple-element.176), channel_id=1, source_target_pairs={{0,16},{8,24},{16,0},{24,8},{1,17},{9,25},{17,1},{25,9},{2,18},{10... | collective-permute-start | bytes 1179656 | tf_op jit(solution)/shard_map/ppermute | solution.py:60
  998.9 53.5 %collective-permute-start.47 = (bf16[128,1536]{1,0:T(8,128)(2,1)}, bf16[128,1536]{1,0:T(8,128)(2,1)S(1)}, u32[]{:S(2)}, u32[]{:S(2)}) collective-permute-start(bf16[128,1536]{1,0:T(8,128)(2,1)} %get-tuple-element.177), channel_id=1, source_target_pairs={{0,8},{8,0},{16,24},{24,16},{1,9},{9,1},{17,25},{25,17},{2,10},{10... | collective-permute-start | bytes 1179656 | tf_op jit(solution)/shard_map/ppermute | solution.py:60
  999.9 53.9 %collective-permute-start.43 = (bf16[128,1536]{1,0:T(8,128)(2,1)S(1)}, bf16[128,1536]{1,0:T(8,128)(2,1)}, u32[]{:S(2)}, u32[]{:S(2)}) collective-permute-start(bf16[128,1536]{1,0:T(8,128)(2,1)S(1)} %collective-permute-done.42), channel_id=1, source_target_pairs={{0,16},{8,24},{16,0},{24,8},{1,17},{9,25},{17,1},{25,9},{2,18},{10... | collective-permute-start | bytes 1179656 | tf_op jit(solution)/shard_map/ppermute | solution.py:60
  1000.9 53.0 %collective-permute-start.45 = (bf16[128,1536]{1,0:T(8,128)(2,1)S(1)}, bf16[128,1536]{1,0:T(8,128)(2,1)}, u32[]{:S(2)}, u32[]{:S(2)}) collective-permute-start(bf16[128,1536]{1,0:T(8,128)(2,1)S(1)} %collective-permute-done.44), channel_id=1, source_target_pairs={{0,8},{8,0},{16,24},{24,16},{1,9},{9,1},{17,25},{25,17},{2,10},{10... | collective-permute-start | bytes 1179656 | tf_op jit(solution)/shard_map/ppermute | solution.py:60
  1003.3 55.0 %collective-permute-start.56 = (bf16[128,2048]{1,0:T(8,128)(2,1)}, bf16[128,2048]{1,0:T(8,128)(2,1)S(1)}, u32[]{:S(2)}, u32[]{:S(2)}) collective-permute-start(bf16[128,2048]{1,0:T(8,128)(2,1)} %get-tuple-element.172), channel_id=1, source_target_pairs={{0,8},{8,0},{16,24},{24,16},{1,9},{9,1},{17,25},{25,17},{2,10},{10... | collective-permute-start | bytes 1572872 | tf_op jit(solution)/shard_map/ppermute | solution.py:60
  (160 other events, 3336.9 us)
Sparse Core Ops, SparseCore 0:
  14.9 68.5 all-gather.6
  85.8 80.2 all-gather.8
  167.6 81.0 all-gather.10
  250.2 80.2 all-gather.12
  676.7 117.4 all-reduce.1
  796.3 70.6 reduce-scatter.4
  869.3 87.9 reduce-scatter.10
  959.5 89.0 reduce-scatter.8
  1051.5 87.9 reduce-scatter.6

commit v2 on v1

--- a/solution.py
+++ b/solution.py
@@ -211,6 +211,123 @@
         ),
         name="attn_backward",
     )(inv, slopes, *([joined] * 24), *([grad] * 8))
+
+
+def gather_small_kernel(nf, x_ref, o_ref, send_sem, recv_sem):
+    f = lax.axis_index("fsdp")
+    barrier = pltpu.get_barrier_semaphore()
+    for d in range(1, nf):
+        pl.semaphore_signal(
+            barrier,
+            inc=1,
+            device_id={"fsdp": lax.rem(f + d, nf)},
+            device_id_type=pl.DeviceIdType.MESH,
+        )
+    pl.semaphore_wait(barrier, nf - 1)
+    copies = []
+    for d in range(1, nf):
+        copies.append(
+            pltpu.make_async_remote_copy(
+                src_ref=x_ref,
+                dst_ref=o_ref.at[f],
+                send_sem=send_sem.at[d],
+                recv_sem=recv_sem.at[d],
+                device_id={"fsdp": lax.rem(f + d, nf)},
+                device_id_type=pl.DeviceIdType.MESH,
+            )
+        )
+        copies[-1].start()
+    o_ref[f] = x_ref[...]
+    for copy in copies:
+        copy.wait()
+
+
+def gather_small(x, nf):
+    return pl.pallas_call(
+        functools.partial(gather_small_kernel, nf),
+        out_shape=jax.ShapeDtypeStruct((nf,) + x.shape, single),
+        in_specs=[pl.BlockSpec(memory_space=pltpu.VMEM)],
+        out_specs=pl.BlockSpec(memory_space=pltpu.VMEM),
+        scratch_shapes=[pltpu.SemaphoreType.DMA((nf,)), pltpu.SemaphoreType.DMA((nf,))],
+        compiler_params=pltpu.CompilerParams(collective_id=1, has_side_effects=True),
+        name="gather_small",
+    )(x)
+
+
+def reduce_small_kernel(nf, nc, x_ref, o_ref, land, stage, send_sem, recv_sem):
+    f = lax.axis_index("fsdp")
+    c = lax.axis_index("ctx")
+    barrier = pltpu.get_barrier_semaphore()
+    for d in range(1, nf):
+        pl.semaphore_signal(
+            barrier,
+            inc=1,
+            device_id={"fsdp": lax.rem(f + d, nf)},
+            device_id_type=pl.DeviceIdType.MESH,
+        )
+    for d in range(1, nc):
+        pl.semaphore_signal(
+            barrier,
+            inc=1,
+            device_id={"ctx": lax.rem(c + d, nc)},
+            device_id_type=pl.DeviceIdType.MESH,
+        )
+    pl.semaphore_wait(barrier, nf + nc - 2)
+    copies = []
+    for d in range(1, nf):
+        to = lax.rem(f + d, nf)
+        copies.append(
+            pltpu.make_async_remote_copy(
+                src_ref=x_ref.at[to],
+                dst_ref=land.at[d],
+                send_sem=send_sem.at[d],
+                recv_sem=recv_sem.at[d],
+                device_id={"fsdp": to},
+                device_id_type=pl.DeviceIdType.MESH,
+            )
+        )
+        copies[-1].start()
+    total = x_ref[f]
+    for d in range(1, nf):
+        copies[d - 1].wait()
+        total = total + land[d]
+    stage[0] = total
+    copies = []
+    for d in range(1, nc):
+        copies.append(
+            pltpu.make_async_remote_copy(
+                src_ref=stage.at[0],
+                dst_ref=stage.at[d],
+                send_sem=send_sem.at[nf + d],
+                recv_sem=recv_sem.at[nf + d],
+                device_id={"ctx": lax.rem(c + d, nc)},
+                device_id_type=pl.DeviceIdType.MESH,
+            )
+        )
+        copies[-1].start()
+    for d in range(1, nc):
+        copies[d - 1].wait()
+        total = total + stage[d]
+    o_ref[...] = total
+
+
+def reduce_small(x, nf, nc, call):
+    block = x.shape[1:]
+    sems = pltpu.SemaphoreType.DMA((nf + nc,))
+    return pl.pallas_call(
+        functools.partial(reduce_small_kernel, nf, nc),
+        out_shape=jax.ShapeDtypeStruct(block, single),
+        in_specs=[pl.BlockSpec(memory_space=pltpu.VMEM)],
+        out_specs=pl.BlockSpec(memory_space=pltpu.VMEM),
+        scratch_shapes=[
+            pltpu.VMEM((nf,) + block, single),
+            pltpu.VMEM((nc,) + block, single),
+            sems,
+            sems,
+        ],
+        compiler_params=pltpu.CompilerParams(collective_id=call, has_side_effects=True),
+        name="reduce_small",
+    )(x)
 
 
 def per_device(
@@ -245,20 +362,35 @@
     fpart = wide // nf // CTX
     wpart = wide // CTX
 
+    def columns(x, width_each, stride, count):
+        return jnp.concatenate(
+            [
+                lax.dynamic_slice_in_dim(x, k * stride + c * width_each, width_each, axis=1)
+                for k in range(count)
+            ],
+            axis=1,
+        )
+
+    def after(x, *others):
+        return lax.optimization_barrier((x, others))[0]
+
     def pick(x, axis):
         return lax.dynamic_index_in_dim(x, c, axis, keepdims=False)
 
     def gather_f(x):
         return lax.all_gather(x, "fsdp", axis=0, tiled=True)
 
-    qkv_own = pick(qkv_weight.reshape(shard, 3, CTX, part), 2).reshape(shard, 3 * part)
-    up_own = pick(up_weight.reshape(shard, nf, CTX, fpart), 2).reshape(shard, wpart)
-    down_own = pick(down_weight.reshape(CTX, fpart, width), 0)
+    qkv_own = columns(qkv_weight, part, width, 3)
+    up_own = columns(up_weight, fpart, wide // nf, nf)
+    down_own = lax.dynamic_slice_in_dim(down_weight, c * fpart, fpart, axis=0)
     w_qkv = gather_f(qkv_own.astype(half))
     small = jnp.concatenate(
         [ln1_gain, ln1_shift, q_bias, v_bias, out_bias, ln2_gain, ln2_shift, down_bias, up_bias]
-    ).astype(half)
-    small_all = lax.all_gather(small, "fsdp", axis=0).astype(single)
+    )
+    small_len = small.shape[0]
+    small = jnp.pad(small, (0, -small_len % 1024)).reshape(-1, 128)
+    small_all = gather_small(small, nf).reshape(nf, -1)[:, :small_len]
+    small_all = small_all.astype(half).astype(single)
 
     def vector(k):
         return small_all[:, k * shard : (k + 1) * shard].reshape(width)
@@ -269,8 +401,6 @@
         [pick(bias_q.reshape(CTX, part), 0), jnp.zeros((part,), single), pick(bias_v.reshape(CTX, part), 0)]
     )
     w_out = gather_f(out_weight.astype(half))
-    w_down = gather_f(down_own.astype(half))
-    w_up = gather_f(up_own.astype(half))
 
     per = rows // SPAN
     table = jnp.arange(CTX * per, dtype=jnp.int32)
@@ -288,9 +418,11 @@
         return jnp.concatenate([h for p in pieces for h in p], axis=0)
 
     tok_all = join(gather_ctx(tokens))
+    w_down = gather_f(after(down_own.astype(half), tok_all))
     normed1, _ = norm_parts(tok_all.astype(single))
     a1 = (normed1 * gain1 + shift1).astype(half)
     joined = (dot_nn(a1, w_qkv) + bias_qkv).astype(half)
+    w_up = gather_f(after(up_own.astype(half), joined))
     attended = to_rows(attn_forward(joined, inv, slopes, heads, scale))
 
     def pieces_of(x):
@@ -317,59 +449,66 @@
         dh2[j] = dot_nt(du[j], w_up)
         if j:
             dh2[j] = dh2[j].astype(half)
+    dh2_own = dh2[0]
+    dh2 = scatter_ctx(dh2)
+    gb_all = jnp.concatenate(after(gb, dh2_own), axis=0)
+    du = jnp.concatenate(du, axis=0)
+    a2 = jnp.concatenate(a2_pieces, axis=0)
+    dz2 = jnp.concatenate(dz2_pieces, axis=0)
+    down_grad = dot_tn(gb_all, dz2).astype(half)
+    up_grad = dot_tn(a2, du).astype(half)
+    up_bias_grad = jnp.sum(du.astype(single), axis=0)
+    down_bias_grad = jnp.sum(dz2_own.astype(single), axis=0)
+    gb = after(gb, dh2_own)
     for j in reversed(range(CTX)):
         mix[j] = dot_nn(gb[j], w_down)
         if j:
             mix[j] = mix[j].astype(half)
-    dh2 = scatter_ctx(dh2)
     mixed = y1 + scatter_ctx(mix) + bias_d
-    gb = jnp.concatenate(gb, axis=0)
-    du = jnp.concatenate(du, axis=0)
-    a2 = jnp.concatenate(a2_pieces, axis=0)
-    dz2 = jnp.concatenate(dz2_pieces, axis=0)
-    down_grad = dot_tn(gb, dz2).astype(half)
-    up_grad = dot_tn(a2, du).astype(half)
-    up_bias_grad = jnp.sum(du.astype(single), axis=0)
-    down_bias_grad = jnp.sum(dz2_own.astype(single), axis=0)
     gain2_grad = jnp.sum(dh2 * normed2, axis=0)
     shift2_grad = jnp.sum(dh2, axis=0)
     dy1 = cotangent + norm_back(normed2, inv2, gain2, dh2)
 
+    def scatter_f(x):
+        return lax.psum_scatter(x, "fsdp", scatter_dimension=0, tiled=True)
+
+    down_part = scatter_f(down_grad)
     dz1 = dy1.astype(half)
     out_bias_grad = jnp.sum(dz1.astype(single), axis=0)
     out_grad = dot_tn(ob, dz1).astype(half)
+    up_part = scatter_f(after(up_grad, down_part))
     dattn = dot_nt(dz1, w_out).astype(half)
     dattn = xor_order([dattn[:, s * part : (s + 1) * part] for s in range(CTX)], c)
     dattn = jnp.concatenate([dattn[0]] + [swap(dattn[j], j) for j in range(1, CTX)], axis=0)
-    dqkv = jnp.concatenate(attn_backward(joined, dattn, inv, slopes, heads, scale), axis=1)
+    dqkv = jnp.concatenate(attn_backward(joined, after(dattn, up_grad), inv, slopes, heads, scale), axis=1)
     dqkv = to_rows(dqkv)
     dh1 = [dot_nt(p, w_qkv) for p in pieces_of(dqkv)]
+    dh1_own = dh1[0]
     dh1 = scatter_ctx(dh1[:1] + [p.astype(half) for p in dh1[1:]])
-    qkv_grad = dot_tn(a1, dqkv).astype(half)
+    qkv_grad = dot_tn(a1, after(dqkv, dh1_own)).astype(half)
     sums = jnp.sum(dqkv.astype(single), axis=0)
     normed1_own, inv1_own = norm_parts(tokens.astype(single))
     gain1_grad = jnp.sum(dh1 * normed1_own, axis=0)
     shift1_grad = jnp.sum(dh1, axis=0)
     input_grad = dy1 + norm_back(normed1_own, inv1_own, gain1, dh1)
 
-    def scatter_f(x):
-        return lax.psum_scatter(x, "fsdp", scatter_dimension=0, tiled=True)
+    out_part = scatter_f(after(out_grad, up_part))
+    qkv_part = scatter_f(after(qkv_grad, out_part))
 
     def everywhere(x):
         pieces = [jnp.concatenate(p, axis=0) for p in gather_ctx(x)]
         return xor_order([p.astype(single) for p in pieces], c)
 
-    down_out = jnp.concatenate(everywhere(scatter_f(down_grad)), axis=0)
-    up_out = everywhere(scatter_f(up_grad))
+    down_out = jnp.concatenate(everywhere(down_part), axis=0)
+    up_out = everywhere(up_part)
     up_out = jnp.stack([p.reshape(shard, nf, fpart) for p in up_out], axis=2).reshape(shard, wide)
-    out_part = scatter_f(out_grad)
     bit = 1
     while bit < CTX:
         out_part = out_part.astype(half)
         out_part = out_part.astype(single) + swap(out_part, bit).astype(single)
         bit *= 2
     out_out = out_part
-    qkv_out = everywhere(scatter_f(qkv_grad))
+    qkv_out = everywhere(qkv_part)
     qkv_out = jnp.stack([p.reshape(shard, 3, part) for p in qkv_out], axis=2)
     qkv_out = qkv_out.reshape(shard, 3 * width)
 
@@ -381,19 +520,19 @@
     early = [out_bias_grad, gain2_grad, shift2_grad, down_bias_grad, spread(up_bias_grad, fpart)]
     late = [gain1_grad, shift1_grad, spread(sums[:part], part), spread(sums[2 * part :], part)]
 
-    def reduced(items):
+    def reduced(items, call):
         sizes = [x.shape[0] // nf for x in items]
         x = jnp.concatenate([x.reshape(nf, -1) for x in items], axis=1)
-        x = lax.psum(x, ("ctx", "fsdp"))
-        x = lax.dynamic_index_in_dim(x, f, 0, keepdims=False)
+        x = jnp.pad(x, ((0, 0), (0, -x.shape[1] % 1024))).reshape(nf, -1, 128)
+        x = reduce_small(x, nf, CTX, call).reshape(-1)
         out, at = [], 0
         for n in sizes:
             out.append(x[at : at + n])
             at += n
         return out
 
-    out_bias_out, gain2_out, shift2_out, down_bias_out, up_bias_out = reduced(early)
-    gain1_out, shift1_out, q_bias_out, v_bias_out = reduced(late)
+    out_bias_out, gain2_out, shift2_out, down_bias_out, up_bias_out = reduced(early, 2)
+    gain1_out, shift1_out, q_bias_out, v_bias_out = reduced(late, 3)
     return (
         mixed,
         input_grad,

time: 1220 us -> 1080 us (0.89)
  blocking collectives: 57.7 us -> 0 us
  local copies, waits for them, and re-layouts: 175 us -> 129 us
  waiting for transfers between devices: 435 us -> 393 us
  Pallas kernels: 59 us -> 92.6 us
  other arithmetic: 101 us -> 79 us
    ppermute x62, waiting for transfers between devices: 254 us -> 353 us  [swap(): return lax.ppermute(x, 'ctx', [(i, i ^ mask) for i in range(n)])]
    all_gather x4, waiting for transfers between devices: 106 us -> 22.7 us  [gather_f(): return lax.all_gather(x, 'fsdp', axis=0, tiled=True)]
    reduce_scatter x4, waiting for transfers between devices: 74.2 us -> 16.6 us  [scatter_f(): return lax.psum_scatter(x, 'fsdp', scatter_dimension=0, tiled=True)]
    psum x1 -> x0, blocking collectives: 40.3 us -> none  [reduced(): x = lax.psum(x, ('ctx', 'fsdp'))]
    pallas_call x0 -> x3, Pallas kernels: none -> 33.5 us  [the longest x2 23.9 us: reduce_small(): pl.pallas_call(functools.partial(reduce_small_kernel, nf, nc), out_shape=...]
    unnamed x304 -> x269, local copies, waits for them, and re-layouts: 87.5 us -> 69.2 us
    all_gather x1 -> x0, blocking collectives: 17.4 us -> none  [per_device(): small_all = lax.all_gather(small, 'fsdp', axis=0).astype(single)]
  transfers between devices with their start and end apart: 71 -> 70, of which waited for: 28 -> 40; matrix products, arithmetic and copies ran while one was open for 43% -> 38% of each run, Pallas kernels for 5% -> 9%
where the time goes in v2:
time: 1080 us; the launch traced here: 1070 us
  waiting for transfers between devices  393 us (36%)
  matrix products  281 us (26%)
  local copies, waits for them, and re-layouts  129 us (12%)
  Pallas kernels  92.6 us (9%)
  other arithmetic  79 us (7%)
  starting transfers between devices  69.7 us (6%)
  between operations  26.7 us (2%)
    ppermute x62, waiting for transfers between devices, swap(): return lax.ppermute(x, 'ctx', [(i, i ^ mask) for i in range(n)])  353 us
    dot_general x13, matrix products, dot_nt(): lax.dot_general(a, b, (((1,), (1,)), ((), ())), preferred_element_type=si...  117 us
    dot_general x10, matrix products, dot_nn(): lax.dot_general(a, b, (((1,), (0,)), ((), ())), preferred_element_type=si...  97.3 us
    unnamed x269, local copies, waits for them, and re-layouts  69.2 us
    ppermute x62, starting transfers between devices, swap(): return lax.ppermute(x, 'ctx', [(i, i ^ mask) for i in range(n)])  68.9 us
    dot_general x4, matrix products, dot_tn(): lax.dot_general(a, b, (((0,), (0,)), ((), ())), preferred_element_type=si...  67.3 us
    pallas_call x1, Pallas kernels, attn_backward(): pl.pallas_call(functools.partial(attn_bwd_kernel, scale), grid_spec=pltpu...  35.3 us
    pallas_call x2, Pallas kernels, reduce_small(): pl.pallas_call(functools.partial(reduce_small_kernel, nf, nc), out_shape=...  23.9 us
  transfers between devices with their start and end apart: 70, of which 40 were waited for; matrix products, arithmetic and copies ran while one was open for 38% of the time, Pallas kernels for 9%

profile of v2, /device:TPU:0, one launch (start us, length us, event | category | flops | bytes accessed | tf_op | source)
XLA Modules:
  0.0 1071.0 jit_solution(16585447720256105996)
XLA Ops:
  43.6 22.4 %collective-permute-done.3 = bf16[256,2048]{1,0:T(8,128)(2,1)} collective-permute-done((bf16[256,2048]{1,0:T(8,128)(2,1)}, bf16[256,2048]{1,0:T(8,128)(2,1)}, u32[]{:S(2)}, u32[]{:S(2)}) %collective-permute-start.3) | collective-permute-done | bytes 1048608 | tf_op jit(solution)/shard_map/ppermute | solution.py:60
  71.3 15.7 %collective-permute-done.4 = bf16[256,2048]{1,0:T(8,128)(2,1)S(1)} collective-permute-done((bf16[256,2048]{1,0:T(8,128)(2,1)}, bf16[256,2048]{1,0:T(8,128)(2,1)S(1)}, u32[]{:S(2)}, u32[]{:S(2)}) %collective-permute-start.4) | collective-permute-done | bytes 1048608 | tf_op jit(solution)/shard_map/ppermute | solution.py:60
  94.5 19.3 %add_convert_fusion.refs_0_.refs_1_.refs_2_.refs_3_.refs_4_.refs_5_.refs_6_.refs_7_.refs_8_.refs_9_.refs_10_.refs_11_.refs_12_.refs_13_.refs_14_.refs_15_.refs_16_.refs_17_.refs_18_.refs_19_.refs_20_.refs_21_.refs_22_.refs_23_ = bf16[2048,1536]{1,0:T(8,128)(2,1)} fusion(bf16[2048,1536]{1,0:T(8,128)(2,1)} %all-gather.5.cloned.1.call-done, ...), kind=kOutput, calls=%fused_computation.10 | convolution fusion | flops 12916359168 | bytes 21010432 | tf_op jit(solution)/shard_map/dot_general | solution.py:24
  136.8 23.8 %attn_forward.1 = bf16[2048,512]{1,0:T(8,128)(2,1)S(1)} custom-call(s32[16]{0:T(128)S(1)} %select_reduce_fusion.inv_ref, f32[4]{0:T(128)S(1)} %multiply_power_fusion.slope_ref, ...), custom_call_target="tpu_custom_call" | custom-call | flops 20000000000 | bytes 8388608 | tf_op jit(solution)/shard_map/attn_forward/pallas_call | solution.py:179
  168.0 15.7 %collective-permute-done.7 = bf16[512,512]{1,0:T(8,128)(2,1)S(1)} collective-permute-done((bf16[512,512]{1,0:T(8,128)(2,1)S(1)}, bf16[512,512]{1,0:T(8,128)(2,1)S(1)}, u32[]{:S(2)}, u32[]{:S(2)}) %collective-permute-start.7) | collective-permute-done | bytes 524320 | tf_op jit(solution)/shard_map/ppermute | solution.py:60
  218.2 10.6 collective-permute-done.26
  236.6 14.6 %collective-permute-done.12 = bf16[256,2048]{1,0:T(8,128)(2,1)} collective-permute-done((bf16[256,2048]{1,0:T(8,128)(2,1)S(1)}, bf16[256,2048]{1,0:T(8,128)(2,1)}, u32[]{:S(2)}, u32[]{:S(2)}) %collective-permute-start.12) | collective-permute-done | bytes 1048608 | tf_op jit(solution)/shard_map/ppermute | solution.py:60
  252.7 26.0 %collective-permute-done.9 = bf16[256,2048]{1,0:T(8,128)(2,1)} collective-permute-done((bf16[256,2048]{1,0:T(8,128)(2,1)}, bf16[256,2048]{1,0:T(8,128)(2,1)}, u32[]{:S(2)}, u32[]{:S(2)}) %collective-permute-start.9) | collective-permute-done | bytes 1048608 | tf_op jit(solution)/shard_map/ppermute | solution.py:60
  279.2 10.8 %fusion.64 = f32[512,2048]{1,0:T(8,128)} fusion(bf16[2048,2048]{1,0:T(8,128)(2,1)} %all-gather.9.cloned.1.call-done, bf16[256,2048]{1,0:T(8,128)(2,1)} %collective-permute-done.10, bf16[256,2048]{1,0:T(8,128)(2,1)} %collective-permute-done.9), kind=kOutput, calls=%fused_computation.131 | convolution fusion | flops 4299161600 | bytes 14680064 | tf_op jit(solution)/shard_map/dot_general | solution.py:24
  304.2 22.7 %all-gather.11.cloned.1.call-done = bf16[2048,2048]{1,0:T(8,128)(2,1)} async-done(((bf16[256,2048]{1,0:T(8,128)(2,1)}), bf16[2048,2048]{1,0:T(8,128)(2,1)}) %all-gather.11.cloned.1.call-update) | async-done | bytes 8388624 | tf_op jit(solution)/shard_map/all_gather | solution.py:381
  326.9 10.8 %fusion.41 = bf16[512,2048]{1,0:T(8,128)(2,1)S(1)} fusion(f32[512,2048]{1,0:T(8,128)} %fusion.176, bf16[2048,2048]{1,0:T(8,128)(2,1)} %all-gather.11.cloned.1.call-done, bf16[512,2048]{1,0:T(8,128)(2,1)S(1)} %copy-done.11, f32[2048]{0:T(1024)S(1)} %bitcast.181), kind=kOutput, calls=%fused_computation.62 | convolution fusion | flops 4318035968 | bytes 16785408 | tf_op jit(solution)/shard_map/dot_general | solution.py:28
  337.8 10.3 fusion.177
  348.1 15.3 %multiply_convert_fusion = (bf16[512,2048]{1,0:T(8,128)(2,1)}, bf16[512,2048]{1,0:T(8,128)(2,1)}, bf16[512,2048]{1,0:T(8,128)(2,1)}, bf16[512,2048]{1,0:T(8,128)(2,1)S(1)}, f32[512,2048]{1,0:T(8,128)}) fusion(f32[2048]{0:T(1024)S(1)} %bitcast.182, f32[512,2048]{1,0:T(8,128)} %fusion.64, f32[512,2048]{1,0:T(8,128)} %fusion.68, ...), kind=kOutput, calls=%fused_computation.87 | convolution fusion | flops 4341104640 | bytes 35659776 | tf_op jit(solution)/shard_map/dot_general | solution.py:24
  364.7 21.9 %fusion.14 = bf16[2048,2048]{1,0:T(8,128)(2,1)} fusion(bf16[2048,2048]{1,0:T(8,128)(2,1)S(1)} %bitcast.158, bf16[512,2048]{1,0:T(8,128)(2,1)} %get-tuple-element.34, bf16[512,2048]{1,0:T(8,128)(2,1)} %get-tuple-element.33, bf16[512,2048]{1,0:T(8,128)(2,1)} %get-tuple-element.32, bf16[512,2048]{1,0:T(8,128)(2,1)S(1)} %get-tuple-element.31), kind=kOutput, calls=%fused_computation.22 | convolution fusion | flops 17217617920 | bytes 25165824 | tf_op jit(solution)/shard_map/dot_general | solution.py:32
  401.3 10.5 fusion.51
  421.7 12.7 %fusion.56 = bf16[512,2048]{1,0:T(8,128)(2,1)S(1)} fusion(f32[512,2048]{1,0:T(8,128)} %get-tuple-element.230, bf16[2048,2048]{1,0:T(8,128)(2,1)} %all-gather.11.cloned.1.call-done, bf16[256,2048]{1,0:T(8,128)(2,1)} %collective-permute-done.27, bf16[256,2048]{1,0:T(8,128)(2,1)} %collective-permute-done.26, f32[2048]{0:T(1024)S(1)} %bitcast.185), kind=kOutput, calls=%fused_computation.77 | convolution fusion | flops 4322230272 | bytes 16785408 | tf_op jit(solution)/shard_map/dot_general | solution.py:28
  435.7 22.7 %convolution_convert_fusion.1 = bf16[2048,2048]{1,0:T(8,128)(2,1)} fusion(bf16[2048,2048]{1,0:T(8,128)(2,1)} %constant_dynamic-update-slice_fusion.8, bf16[512,2048]{1,0:T(8,128)(2,1)S(1)} %fusion.56, bf16[512,2048]{1,0:T(8,128)(2,1)S(1)} %fusion.51, bf16[512,2048]{1,0:T(8,128)(2,1)S(1)} %fusion.46, bf16[512,2048]{1,0:T(8,128)(2,1)S(1)} %copy-done.26), kind=kOutput, calls=%fused_computation.24 | convolution fusion | flops 17217617920 | bytes 25165824 | tf_op jit(solution)/shard_map/dot_general | solution.py:32
  458.4 16.6 %reduce-scatter.5.cloned.1.call-done = bf16[256,2048]{1,0:T(8,128)(2,1)} async-done(((bf16[2048,2048]{1,0:T(8,128)(2,1)}), bf16[256,2048]{1,0:T(8,128)(2,1)}) %reduce-scatter.5.cloned.1.call-update) | async-done | bytes 1048592 | tf_op jit(solution)/shard_map/reduce_scatter | solution.py:473
  541.3 12.6 %collective-permute-done.30 = bf16[256,2048]{1,0:T(8,128)(2,1)S(1)} collective-permute-done((bf16[256,2048]{1,0:T(8,128)(2,1)S(1)}, bf16[256,2048]{1,0:T(8,128)(2,1)S(1)}, u32[]{:S(2)}, u32[]{:S(2)}) %collective-permute-start.30) | collective-permute-done | bytes 1048608 | tf_op jit(solution)/shard_map/ppermute | solution.py:60
  557.3 19.1 %collective-permute-done.18 = bf16[256,2048]{1,0:T(8,128)(2,1)S(1)} collective-permute-done((bf16[256,2048]{1,0:T(8,128)(2,1)S(1)}, bf16[256,2048]{1,0:T(8,128)(2,1)S(1)}, u32[]{:S(2)}, u32[]{:S(2)}) %collective-permute-start.18) | collective-permute-done | bytes 1048608 | tf_op jit(solution)/shard_map/ppermute | solution.py:60
  579.9 19.0 %collective-permute-done.29 = bf16[256,2048]{1,0:T(8,128)(2,1)S(1)} collective-permute-done((bf16[256,2048]{1,0:T(8,128)(2,1)S(1)}, bf16[256,2048]{1,0:T(8,128)(2,1)S(1)}, u32[]{:S(2)}, u32[]{:S(2)}) %collective-permute-start.29) | collective-permute-done | bytes 1048608 | tf_op jit(solution)/shard_map/ppermute | solution.py:60
  603.2 18.1 %collective-permute-done.20 = bf16[256,2048]{1,0:T(8,128)(2,1)S(1)} collective-permute-done((bf16[256,2048]{1,0:T(8,128)(2,1)S(1)}, bf16[256,2048]{1,0:T(8,128)(2,1)S(1)}, u32[]{:S(2)}, u32[]{:S(2)}) %collective-permute-start.20) | collective-permute-done | bytes 1048608 | tf_op jit(solution)/shard_map/ppermute | solution.py:60
  621.3 19.3 %collective-permute-done.17 = bf16[256,2048]{1,0:T(8,128)(2,1)S(1)} collective-permute-done((bf16[256,2048]{1,0:T(8,128)(2,1)S(1)}, bf16[256,2048]{1,0:T(8,128)(2,1)S(1)}, u32[]{:S(2)}, u32[]{:S(2)}) %collective-permute-start.17) | collective-permute-done | bytes 1048608 | tf_op jit(solution)/shard_map/ppermute | solution.py:60
  672.1 11.7 %collective-permute-done.35 = bf16[512,512]{1,0:T(8,128)(2,1)} collective-permute-done((bf16[512,512]{1,0:T(8,128)(2,1)}, bf16[512,512]{1,0:T(8,128)(2,1)}, u32[]{:S(2)}, u32[]{:S(2)}) %collective-permute-start.35) | collective-permute-done | bytes 524320 | tf_op jit(solution)/shard_map/ppermute | solution.py:60
  693.3 35.3 %attn_backward.1 = (bf16[2048,512]{1,0:T(8,128)(2,1)S(1)}, bf16[2048,512]{1,0:T(8,128)(2,1)S(1)}, bf16[2048,512]{1,0:T(8,128)(2,1)}) custom-call(s32[16]{0:T(128)S(1)} %copy-done.3, f32[4]{0:T(128)S(1)} %copy-done.1, ...), custom_call_target="tpu_custom_call" | custom-call | flops 40000000000 | bytes 14680064 | tf_op jit(solution)/shard_map/attn_backward/pallas_call | solution.py:198
  746.2 15.9 %convolution_convert_fusion.2 = bf16[2048,1536]{1,0:T(8,128)(2,1)} fusion(bf16[2048,1536]{1,0:T(8,128)(2,1)S(1)} %copy-done.21, bf16[2048,2048]{1,0:T(8,128)(2,1)S(1)} %bitcast.141, f32[2048]{0:T(1024)S(1)} %bitcast.180, f32[2048]{0:T(1024)S(1)} %bitcast.168, f32[2048]{0:T(1024)S(1)} %copy-done.70, f32[2048]{0:T(1024)S(1)} %copy-done.62), kind=kOutput, calls=%fused_computation.25 | convolution fusion | flops 12913213440 | bytes 21004288 | tf_op jit(solution)/shard_map/dot_general | solution.py:32
  767.9 13.9 %reduce_small.3 = f32[16,128]{1,0:T(8,128)} custom-call(f32[8,16,128]{2,1,0:T(8,128)} %bitcast.161), custom_call_target="tpu_custom_call" | custom-call | tf_op jit(solution)/shard_map/reduce_small/pallas_call | solution.py:317
  847.2 21.4 %collective-permute-done.38 = bf16[256,2048]{1,0:T(8,128)(2,1)S(1)} collective-permute-done((bf16[256,2048]{1,0:T(8,128)(2,1)S(1)}, bf16[256,2048]{1,0:T(8,128)(2,1)S(1)}, u32[]{:S(2)}, u32[]{:S(2)}) %collective-permute-start.38) | collective-permute-done | bytes 1048608 | tf_op jit(solution)/shard_map/ppermute | solution.py:60
  911.3 10.1 collective-permute-done.59
  957.4 18.4 %collective-permute-done.48 = bf16[256,2048]{1,0:T(8,128)(2,1)S(1)} collective-permute-done((bf16[256,2048]{1,0:T(8,128)(2,1)S(1)}, bf16[256,2048]{1,0:T(8,128)(2,1)S(1)}, u32[]{:S(2)}, u32[]{:S(2)}) %collective-permute-start.48) | collective-permute-done | bytes 1048608 | tf_op jit(solution)/shard_map/ppermute | solution.py:60
  992.7 12.2 %copy.50 = f32[256,8,4,256]{3,2,1,0:T(4,128)} copy(f32[256,8,4,256]{3,1,0,2:T(8,128)} %pad_maximum_fusion.1) | data formatting | bytes 16777216 | tf_op jit(solution)/shard_map/stack | solution.py:504
  1004.8 10.7 %reshape.269 = f32[256,8192]{1,0:T(8,128)} reshape(f32[256,8,4,256]{3,2,1,0:T(4,128)} %copy.50) | data formatting | bytes 16777216 | tf_op jit(solution)/shard_map/reshape | solution.py:504
  (540 shorter events, 504.1 us)
Async XLA Ops:
  7.2 87.3 %all-gather.5.cloned.1.call-start = ((), (), s32[]{:S(2)}) async-start(), calls=%async_computation.4 | async-start | bytes 7077888 | tf_op jit(solution)/shard_map/all_gather | solution.py:381
  9.9 181.7 %all-gather.7.cloned.1.call-start = ((), (), s32[]{:S(2)}) async-start(), calls=%async_computation.5 | async-start | bytes 9437184 | tf_op jit(solution)/shard_map/all_gather | solution.py:381
  12.7 266.5 %all-gather.9.cloned.1.call-start = ((), (), s32[]{:S(2)}) async-start(), calls=%async_computation.6 | async-start | bytes 9437184 | tf_op jit(solution)/shard_map/all_gather | solution.py:381
  17.2 51.5 %collective-permute-start.2 = (bf16[256,2048]{1,0:T(8,128)(2,1)}, bf16[256,2048]{1,0:T(8,128)(2,1)}, u32[]{:S(2)}, u32[]{:S(2)}) collective-permute-start(bf16[256,2048]{1,0:T(8,128)(2,1)} %get-tuple-element.181), channel_id=1, source_target_pairs={{0,16},{8,24},{16,0},{24,8},{1,17},{9,25},{17,1},{25,9},{2,18},{10... | collective-permute-start | bytes 3145736 | tf_op jit(solution)/shard_map/ppermute | solution.py:60
  18.7 48.7 %collective-permute-start.1 = (bf16[256,2048]{1,0:T(8,128)(2,1)}, bf16[256,2048]{1,0:T(8,128)(2,1)}, u32[]{:S(2)}, u32[]{:S(2)}) collective-permute-start(bf16[256,2048]{1,0:T(8,128)(2,1)} %get-tuple-element.180), channel_id=1, source_target_pairs={{0,8},{8,0},{16,24},{24,16},{1,9},{9,1},{17,25},{25,17},{2,10},{10... | collective-permute-start | bytes 3145736 | tf_op jit(solution)/shard_map/ppermute | solution.py:60
  19.2 46.8 %collective-permute-start.3 = (bf16[256,2048]{1,0:T(8,128)(2,1)}, bf16[256,2048]{1,0:T(8,128)(2,1)}, u32[]{:S(2)}, u32[]{:S(2)}) collective-permute-start(bf16[256,2048]{1,0:T(8,128)(2,1)} %get-tuple-element.180), channel_id=1, source_target_pairs={{0,16},{8,24},{16,0},{24,8},{1,17},{9,25},{17,1},{25,9},{2,18},{10... | collective-permute-start | bytes 3145736 | tf_op jit(solution)/shard_map/ppermute | solution.py:60
  41.5 45.5 %collective-permute-start.4 = (bf16[256,2048]{1,0:T(8,128)(2,1)}, bf16[256,2048]{1,0:T(8,128)(2,1)S(1)}, u32[]{:S(2)}, u32[]{:S(2)}) collective-permute-start(bf16[256,2048]{1,0:T(8,128)(2,1)} %collective-permute-done), channel_id=1, source_target_pairs={{0,16},{8,24},{16,0},{24,8},{1,17},{9,25},{17,1},{25,9},{2,18},{10... | collective-permute-start | bytes 3145736 | tf_op jit(solution)/shard_map/ppermute | solution.py:60
  113.9 213.0 %all-gather.11.cloned.1.call-start = ((), (), s32[]{:S(2)}) async-start(), calls=%async_computation.7 | async-start | bytes 9437184 | tf_op jit(solution)/shard_map/all_gather | solution.py:381
  116.7 358.3 %reduce-scatter.5.cloned.1.call-start = ((), (), s32[]{:S(2)}) async-start(), calls=%async_computation.8 | async-start | bytes 9437184 | tf_op jit(solution)/shard_map/reduce_scatter | solution.py:473
  122.9 44.1 %collective-permute-start.25 = (bf16[256,2048]{1,0:T(8,128)(2,1)}, bf16[256,2048]{1,0:T(8,128)(2,1)S(1)}, u32[]{:S(2)}, u32[]{:S(2)}) collective-permute-start(bf16[256,2048]{1,0:T(8,128)(2,1)} %get-tuple-element.156), channel_id=1, source_target_pairs={{0,16},{8,24},{16,0},{24,8},{1,17},{9,25},{17,1},{25,9},{2,18},{10... | collective-permute-start | bytes 3145736 | tf_op jit(solution)/shard_map/ppermute | solution.py:60
  166.9 44.3 %collective-permute-start.22 = (bf16[256,2048]{1,0:T(8,128)(2,1)}, bf16[256,2048]{1,0:T(8,128)(2,1)}, u32[]{:S(2)}, u32[]{:S(2)}) collective-permute-start(bf16[256,2048]{1,0:T(8,128)(2,1)} %get-tuple-element.156), channel_id=1, source_target_pairs={{0,8},{8,0},{16,24},{24,16},{1,9},{9,1},{17,25},{25,17},{2,10},{10... | collective-permute-start | bytes 3145736 | tf_op jit(solution)/shard_map/ppermute | solution.py:60
  183.7 45.0 %collective-permute-start.26 = (bf16[256,2048]{1,0:T(8,128)(2,1)}, bf16[256,2048]{1,0:T(8,128)(2,1)}, u32[]{:S(2)}, u32[]{:S(2)}) collective-permute-start(bf16[256,2048]{1,0:T(8,128)(2,1)} %collective-permute-done.21), channel_id=1, source_target_pairs={{0,16},{8,24},{16,0},{24,8},{1,17},{9,25},{17,1},{25,9},{2,18},{10... | collective-permute-start | bytes 3145736 | tf_op jit(solution)/shard_map/ppermute | solution.py:60
  185.2 48.5 %collective-permute-start.27 = (bf16[256,2048]{1,0:T(8,128)(2,1)S(1)}, bf16[256,2048]{1,0:T(8,128)(2,1)}, u32[]{:S(2)}, u32[]{:S(2)}) collective-permute-start(bf16[256,2048]{1,0:T(8,128)(2,1)S(1)} %collective-permute-done.25), channel_id=1, source_target_pairs={{0,8},{8,0},{16,24},{24,16},{1,9},{9,1},{17,25},{25,17},{2,10},{10... | collective-permute-start | bytes 3145736 | tf_op jit(solution)/shard_map/ppermute | solution.py:60
  203.3 75.9 %collective-permute-start.10 = (bf16[256,2048]{1,0:T(8,128)(2,1)S(1)}, bf16[256,2048]{1,0:T(8,128)(2,1)}, u32[]{:S(2)}, u32[]{:S(2)}) collective-permute-start(bf16[256,2048]{1,0:T(8,128)(2,1)S(1)} %get-tuple-element.160), channel_id=1, source_target_pairs={{0,8},{8,0},{16,24},{24,16},{1,9},{9,1},{17,25},{25,17},{2,10},{10... | collective-permute-start | bytes 3145736 | tf_op jit(solution)/shard_map/ppermute | solution.py:60
  206.3 44.9 %collective-permute-start.12 = (bf16[256,2048]{1,0:T(8,128)(2,1)S(1)}, bf16[256,2048]{1,0:T(8,128)(2,1)}, u32[]{:S(2)}, u32[]{:S(2)}) collective-permute-start(bf16[256,2048]{1,0:T(8,128)(2,1)S(1)} %get-tuple-element.160), channel_id=1, source_target_pairs={{0,16},{8,24},{16,0},{24,8},{1,17},{9,25},{17,1},{25,9},{2,18},{10... | collective-permute-start | bytes 3145736 | tf_op jit(solution)/shard_map/ppermute | solution.py:60
  211.2 67.4 %collective-permute-start.9 = (bf16[256,2048]{1,0:T(8,128)(2,1)}, bf16[256,2048]{1,0:T(8,128)(2,1)}, u32[]{:S(2)}, u32[]{:S(2)}) collective-permute-start(bf16[256,2048]{1,0:T(8,128)(2,1)} %get-tuple-element.159), channel_id=1, source_target_pairs={{0,8},{8,0},{16,24},{24,16},{1,9},{9,1},{17,25},{25,17},{2,10},{10... | collective-permute-start | bytes 3145736 | tf_op jit(solution)/shard_map/ppermute | solution.py:60
  236.0 60.4 %collective-permute-start.11 = (bf16[256,2048]{1,0:T(8,128)(2,1)}, bf16[256,2048]{1,0:T(8,128)(2,1)}, u32[]{:S(2)}, u32[]{:S(2)}) collective-permute-start(bf16[256,2048]{1,0:T(8,128)(2,1)} %get-tuple-element.159), channel_id=1, source_target_pairs={{0,16},{8,24},{16,0},{24,8},{1,17},{9,25},{17,1},{25,9},{2,18},{10... | collective-permute-start | bytes 3145736 | tf_op jit(solution)/shard_map/ppermute | solution.py:60
  251.3 96.8 %collective-permute-start.14 = (bf16[256,2048]{1,0:T(8,128)(2,1)}, bf16[256,2048]{1,0:T(8,128)(2,1)}, u32[]{:S(2)}, u32[]{:S(2)}) collective-permute-start(bf16[256,2048]{1,0:T(8,128)(2,1)} %collective-permute-done.12), channel_id=1, source_target_pairs={{0,8},{8,0},{16,24},{24,16},{1,9},{9,1},{17,25},{25,17},{2,10},{10... | collective-permute-start | bytes 3145736 | tf_op jit(solution)/shard_map/ppermute | solution.py:60
  278.6 69.4 %collective-permute-start.13 = (bf16[256,2048]{1,0:T(8,128)(2,1)}, bf16[256,2048]{1,0:T(8,128)(2,1)}, u32[]{:S(2)}, u32[]{:S(2)}) collective-permute-start(bf16[256,2048]{1,0:T(8,128)(2,1)} %collective-permute-done.9), channel_id=1, source_target_pairs={{0,16},{8,24},{16,0},{24,8},{1,17},{9,25},{17,1},{25,9},{2,18},{10... | collective-permute-start | bytes 3145736 | tf_op jit(solution)/shard_map/ppermute | solution.py:60
  386.6 268.1 %reduce-scatter.7.cloned.1.call-start = ((), (), s32[]{:S(2)}) async-start(), calls=%async_computation.9 | async-start | bytes 9437184 | tf_op jit(solution)/shard_map/reduce_scatter | solution.py:473
  475.0 287.2 %reduce-scatter.9.cloned.1.call-start = ((), (), s32[]{:S(2)}) async-start(), calls=%async_computation.10 | async-start | bytes 9437184 | tf_op jit(solution)/shard_map/reduce_scatter | solution.py:473
  483.9 55.4 %collective-permute-start.28 = (bf16[256,2048]{1,0:T(8,128)(2,1)S(1)}, bf16[256,2048]{1,0:T(8,128)(2,1)S(1)}, u32[]{:S(2)}, u32[]{:S(2)}) collective-permute-start(bf16[256,2048]{1,0:T(8,128)(2,1)S(1)} %get-tuple-element.153), channel_id=1, source_target_pairs={{0,8},{8,0},{16,24},{24,16},{1,9},{9,1},{17,25},{25,17},{2,10},{10... | collective-permute-start | bytes 3145736 | tf_op jit(solution)/shard_map/ppermute | solution.py:60
  495.1 82.7 %collective-permute-start.23 = (bf16[256,2048]{1,0:T(8,128)(2,1)}, bf16[256,2048]{1,0:T(8,128)(2,1)S(1)}, u32[]{:S(2)}, u32[]{:S(2)}) collective-permute-start(bf16[256,2048]{1,0:T(8,128)(2,1)} %slice.420), channel_id=1, source_target_pairs={{0,8},{8,0},{16,24},{24,16},{1,9},{9,1},{17,25},{25,17},{2,10},{10... | collective-permute-start | bytes 3145736 | tf_op jit(solution)/shard_map/ppermute | solution.py:60
  505.3 74.1 %collective-permute-start.32 = (bf16[256,2048]{1,0:T(8,128)(2,1)S(1)}, bf16[256,2048]{1,0:T(8,128)(2,1)S(1)}, u32[]{:S(2)}, u32[]{:S(2)}) collective-permute-start(bf16[256,2048]{1,0:T(8,128)(2,1)S(1)} %slice.426), channel_id=1, source_target_pairs={{0,16},{8,24},{16,0},{24,8},{1,17},{9,25},{17,1},{25,9},{2,18},{10... | collective-permute-start | bytes 3145736 | tf_op jit(solution)/shard_map/ppermute | solution.py:60
  506.8 47.1 %collective-permute-start.30 = (bf16[256,2048]{1,0:T(8,128)(2,1)S(1)}, bf16[256,2048]{1,0:T(8,128)(2,1)S(1)}, u32[]{:S(2)}, u32[]{:S(2)}) collective-permute-start(bf16[256,2048]{1,0:T(8,128)(2,1)S(1)} %get-tuple-element.154), channel_id=1, source_target_pairs={{0,16},{8,24},{16,0},{24,8},{1,17},{9,25},{17,1},{25,9},{2,18},{10... | collective-permute-start | bytes 3145736 | tf_op jit(solution)/shard_map/ppermute | solution.py:60
  553.9 44.9 %collective-permute-start.29 = (bf16[256,2048]{1,0:T(8,128)(2,1)S(1)}, bf16[256,2048]{1,0:T(8,128)(2,1)S(1)}, u32[]{:S(2)}, u32[]{:S(2)}) collective-permute-start(bf16[256,2048]{1,0:T(8,128)(2,1)S(1)} %add_convert_fusion.6), channel_id=1, source_target_pairs={{0,16},{8,24},{16,0},{24,8},{1,17},{9,25},{17,1},{25,9},{2,18},{10... | collective-permute-start | bytes 3145736 | tf_op jit(solution)/shard_map/ppermute | solution.py:60
  555.8 44.0 %collective-permute-start.31 = (bf16[256,2048]{1,0:T(8,128)(2,1)S(1)}, bf16[256,2048]{1,0:T(8,128)(2,1)S(1)}, u32[]{:S(2)}, u32[]{:S(2)}) collective-permute-start(bf16[256,2048]{1,0:T(8,128)(2,1)S(1)} %add_convert_fusion.5), channel_id=1, source_target_pairs={{0,8},{8,0},{16,24},{24,16},{1,9},{9,1},{17,25},{25,17},{2,10},{10... | collective-permute-start | bytes 3145736 | tf_op jit(solution)/shard_map/ppermute | solution.py:60
  577.8 43.5 %collective-permute-start.20 = (bf16[256,2048]{1,0:T(8,128)(2,1)S(1)}, bf16[256,2048]{1,0:T(8,128)(2,1)S(1)}, u32[]{:S(2)}, u32[]{:S(2)}) collective-permute-start(bf16[256,2048]{1,0:T(8,128)(2,1)S(1)} %slice.415), channel_id=1, source_target_pairs={{0,16},{8,24},{16,0},{24,8},{1,17},{9,25},{17,1},{25,9},{2,18},{10... | collective-permute-start | bytes 3145736 | tf_op jit(solution)/shard_map/ppermute | solution.py:60
  579.4 61.2 %collective-permute-start.17 = (bf16[256,2048]{1,0:T(8,128)(2,1)S(1)}, bf16[256,2048]{1,0:T(8,128)(2,1)S(1)}, u32[]{:S(2)}, u32[]{:S(2)}) collective-permute-start(bf16[256,2048]{1,0:T(8,128)(2,1)S(1)} %add_convert_fusion.8), channel_id=1, source_target_pairs={{0,16},{8,24},{16,0},{24,8},{1,17},{9,25},{17,1},{25,9},{2,18},{10... | collective-permute-start | bytes 3145736 | tf_op jit(solution)/shard_map/ppermute | solution.py:60
  654.8 323.5 %reduce-scatter.11.cloned.1.call-start = ((), (), s32[]{:S(2)}) async-start(), calls=%async_computation.11 | async-start | bytes 7077888 | tf_op jit(solution)/shard_map/reduce_scatter | solution.py:473
  815.4 53.2 %collective-permute-start.38 = (bf16[256,2048]{1,0:T(8,128)(2,1)S(1)}, bf16[256,2048]{1,0:T(8,128)(2,1)S(1)}, u32[]{:S(2)}, u32[]{:S(2)}) collective-permute-start(bf16[256,2048]{1,0:T(8,128)(2,1)S(1)} %add_convert_fusion.4), channel_id=1, source_target_pairs={{0,16},{8,24},{16,0},{24,8},{1,17},{9,25},{17,1},{25,9},{2,18},{10... | collective-permute-start | bytes 3145736 | tf_op jit(solution)/shard_map/ppermute | solution.py:60
  825.1 43.5 %collective-permute-start.40 = (bf16[256,2048]{1,0:T(8,128)(2,1)S(1)}, bf16[256,2048]{1,0:T(8,128)(2,1)S(1)}, u32[]{:S(2)}, u32[]{:S(2)}) collective-permute-start(bf16[256,2048]{1,0:T(8,128)(2,1)S(1)} %add_convert_fusion.3), channel_id=1, source_target_pairs={{0,8},{8,0},{16,24},{24,16},{1,9},{9,1},{17,25},{25,17},{2,10},{10... | collective-permute-start | bytes 3145736 | tf_op jit(solution)/shard_map/ppermute | solution.py:60
  (138 other events, 2437.2 us)
Sparse Core Ops, SparseCore 0:
  10.2 69.4 all-gather.4
  81.9 80.6 all-gather.6
  164.2 80.5 all-gather.8
  246.3 80.5 all-gather.10
  386.8 88.1 reduce-scatter.4
  477.1 87.9 reduce-scatter.6
  654.9 89.3 reduce-scatter.8
  762.3 72.5 reduce-scatter.10

commit v3 on v2

--- a/solution.py
+++ b/solution.py
@@ -61,42 +61,41 @@
 
 
 def gather_ctx(x):
-    n = x.shape[0] // 2
     count = lax.axis_size("ctx")
     if count != 4:
-        c = lax.axis_index("ctx")
-        whole = lax.all_gather(x, "ctx", axis=0)
-        parts = [lax.dynamic_index_in_dim(whole, c ^ j, 0, keepdims=False) for j in range(count)]
-        return [(p[:n], p[n:]) for p in parts]
-    lo, hi = x[:n], x[n:]
-    x_lo = swap(lo, 1)
-    y_hi = swap(hi, 2)
-    x_hi = swap(hi, 1)
-    y_lo = swap(lo, 2)
-    d_lo = swap(x_lo, 2)
-    d_hi = swap(y_hi, 1)
-    return [(lo, hi), (x_lo, x_hi), (y_lo, y_hi), (d_lo, d_hi)]
-
-
-def scatter_ctx(pieces):
-    if len(pieces) != 4:
-        c = lax.axis_index("ctx")
-        ordered = xor_order([p.astype(half) for p in pieces], c)
-        whole = jnp.concatenate(ordered, axis=0)
-        return lax.psum_scatter(whole, "ctx", scatter_dimension=0, tiled=True).astype(single)
-    p0, p1, p2, p3 = pieces
-    n = p0.shape[0] // 2
-    from_x = swap(p3[:n], 1)
-    from_y = swap(p3[n:], 2)
-    p2_lo = (p2[:n].astype(single) + from_x.astype(single)).astype(half)
-    p1_hi = (p1[n:].astype(single) + from_y.astype(single)).astype(half)
-    x_lo = swap(p1[:n], 1)
-    y_hi = swap(p2[n:], 2)
-    x_hi = swap(p1_hi, 1)
-    y_lo = swap(p2_lo, 2)
-    lo = p0[:n].astype(single) + x_lo.astype(single) + y_lo.astype(single)
-    hi = p0[n:].astype(single) + x_hi.astype(single) + y_hi.astype(single)
-    return jnp.concatenate([lo, hi], axis=0)
+        return [[x]] + [[swap(x, j)] for j in range(1, count)]
+    n = x.shape[0] // 2
+    one, two = swap(x, 1), swap(x, 2)
+    lo, hi = swap(one[:n], 2), swap(two[n:], 1)
+    return [[x], [one], [two], [lo, hi]]
+
+
+def scatter_first(far):
+    if lax.axis_size("ctx") != 4:
+        return None
+    n = far.shape[0] // 2
+    return swap(far[:n], 1), swap(far[n:], 2)
+
+
+def scatter_second(pieces, first):
+    if first is None:
+        return [swap(p, j) for j, p in enumerate(pieces) if j]
+    p1, p2 = pieces[1], pieces[2]
+    n = p1.shape[0] // 2
+    from_x, from_y = first
+    p1 = jnp.concatenate(
+        [p1[:n], (p1[n:].astype(single) + from_y.astype(single)).astype(half)], axis=0
+    )
+    p2 = jnp.concatenate(
+        [(p2[:n].astype(single) + from_x.astype(single)).astype(half), p2[n:]], axis=0
+    )
+    return [swap(p1, 1), swap(p2, 2)]
+
+
+def total_of(own, arrived):
+    for x in arrived:
+        own = own + x.astype(single)
+    return own
 
 
 def xor_order(items, c):
@@ -211,6 +210,83 @@
         ),
         name="attn_backward",
     )(inv, slopes, *([joined] * 24), *([grad] * 8))
+
+
+def up_kernel(a_ref, w_ref, b_ref, g_ref, s_ref):
+    u = dot_nn(a_ref[...], w_ref[...]) + b_ref[...]
+    value, slope = gelu_both(u)
+    g_ref[...] = value.astype(half)
+    s_ref[...] = slope.astype(half)
+
+
+def up_gelu(a, w, b):
+    m, k = a.shape
+    n = w.shape[1]
+    t = min(n, 512)
+    col = pl.BlockSpec((m, t), lambda i: (0, i))
+    shape = jax.ShapeDtypeStruct((m, n), half)
+    return pl.pallas_call(
+        up_kernel,
+        grid=(n // t,),
+        in_specs=[
+            pl.BlockSpec((m, k), lambda i: (0, 0)),
+            pl.BlockSpec((k, t), lambda i: (0, i)),
+            pl.BlockSpec((1, t), lambda i: (0, i)),
+        ],
+        out_specs=[col, col],
+        out_shape=[shape, shape],
+        compiler_params=pltpu.CompilerParams(vmem_limit_bytes=48 * 1024 * 1024),
+        cost_estimate=pl.CostEstimate(
+            flops=2 * m * n * k, bytes_accessed=2 * (m * k + n * k + 2 * m * n), transcendentals=m * n
+        ),
+        name="up_gelu",
+    )(a, w, b.reshape(1, n))
+
+
+def lay_out_kernel(axis, layout, c_ref, *refs):
+    out = refs[-1]
+    for (j, row), ref in zip(layout, refs):
+        x = ref[...].astype(single)
+        r, w = x.shape
+        if axis == 0:
+            n = sum(ref.shape[0] for (k, _), ref in zip(layout, refs) if k == j)
+            out[pl.ds(pl.multiple_of((c_ref[0] ^ j) * n + row, r), r), :] = x
+        else:
+            out[row : row + r, pl.ds(pl.multiple_of((c_ref[0] ^ j) * w, w), w)] = x
+
+
+def lay_out(axis, pieces, c, groups):
+    count = len(pieces)
+    r = sum(x.shape[0] for x in pieces[0])
+    n = pieces[0][0].shape[1]
+    w = n // groups
+    if w % 128:
+        whole = xor_order([jnp.concatenate(p, axis=0).astype(single) for p in pieces], c)
+        whole = jnp.stack([p.reshape(r, groups, w) for p in whole], axis=2)
+        return whole.reshape(r, count * n)
+    layout, blocks = [], []
+    for j, p in enumerate(pieces):
+        row = 0
+        for x in p:
+            layout.append((j, row))
+            blocks.append(x)
+            row += x.shape[0]
+    out = (count * r, w) if axis == 0 else (r, count * w)
+    return pl.pallas_call(
+        functools.partial(lay_out_kernel, axis, layout),
+        grid_spec=pltpu.PrefetchScalarGridSpec(
+            num_scalar_prefetch=1,
+            grid=(groups,),
+            in_specs=[pl.BlockSpec((x.shape[0], w), lambda k, c: (0, k)) for x in blocks],
+            out_specs=pl.BlockSpec(out, lambda k, c: (0, k)),
+        ),
+        out_shape=jax.ShapeDtypeStruct((out[0], out[1] * groups), single),
+        compiler_params=pltpu.CompilerParams(vmem_limit_bytes=48 * 1024 * 1024),
+        cost_estimate=pl.CostEstimate(
+            flops=0, bytes_accessed=6 * r * n * count, transcendentals=0
+        ),
+        name="lay_out",
+    )(c.reshape(1), *blocks)
 
 
 def gather_small_kernel(nf, x_ref, o_ref, send_sem, recv_sem):
@@ -415,102 +491,109 @@
         )
 
     def join(pieces):
-        return jnp.concatenate([h for p in pieces for h in p], axis=0)
+        return jnp.concatenate([x for p in pieces for x in p], axis=0)
+
+    def pieces_of(x):
+        return [x[j * rows : (j + 1) * rows] for j in range(CTX)]
+
+    def scatter_f(x):
+        return lax.psum_scatter(x, "fsdp", scatter_dimension=0, tiled=True)
 
     tok_all = join(gather_ctx(tokens))
-    w_down = gather_f(after(down_own.astype(half), tok_all))
+    dz2_own = after(cotangent, tok_all).astype(half)
+    dz2 = [jnp.concatenate(p, axis=0) for p in gather_ctx(dz2_own)]
+    w_up = gather_f(after(up_own.astype(half), tok_all))
     normed1, _ = norm_parts(tok_all.astype(single))
     a1 = (normed1 * gain1 + shift1).astype(half)
     joined = (dot_nn(a1, w_qkv) + bias_qkv).astype(half)
-    w_up = gather_f(after(up_own.astype(half), joined))
+    w_down = gather_f(after(down_own.astype(half), joined))
     attended = to_rows(attn_forward(joined, inv, slopes, heads, scale))
-
-    def pieces_of(x):
-        return [x[j * rows : (j + 1) * rows] for j in range(CTX)]
-
     mine = pieces_of(attended)
     mine = [mine[0]] + [swap(mine[j], j) for j in range(1, CTX)]
     ob = jnp.concatenate(xor_order(mine, c), axis=1)
     y1 = tokens.astype(single) + dot_nn(ob, w_out) + bias_o
 
     normed2, inv2 = norm_parts(y1)
-    a2_pieces = gather_ctx((normed2 * gain2 + shift2).astype(half))
-    dz2_own = cotangent.astype(half)
-    dz2_pieces = gather_ctx(dz2_own)
-    a2_pieces = [jnp.concatenate(p, axis=0) for p in a2_pieces]
-    dz2_pieces = [jnp.concatenate(p, axis=0) for p in dz2_pieces]
-    gb, du, dh2, mix = [], [], [None] * CTX, [None] * CTX
-    for j in range(CTX):
-        dgb = dot_nt(dz2_pieces[j], w_down).astype(half).astype(single)
-        value, slope = gelu_both(dot_nn(a2_pieces[j], w_up) + bias_u)
-        gb.append(value.astype(half))
-        du.append((dgb * slope).astype(half))
-    for j in reversed(range(CTX)):
-        dh2[j] = dot_nt(du[j], w_up)
-        if j:
-            dh2[j] = dh2[j].astype(half)
-    dh2_own = dh2[0]
-    dh2 = scatter_ctx(dh2)
-    gb_all = jnp.concatenate(after(gb, dh2_own), axis=0)
-    du = jnp.concatenate(du, axis=0)
-    a2 = jnp.concatenate(a2_pieces, axis=0)
-    dz2 = jnp.concatenate(dz2_pieces, axis=0)
-    down_grad = dot_tn(gb_all, dz2).astype(half)
-    up_grad = dot_tn(a2, du).astype(half)
-    up_bias_grad = jnp.sum(du.astype(single), axis=0)
+    a2 = gather_ctx((normed2 * gain2 + shift2).astype(half))
+    a2 = [jnp.concatenate(p, axis=0) for p in a2]
+    gb, slope = zip(*[up_gelu(p, w_up, bias_u) for p in a2])
+    dz2_all = jnp.concatenate(dz2, axis=0)
+    down_grad = dot_tn(jnp.concatenate(gb, axis=0), dz2_all).astype(half)
+    down_part = scatter_f(down_grad)
+    w_down = after(w_down, down_grad)
+
+    du, dh2, mix = [None] * CTX, [None] * CTX, [None] * CTX
+    far = CTX - 1
+
+    def hidden_grad(j, *others):
+        grad = dot_nt(after(dz2[j], *others), w_down).astype(half)
+        return (grad * slope[j].astype(single)).astype(half)
+
+    du[far] = hidden_grad(far)
+    dh2[far] = dot_nt(du[far], w_up).astype(half)
+    first = scatter_first(dh2[far])
+    last = dh2[far]
+    for j in reversed(range(1, far)):
+        du[j] = hidden_grad(j, last)
+        last = du[j]
+        if j == 1 and first is not None:
+            du[j] = after(du[j], first)
+        dh2[j] = last = dot_nt(du[j], w_up).astype(half)
+    arrived = scatter_second(dh2, first)
+    du[0] = hidden_grad(0, last)
+    dh2[0] = dot_nt(du[0], w_up)
+    up_grad = dot_tn(
+        jnp.concatenate(a2, axis=0), jnp.concatenate(after(du, dh2[0]), axis=0)
+    ).astype(half)
+    up_part = scatter_f(after(up_grad, down_part))
+    mix[far] = dot_nn(after(gb[far], up_grad), w_down).astype(half)
+    dh2 = total_of(after(dh2[0], mix[far]), arrived)
+    up_bias_grad = jnp.sum(jnp.concatenate(du, axis=0).astype(single), axis=0)
     down_bias_grad = jnp.sum(dz2_own.astype(single), axis=0)
-    gb = after(gb, dh2_own)
-    for j in reversed(range(CTX)):
-        mix[j] = dot_nn(gb[j], w_down)
-        if j:
-            mix[j] = mix[j].astype(half)
-    mixed = y1 + scatter_ctx(mix) + bias_d
     gain2_grad = jnp.sum(dh2 * normed2, axis=0)
     shift2_grad = jnp.sum(dh2, axis=0)
     dy1 = cotangent + norm_back(normed2, inv2, gain2, dh2)
 
-    def scatter_f(x):
-        return lax.psum_scatter(x, "fsdp", scatter_dimension=0, tiled=True)
-
-    down_part = scatter_f(down_grad)
     dz1 = dy1.astype(half)
+    dattn = dot_nt(after(dz1, down_part), w_out).astype(half)
+    dattn = xor_order([dattn[:, s * part : (s + 1) * part] for s in range(CTX)], c)
     out_bias_grad = jnp.sum(dz1.astype(single), axis=0)
-    out_grad = dot_tn(ob, dz1).astype(half)
-    up_part = scatter_f(after(up_grad, down_part))
-    dattn = dot_nt(dz1, w_out).astype(half)
-    dattn = xor_order([dattn[:, s * part : (s + 1) * part] for s in range(CTX)], c)
+    out_grad = dot_tn(ob, after(dz1, dattn)).astype(half)
+    for j in range(1, far):
+        mix[j] = dot_nn(after(gb[j], out_grad), w_down).astype(half)
     dattn = jnp.concatenate([dattn[0]] + [swap(dattn[j], j) for j in range(1, CTX)], axis=0)
-    dqkv = jnp.concatenate(attn_backward(joined, after(dattn, up_grad), inv, slopes, heads, scale), axis=1)
-    dqkv = to_rows(dqkv)
-    dh1 = [dot_nt(p, w_qkv) for p in pieces_of(dqkv)]
-    dh1_own = dh1[0]
-    dh1 = scatter_ctx(dh1[:1] + [p.astype(half) for p in dh1[1:]])
-    qkv_grad = dot_tn(a1, after(dqkv, dh1_own)).astype(half)
+    dqkv = attn_backward(joined, after(dattn, mix[1:far]), inv, slopes, heads, scale)
+    down_out = gather_ctx(after(down_part, dattn))
+    dqkv = to_rows(jnp.concatenate(dqkv, axis=1))
+    dqkv_at = pieces_of(dqkv)
+    dh1 = [None] * CTX
+    for j in reversed(range(1, CTX)):
+        dh1[j] = dot_nt(dqkv_at[j], w_qkv).astype(half)
+    first = scatter_first(dh1[far])
+    arrived = scatter_second(dh1, first)
+    dh1[0] = dot_nt(after(dqkv_at[0], up_part, dh1[1:]), w_qkv)
+    qkv_grad = dot_tn(a1, after(dqkv, dh1[0])).astype(half)
+    mix[0] = dot_nn(after(gb[0], qkv_grad), w_down)
+    dh1 = total_of(after(dh1[0], mix[0]), arrived)
+    out_part = scatter_f(after(out_grad, up_part))
+    qkv_part = scatter_f(after(qkv_grad, out_part, dh1))
+    mix = after(mix, dh1)
+    mixed = total_of(y1 + bias_d + mix[0], scatter_second(mix, scatter_first(mix[far])))
+    down_out = lay_out(0, down_out, c, width // min(width, 512))
+    up_out = lay_out(1, gather_ctx(after(up_part, dh1)), c, nf)
     sums = jnp.sum(dqkv.astype(single), axis=0)
     normed1_own, inv1_own = norm_parts(tokens.astype(single))
     gain1_grad = jnp.sum(dh1 * normed1_own, axis=0)
     shift1_grad = jnp.sum(dh1, axis=0)
     input_grad = dy1 + norm_back(normed1_own, inv1_own, gain1, dh1)
 
-    out_part = scatter_f(after(out_grad, up_part))
-    qkv_part = scatter_f(after(qkv_grad, out_part))
-
-    def everywhere(x):
-        pieces = [jnp.concatenate(p, axis=0) for p in gather_ctx(x)]
-        return xor_order([p.astype(single) for p in pieces], c)
-
-    down_out = jnp.concatenate(everywhere(down_part), axis=0)
-    up_out = everywhere(up_part)
-    up_out = jnp.stack([p.reshape(shard, nf, fpart) for p in up_out], axis=2).reshape(shard, wide)
     bit = 1
     while bit < CTX:
         out_part = out_part.astype(half)
         out_part = out_part.astype(single) + swap(out_part, bit).astype(single)
         bit *= 2
     out_out = out_part
-    qkv_out = everywhere(qkv_part)
-    qkv_out = jnp.stack([p.reshape(shard, 3, part) for p in qkv_out], axis=2)
-    qkv_out = qkv_out.reshape(shard, 3 * width)
+    qkv_out = lay_out(1, gather_ctx(qkv_part), c, 3)
 
     def spread(x, inner):
         x = x.reshape(-1, 1, inner)

time: 1080 us -> 1000 us (0.926)
  Pallas kernels: 92.6 us -> 222 us
  waiting for transfers between devices: 393 us -> 293 us
  local copies, waits for them, and re-layouts: 129 us -> 67 us
  matrix products: 281 us -> 242 us
  starting transfers between devices: 69.7 us -> 49.6 us
  other arithmetic: 79 us -> 94.2 us
    pallas_call x2, Pallas kernels: 23.9 us -> 99.1 us  [reduce_small(): pl.pallas_call(functools.partial(reduce_small_kernel, nf, nc), out_shape=...]
    ppermute x62 -> x44, waiting for transfers between devices: 353 us -> 293 us  [swap(): return lax.ppermute(x, 'ctx', [(i, i ^ mask) for i in range(n)])]
    pallas_call x0 -> x7, Pallas kernels: none -> 54.4 us  [the longest x4 42.6 us: up_gelu(): pl.pallas_call(up_kernel, grid=(n // t,), in_specs=[pl.BlockSpec((m, k),...]
    dot_general x10 -> x6, matrix products: 97.3 us -> 65.3 us  [dot_nn(): lax.dot_general(a, b, (((1,), (0,)), ((), ())), preferred_element_type=si...]
    unnamed x269 -> x260, local copies, waits for them, and re-layouts: 69.2 us -> 45.5 us
    all_gather x4, waiting for transfers between devices: 22.7 us -> 0.03 us  [gather_f(): return lax.all_gather(x, 'fsdp', axis=0, tiled=True)]
    ppermute x62 -> x44, starting transfers between devices: 68.9 us -> 49.1 us  [swap(): return lax.ppermute(x, 'ctx', [(i, i ^ mask) for i in range(n)])]
    reduce_scatter x4, waiting for transfers between devices: 16.6 us -> 0.03 us  [scatter_f(): return lax.psum_scatter(x, 'fsdp', scatter_dimension=0, tiled=True)]
  transfers between devices with their start and end apart: 70 -> 52, of which waited for: 40 -> 24; matrix products, arithmetic and copies ran while one was open for 38% -> 39% of each run, Pallas kernels for 9% -> 22%
where the time goes in v3:
time: 1000 us; the launch traced here: 994 us
  waiting for transfers between devices  293 us (29%)
  matrix products  242 us (24%)
  Pallas kernels  222 us (22%)
  other arithmetic  94.2 us (9%)
  local copies, waits for them, and re-layouts  67 us (7%)
  starting transfers between devices  49.6 us (5%)
  between operations  26.7 us (3%)
    ppermute x44, waiting for transfers between devices, swap(): return lax.ppermute(x, 'ctx', [(i, i ^ mask) for i in range(n)])  293 us
    dot_general x13, matrix products, dot_nt(): lax.dot_general(a, b, (((1,), (1,)), ((), ())), preferred_element_type=si...  106 us
    pallas_call x2, Pallas kernels, reduce_small(): pl.pallas_call(functools.partial(reduce_small_kernel, nf, nc), out_shape=...  99.1 us
    dot_general x4, matrix products, dot_tn(): lax.dot_general(a, b, (((0,), (0,)), ((), ())), preferred_element_type=si...  71 us
    dot_general x6, matrix products, dot_nn(): lax.dot_general(a, b, (((1,), (0,)), ((), ())), preferred_element_type=si...  65.3 us
    ppermute x44, starting transfers between devices, swap(): return lax.ppermute(x, 'ctx', [(i, i ^ mask) for i in range(n)])  49.1 us
    unnamed x260, local copies, waits for them, and re-layouts  45.5 us
    pallas_call x4, Pallas kernels, up_gelu(): pl.pallas_call(up_kernel, grid=(n // t,), in_specs=[pl.BlockSpec((m, k),...  42.6 us
  transfers between devices with their start and end apart: 52, of which 24 were waited for; matrix products, arithmetic and copies ran while one was open for 39% of the time, Pallas kernels for 22%

profile of v3, /device:TPU:0, one launch (start us, length us, event | category | flops | bytes accessed | tf_op | source)
XLA Modules:
  0.0 994.5 jit_solution(3997830357702438020)
XLA Ops:
  23.1 38.3 %collective-permute-done = bf16[512,2048]{1,0:T(8,128)(2,1)} collective-permute-done((bf16[512,2048]{1,0:T(8,128)(2,1)S(1)}, bf16[512,2048]{1,0:T(8,128)(2,1)}, u32[]{:S(2)}, u32[]{:S(2)}) %collective-permute-start) | collective-permute-done | bytes 2097184 | tf_op jit(solution)/shard_map/ppermute | solution.py:60
  78.6 9.7 collective-permute-done.2
  106.2 9.1 gather_small.1
  131.1 19.3 %add_convert_fusion.refs_0_.refs_1_.refs_2_.refs_3_.refs_4_.refs_5_.refs_6_.refs_7_.refs_8_.refs_9_.refs_10_.refs_11_.refs_12_.refs_13_.refs_14_.refs_15_.refs_16_.refs_17_.refs_18_.refs_19_.refs_20_.refs_21_.refs_22_.refs_23_ = bf16[2048,1536]{1,0:T(8,128)(2,1)} fusion(bf16[2048,1536]{1,0:T(8,128)(2,1)} %all-gather.5.cloned.1.call-done, ...), kind=kOutput, calls=%fused_computation.10 | convolution fusion | flops 12916359168 | bytes 21010432 | tf_op jit(solution)/shard_map/dot_general | solution.py:24
  150.6 23.6 %attn_forward.1 = bf16[2048,512]{1,0:T(8,128)(2,1)S(1)} custom-call(s32[16]{0:T(128)S(1)} %select_reduce_fusion.inv_ref, f32[4]{0:T(128)S(1)} %multiply_power_fusion.slope_ref, ...), custom_call_target="tpu_custom_call" | custom-call | flops 20000000000 | bytes 8388608 | tf_op jit(solution)/shard_map/attn_forward/pallas_call | solution.py:178
  191.5 11.7 %collective-permute-done.5 = bf16[512,512]{1,0:T(8,128)(2,1)S(1)} collective-permute-done((bf16[512,512]{1,0:T(8,128)(2,1)}, bf16[512,512]{1,0:T(8,128)(2,1)S(1)}, u32[]{:S(2)}, u32[]{:S(2)}) %collective-permute-start.5) | collective-permute-done | bytes 524320 | tf_op jit(solution)/shard_map/ppermute | solution.py:60
  220.0 27.4 %collective-permute-done.7 = bf16[512,2048]{1,0:T(8,128)(2,1)} collective-permute-done((bf16[512,2048]{1,0:T(8,128)(2,1)}, bf16[512,2048]{1,0:T(8,128)(2,1)}, u32[]{:S(2)}, u32[]{:S(2)}) %collective-permute-start.7) | collective-permute-done | bytes 2097184 | tf_op jit(solution)/shard_map/ppermute | solution.py:60
  255.3 37.7 %collective-permute-done.12.a_ref = bf16[512,2048]{1,0:T(8,128)(2,1)S(1)} collective-permute-done((bf16[512,2048]{1,0:T(8,128)(2,1)S(1)}, bf16[512,2048]{1,0:T(8,128)(2,1)S(1)}, u32[]{:S(2)}, u32[]{:S(2)}) %collective-permute-start.12) | collective-permute-done | bytes 2097184 | tf_op jit(solution)/shard_map/ppermute | solution.py:60
  299.1 16.4 %collective-permute-done.9 = bf16[256,2048]{1,0:T(8,128)(2,1)S(1)} collective-permute-done((bf16[256,2048]{1,0:T(8,128)(2,1)S(1)}, bf16[256,2048]{1,0:T(8,128)(2,1)S(1)}, u32[]{:S(2)}, u32[]{:S(2)}) %collective-permute-start.9) | collective-permute-done | bytes 1048608 | tf_op jit(solution)/shard_map/ppermute | solution.py:60
  315.7 21.5 %collective-permute-done.14 = bf16[256,2048]{1,0:T(8,128)(2,1)S(1)} collective-permute-done((bf16[256,2048]{1,0:T(8,128)(2,1)S(1)}, bf16[256,2048]{1,0:T(8,128)(2,1)S(1)}, u32[]{:S(2)}, u32[]{:S(2)}) %collective-permute-start.14) | collective-permute-done | bytes 1048608 | tf_op jit(solution)/shard_map/ppermute | solution.py:60
  340.6 9.9 up_gelu.5
  350.6 10.7 %up_gelu.6 = (bf16[512,2048]{1,0:T(8,128)(2,1)S(1)}, bf16[512,2048]{1,0:T(8,128)(2,1)S(1)}) custom-call(bf16[512,2048]{1,0:T(8,128)(2,1)} %copy-done.33, bf16[2048,2048]{1,0:T(8,128)(2,1)} %all-gather.9.cloned.1.call-done.w_ref, f32[1,2048]{1,0:T(1,128)S(1)} %bitcast.120), custom_call_target="tpu_custom_call" | custom-call | flops 4294967296 | bytes 14680064 | tf_op jit(solution)/shard_map/up_gelu/pallas_call | solution.py:228
  362.6 10.7 %up_gelu.4 = (bf16[512,2048]{1,0:T(8,128)(2,1)S(1)}, bf16[512,2048]{1,0:T(8,128)(2,1)S(1)}) custom-call(bf16[512,2048]{1,0:T(8,128)(2,1)} %copy-done.49, bf16[2048,2048]{1,0:T(8,128)(2,1)} %all-gather.9.cloned.1.call-done.w_ref, f32[1,2048]{1,0:T(1,128)S(1)} %bitcast.121), custom_call_target="tpu_custom_call" | custom-call | flops 4294967296 | bytes 14680064 | tf_op jit(solution)/shard_map/up_gelu/pallas_call | solution.py:228
  373.3 11.4 %up_gelu.7 = (bf16[512,2048]{1,0:T(8,128)(2,1)S(1)}, bf16[512,2048]{1,0:T(8,128)(2,1)S(1)}) custom-call(bf16[512,2048]{1,0:T(8,128)(2,1)} %pad_maximum_fusion.2.a_ref, bf16[2048,2048]{1,0:T(8,128)(2,1)} %all-gather.9.cloned.1.call-done.w_ref, f32[1,2048]{1,0:T(1,128)S(1)} %bitcast.122), custom_call_target="tpu_custom_call" | custom-call | flops 4294967296 | bytes 14680064 | tf_op jit(solution)/shard_map/up_gelu/pallas_call | solution.py:228
  387.4 22.0 %fusion.25 = bf16[2048,2048]{1,0:T(8,128)(2,1)} fusion(bf16[2048,2048]{1,0:T(8,128)(2,1)} %copy-done.55, bf16[512,2048]{1,0:T(8,128)(2,1)S(1)} %get-tuple-element.78, bf16[512,2048]{1,0:T(8,128)(2,1)S(1)} %get-tuple-element.83, bf16[512,2048]{1,0:T(8,128)(2,1)S(1)} %get-tuple-element.82, bf16[512,2048]{1,0:T(8,128)(2,1)S(1)} %get-tuple-element.91), kind=kOutput, calls=%fused_computation.28 | convolution fusion | flops 17217617920 | bytes 25165824 | tf_op jit(solution)/shard_map/dot_general | solution.py:32
  446.1 10.1 %convolution_convert_fusion.12 = bf16[512,2048]{1,0:T(8,128)(2,1)} fusion(bf16[512,2048]{1,0:T(8,128)(2,1)S(1)} %multiply_convert_fusion.2, bf16[2048,2048]{1,0:T(8,128)(2,1)} %all-gather.9.cloned.1.call-done.w_ref), kind=kOutput, calls=%fused_computation.73 | convolution fusion | flops 4296015872 | bytes 12582912 | tf_op jit(solution)/shard_map/dot_general | solution.py:28
  468.8 13.1 %collective-permute-done.16 = bf16[256,2048]{1,0:T(8,128)(2,1)S(1)} collective-permute-done((bf16[256,2048]{1,0:T(8,128)(2,1)S(1)}, bf16[256,2048]{1,0:T(8,128)(2,1)S(1)}, u32[]{:S(2)}, u32[]{:S(2)}) %collective-permute-start.16) | collective-permute-done | bytes 1048608 | tf_op jit(solution)/shard_map/ppermute | solution.py:60
  500.1 10.3 %fusion.88 = f32[512,2048]{1,0:T(8,128)} fusion(bf16[512,2048]{1,0:T(8,128)(2,1)S(1)} %multiply_convert_fusion, bf16[2048,2048]{1,0:T(8,128)(2,1)} %all-gather.9.cloned.1.call-done.w_ref), kind=kOutput, calls=%fused_computation.301 | convolution fusion | flops 4294967296 | bytes 14680064 | tf_op jit(solution)/shard_map/dot_general | solution.py:28
  510.3 22.6 %fusion.22 = bf16[2048,2048]{1,0:T(8,128)(2,1)} fusion(bf16[2048,2048]{1,0:T(8,128)(2,1)} %constant_dynamic-update-slice_fusion.11, bf16[512,2048]{1,0:T(8,128)(2,1)S(1)} %multiply_convert_fusion.3, bf16[512,2048]{1,0:T(8,128)(2,1)S(1)} %multiply_convert_fusion.2, bf16[512,2048]{1,0:T(8,128)(2,1)S(1)} %multiply_convert_fusion.1, ...), kind=kOutput, calls=%fused_computation.27 | convolution fusion | flops 17217617920 | bytes 25165824 | tf_op jit(solution)/shard_map/dot_general | solution.py:32
  539.3 10.1 %convolution_convert_fusion.8 = bf16[512,2048]{1,0:T(8,128)(2,1)} fusion(bf16[512,2048]{1,0:T(8,128)(2,1)S(1)} %copy-done.19, bf16[2048,2048]{1,0:T(8,128)(2,1)} %all-gather.11.cloned.1.call-done), kind=kOutput, calls=%fused_computation.69 | convolution fusion | flops 4296015872 | bytes 12582912 | tf_op jit(solution)/shard_map/dot_general | solution.py:24
  549.4 32.5 %collective-permute-done.17 = bf16[512,2048]{1,0:T(8,128)(2,1)S(1)} collective-permute-done((bf16[512,2048]{1,0:T(8,128)(2,1)S(1)}, bf16[512,2048]{1,0:T(8,128)(2,1)S(1)}, u32[]{:S(2)}, u32[]{:S(2)}) %collective-permute-start.17) | collective-permute-done | bytes 2097184 | tf_op jit(solution)/shard_map/ppermute | solution.py:60
  607.5 9.3 convolution_convert_fusion.5
  616.8 9.2 convolution_convert_fusion.6
  629.5 35.6 %attn_backward.1 = (bf16[2048,512]{1,0:T(8,128)(2,1)S(1)}, bf16[2048,512]{1,0:T(8,128)(2,1)S(1)}, bf16[2048,512]{1,0:T(8,128)(2,1)}) custom-call(s32[16]{0:T(128)S(1)} %copy-done.11, f32[4]{0:T(128)S(1)} %copy-done.9, ...), custom_call_target="tpu_custom_call" | custom-call | flops 40000000000 | bytes 14680064 | tf_op jit(solution)/shard_map/attn_backward/pallas_call | solution.py:197
  673.2 9.6 convolution_convert_fusion.2
  692.7 12.9 %collective-permute-done.24 = bf16[256,2048]{1,0:T(8,128)(2,1)S(1)} collective-permute-done((bf16[256,2048]{1,0:T(8,128)(2,1)S(1)}, bf16[256,2048]{1,0:T(8,128)(2,1)S(1)}, u32[]{:S(2)}, u32[]{:S(2)}) %collective-permute-start.24) | collective-permute-done | bytes 1048608 | tf_op jit(solution)/shard_map/ppermute | solution.py:60
  728.6 19.2 %convolution_convert_fusion.1 = bf16[2048,1536]{1,0:T(8,128)(2,1)} fusion(bf16[2048,1536]{1,0:T(8,128)(2,1)S(1)} %get-tuple-element.90, bf16[2048,2048]{1,0:T(8,128)(2,1)} %constant_dynamic-update-slice_fusion, f32[2048]{0:T(1024)S(1)} %bitcast.144, f32[2048]{0:T(1024)S(1)} %bitcast.132, f32[2048]{0:T(1024)S(1)} %copy-done.85, f32[2048]{0:T(1024)S(1)} %copy-done.75), kind=kOutput, calls=%fused_computation.30 | convolution fusion | flops 12913213440 | bytes 21004288 | tf_op jit(solution)/shard_map/dot_general | solution.py:32
  747.8 9.5 fusion.90
  775.0 21.0 %reduce_small.3 = f32[16,128]{1,0:T(8,128)} custom-call(f32[8,16,128]{2,1,0:T(8,128)} %bitcast.125), custom_call_target="tpu_custom_call" | custom-call | tf_op jit(solution)/shard_map/reduce_small/pallas_call | solution.py:393
  807.1 21.3 %collective-permute-done.43.refs_4_ = bf16[128,2048]{1,0:T(8,128)(2,1)S(1)} collective-permute-done((bf16[128,2048]{1,0:T(8,128)(2,1)S(1)}, bf16[128,2048]{1,0:T(8,128)(2,1)S(1)}, u32[]{:S(2)}, u32[]{:S(2)}) %collective-permute-start.43) | collective-permute-done | bytes 524320 | tf_op jit(solution)/shard_map/ppermute | solution.py:60
  841.0 78.2 %reduce_small.2 = f32[8,128]{1,0:T(8,128)} custom-call(f32[8,8,128]{2,1,0:T(8,128)} %pad_maximum_fusion.18.x_ref), custom_call_target="tpu_custom_call" | custom-call | tf_op jit(solution)/shard_map/reduce_small/pallas_call | solution.py:393
  956.7 18.4 %collective-permute-done.31.refs_2_ = bf16[256,1536]{1,0:T(8,128)(2,1)S(1)} collective-permute-done((bf16[256,1536]{1,0:T(8,128)(2,1)}, bf16[256,1536]{1,0:T(8,128)(2,1)S(1)}, u32[]{:S(2)}, u32[]{:S(2)}) %collective-permute-start.31) | collective-permute-done | bytes 786464 | tf_op jit(solution)/shard_map/ppermute | solution.py:60
  (495 shorter events, 345.7 us)
Async XLA Ops:
  7.2 123.8 %all-gather.5.cloned.1.call-start = ((), (), s32[]{:S(2)}) async-start(), calls=%async_computation.4 | async-start | bytes 7077888 | tf_op jit(solution)/shard_map/all_gather | solution.py:457
  9.8 198.4 %all-gather.7.cloned.1.call-start = ((), (), s32[]{:S(2)}) async-start(), calls=%async_computation.5 | async-start | bytes 9437184 | tf_op jit(solution)/shard_map/all_gather | solution.py:457
  12.6 328.0 %all-gather.9.cloned.1.call-start = ((), (), s32[]{:S(2)}) async-start(), calls=%async_computation.6 | async-start | bytes 9437184 | tf_op jit(solution)/shard_map/all_gather | solution.py:457
  12.7 48.7 %collective-permute-start = (bf16[512,2048]{1,0:T(8,128)(2,1)S(1)}, bf16[512,2048]{1,0:T(8,128)(2,1)}, u32[]{:S(2)}, u32[]{:S(2)}) collective-permute-start(bf16[512,2048]{1,0:T(8,128)(2,1)S(1)} %copy-done.24), channel_id=1, source_target_pairs={{0,8},{8,0},{16,24},{24,16},{1,9},{9,1},{17,25},{25,17},{2,10},{10... | collective-permute-start | bytes 6291464 | tf_op jit(solution)/shard_map/ppermute | solution.py:60
  15.7 51.8 %collective-permute-start.1 = (bf16[512,2048]{1,0:T(8,128)(2,1)S(1)}, bf16[512,2048]{1,0:T(8,128)(2,1)}, u32[]{:S(2)}, u32[]{:S(2)}) collective-permute-start(bf16[512,2048]{1,0:T(8,128)(2,1)S(1)} %copy-done.24), channel_id=1, source_target_pairs={{0,16},{8,24},{16,0},{24,8},{1,17},{9,25},{17,1},{25,9},{2,18},{10... | collective-permute-start | bytes 6291464 | tf_op jit(solution)/shard_map/ppermute | solution.py:60
  94.0 323.7 %all-gather.11.cloned.1.call-start = ((), (), s32[]{:S(2)}) async-start(), calls=%async_computation.7 | async-start | bytes 9437184 | tf_op jit(solution)/shard_map/all_gather | solution.py:457
  150.4 382.6 %reduce-scatter.5.cloned.1.call-start = ((), (), s32[]{:S(2)}) async-start(), calls=%async_computation.8 | async-start | bytes 9437184 | tf_op jit(solution)/shard_map/reduce_scatter | solution.py:500
  187.6 62.8 %collective-permute-start.8 = (bf16[512,2048]{1,0:T(8,128)(2,1)}, bf16[512,2048]{1,0:T(8,128)(2,1)}, u32[]{:S(2)}, u32[]{:S(2)}) collective-permute-start(bf16[512,2048]{1,0:T(8,128)(2,1)} %get-tuple-element.72), channel_id=1, source_target_pairs={{0,16},{8,24},{16,0},{24,8},{1,17},{9,25},{17,1},{25,9},{2,18},{10... | collective-permute-start | bytes 6291464 | tf_op jit(solution)/shard_map/ppermute | solution.py:60
  188.4 59.0 %collective-permute-start.7 = (bf16[512,2048]{1,0:T(8,128)(2,1)}, bf16[512,2048]{1,0:T(8,128)(2,1)}, u32[]{:S(2)}, u32[]{:S(2)}) collective-permute-start(bf16[512,2048]{1,0:T(8,128)(2,1)} %get-tuple-element.72), channel_id=1, source_target_pairs={{0,8},{8,0},{16,24},{24,16},{1,9},{9,1},{17,25},{25,17},{2,10},{10... | collective-permute-start | bytes 6291464 | tf_op jit(solution)/shard_map/ppermute | solution.py:60
  219.0 74.0 %collective-permute-start.12 = (bf16[512,2048]{1,0:T(8,128)(2,1)S(1)}, bf16[512,2048]{1,0:T(8,128)(2,1)S(1)}, u32[]{:S(2)}, u32[]{:S(2)}) collective-permute-start(bf16[512,2048]{1,0:T(8,128)(2,1)S(1)} %get-tuple-element.149.a_ref), channel_id=1, source_target_pairs={{0,16},{8,24},{16,0},{24,8},{1,17},{9,25},{17,1},{25,9},{2,18},{10... | collective-permute-start | bytes 6291464 | tf_op jit(solution)/shard_map/ppermute | solution.py:60
  219.8 74.8 %collective-permute-start.11 = (bf16[512,2048]{1,0:T(8,128)(2,1)S(1)}, bf16[512,2048]{1,0:T(8,128)(2,1)S(1)}, u32[]{:S(2)}, u32[]{:S(2)}) collective-permute-start(bf16[512,2048]{1,0:T(8,128)(2,1)S(1)} %get-tuple-element.149.a_ref), channel_id=1, source_target_pairs={{0,8},{8,0},{16,24},{24,16},{1,9},{9,1},{17,25},{25,17},{2,10},{10... | collective-permute-start | bytes 6291464 | tf_op jit(solution)/shard_map/ppermute | solution.py:60
  248.7 66.8 %collective-permute-start.9 = (bf16[256,2048]{1,0:T(8,128)(2,1)S(1)}, bf16[256,2048]{1,0:T(8,128)(2,1)S(1)}, u32[]{:S(2)}, u32[]{:S(2)}) collective-permute-start(bf16[256,2048]{1,0:T(8,128)(2,1)S(1)} %slice.377), channel_id=1, source_target_pairs={{0,16},{8,24},{16,0},{24,8},{1,17},{9,25},{17,1},{25,9},{2,18},{10... | collective-permute-start | bytes 3145736 | tf_op jit(solution)/shard_map/ppermute | solution.py:60
  251.7 63.9 %collective-permute-start.10 = (bf16[256,2048]{1,0:T(8,128)(2,1)S(1)}, bf16[256,2048]{1,0:T(8,128)(2,1)S(1)}, u32[]{:S(2)}, u32[]{:S(2)}) collective-permute-start(bf16[256,2048]{1,0:T(8,128)(2,1)S(1)} %slice.378), channel_id=1, source_target_pairs={{0,8},{8,0},{16,24},{24,16},{1,9},{9,1},{17,25},{25,17},{2,10},{10... | collective-permute-start | bytes 3145736 | tf_op jit(solution)/shard_map/ppermute | solution.py:60
  293.1 44.1 %collective-permute-start.14 = (bf16[256,2048]{1,0:T(8,128)(2,1)S(1)}, bf16[256,2048]{1,0:T(8,128)(2,1)S(1)}, u32[]{:S(2)}, u32[]{:S(2)}) collective-permute-start(bf16[256,2048]{1,0:T(8,128)(2,1)S(1)} %slice.380), channel_id=1, source_target_pairs={{0,8},{8,0},{16,24},{24,16},{1,9},{9,1},{17,25},{25,17},{2,10},{10... | collective-permute-start | bytes 3145736 | tf_op jit(solution)/shard_map/ppermute | solution.py:60
  294.7 43.2 %collective-permute-start.13 = (bf16[256,2048]{1,0:T(8,128)(2,1)S(1)}, bf16[256,2048]{1,0:T(8,128)(2,1)S(1)}, u32[]{:S(2)}, u32[]{:S(2)}) collective-permute-start(bf16[256,2048]{1,0:T(8,128)(2,1)S(1)} %slice.379), channel_id=1, source_target_pairs={{0,16},{8,24},{16,0},{24,8},{1,17},{9,25},{17,1},{25,9},{2,18},{10... | collective-permute-start | bytes 3145736 | tf_op jit(solution)/shard_map/ppermute | solution.py:60
  409.4 219.4 %reduce-scatter.7.cloned.1.call-start = ((), (), s32[]{:S(2)}) async-start(), calls=%async_computation.9 | async-start | bytes 9437184 | tf_op jit(solution)/shard_map/reduce_scatter | solution.py:500
  533.0 232.8 %reduce-scatter.9.cloned.1.call-start = ((), (), s32[]{:S(2)}) async-start(), calls=%async_computation.10 | async-start | bytes 9437184 | tf_op jit(solution)/shard_map/reduce_scatter | solution.py:500
  534.8 47.1 %collective-permute-start.17 = (bf16[512,2048]{1,0:T(8,128)(2,1)S(1)}, bf16[512,2048]{1,0:T(8,128)(2,1)S(1)}, u32[]{:S(2)}, u32[]{:S(2)}) collective-permute-start(bf16[512,2048]{1,0:T(8,128)(2,1)S(1)} %pad_maximum_fusion.3), channel_id=1, source_target_pairs={{0,8},{8,0},{16,24},{24,16},{1,9},{9,1},{17,25},{25,17},{2,10},{10... | collective-permute-start | bytes 6291464 | tf_op jit(solution)/shard_map/ppermute | solution.py:60
  536.8 46.7 %collective-permute-start.18 = (bf16[512,2048]{1,0:T(8,128)(2,1)S(1)}, bf16[512,2048]{1,0:T(8,128)(2,1)S(1)}, u32[]{:S(2)}, u32[]{:S(2)}) collective-permute-start(bf16[512,2048]{1,0:T(8,128)(2,1)S(1)} %pad_maximum_fusion.4), channel_id=1, source_target_pairs={{0,16},{8,24},{16,0},{24,8},{1,17},{9,25},{17,1},{25,9},{2,18},{10... | collective-permute-start | bytes 6291464 | tf_op jit(solution)/shard_map/ppermute | solution.py:60
  628.9 317.3 %reduce-scatter.11.cloned.1.call-start = ((), (), s32[]{:S(2)}) async-start(), calls=%async_computation.11 | async-start | bytes 7077888 | tf_op jit(solution)/shard_map/reduce_scatter | solution.py:500
  707.6 51.4 %collective-permute-start.25 = (bf16[512,2048]{1,0:T(8,128)(2,1)}, bf16[512,2048]{1,0:T(8,128)(2,1)}, u32[]{:S(2)}, u32[]{:S(2)}) collective-permute-start(bf16[512,2048]{1,0:T(8,128)(2,1)} %pad_maximum_fusion.7), channel_id=1, source_target_pairs={{0,16},{8,24},{16,0},{24,8},{1,17},{9,25},{17,1},{25,9},{2,18},{10... | collective-permute-start | bytes 6291464 | tf_op jit(solution)/shard_map/ppermute | solution.py:60
  719.5 40.8 %collective-permute-start.23 = (bf16[512,2048]{1,0:T(8,128)(2,1)}, bf16[512,2048]{1,0:T(8,128)(2,1)}, u32[]{:S(2)}, u32[]{:S(2)}) collective-permute-start(bf16[512,2048]{1,0:T(8,128)(2,1)} %pad_maximum_fusion.6), channel_id=1, source_target_pairs={{0,8},{8,0},{16,24},{24,16},{1,9},{9,1},{17,25},{25,17},{2,10},{10... | collective-permute-start | bytes 6291464 | tf_op jit(solution)/shard_map/ppermute | solution.py:60
  797.8 35.0 %collective-permute-start.28 = (bf16[256,2048]{1,0:T(8,128)(2,1)S(1)}, bf16[256,2048]{1,0:T(8,128)(2,1)S(1)}, u32[]{:S(2)}, u32[]{:S(2)}) collective-permute-start(bf16[256,2048]{1,0:T(8,128)(2,1)S(1)} %get-tuple-element.154), channel_id=1, source_target_pairs={{0,8},{8,0},{16,24},{24,16},{1,9},{9,1},{17,25},{25,17},{2,10},{10... | collective-permute-start | bytes 3145736 | tf_op jit(solution)/shard_map/ppermute | solution.py:60
  799.1 29.3 %collective-permute-start.43 = (bf16[128,2048]{1,0:T(8,128)(2,1)S(1)}, bf16[128,2048]{1,0:T(8,128)(2,1)S(1)}, u32[]{:S(2)}, u32[]{:S(2)}) collective-permute-start(bf16[128,2048]{1,0:T(8,128)(2,1)S(1)} %slice.404), channel_id=1, source_target_pairs={{0,8},{8,0},{16,24},{24,16},{1,9},{9,1},{17,25},{25,17},{2,10},{10... | collective-permute-start | bytes 1572872 | tf_op jit(solution)/shard_map/ppermute | solution.py:60
  802.6 33.7 %collective-permute-start.26 = (bf16[256,2048]{1,0:T(8,128)(2,1)S(1)}, bf16[256,2048]{1,0:T(8,128)(2,1)S(1)}, u32[]{:S(2)}, u32[]{:S(2)}) collective-permute-start(bf16[256,2048]{1,0:T(8,128)(2,1)S(1)} %get-tuple-element.153), channel_id=1, source_target_pairs={{0,16},{8,24},{16,0},{24,8},{1,17},{9,25},{17,1},{25,9},{2,18},{10... | collective-permute-start | bytes 3145736 | tf_op jit(solution)/shard_map/ppermute | solution.py:60
  832.3 93.1 %collective-permute-start.37 = (bf16[256,2048]{1,0:T(8,128)(2,1)S(1)}, bf16[256,2048]{1,0:T(8,128)(2,1)S(1)}, u32[]{:S(2)}, u32[]{:S(2)}) collective-permute-start(bf16[256,2048]{1,0:T(8,128)(2,1)S(1)} %copy-done.4), channel_id=1, source_target_pairs={{0,16},{8,24},{16,0},{24,8},{1,17},{9,25},{17,1},{25,9},{2,18},{10... | collective-permute-start | bytes 3145736 | tf_op jit(solution)/shard_map/ppermute | solution.py:60
  832.3 94.0 %collective-permute-start.36 = (bf16[256,2048]{1,0:T(8,128)(2,1)S(1)}, bf16[256,2048]{1,0:T(8,128)(2,1)S(1)}, u32[]{:S(2)}, u32[]{:S(2)}) collective-permute-start(bf16[256,2048]{1,0:T(8,128)(2,1)S(1)} %copy-done.4), channel_id=1, source_target_pairs={{0,8},{8,0},{16,24},{24,16},{1,9},{9,1},{17,25},{25,17},{2,10},{10... | collective-permute-start | bytes 3145736 | tf_op jit(solution)/shard_map/ppermute | solution.py:60
  835.9 112.5 %collective-permute-start.29 = (bf16[512,2048]{1,0:T(8,128)(2,1)}, bf16[512,2048]{1,0:T(8,128)(2,1)}, u32[]{:S(2)}, u32[]{:S(2)}) collective-permute-start(bf16[512,2048]{1,0:T(8,128)(2,1)} %pad_maximum_fusion.9), channel_id=1, source_target_pairs={{0,16},{8,24},{16,0},{24,8},{1,17},{9,25},{17,1},{25,9},{2,18},{10... | collective-permute-start | bytes 6291464 | tf_op jit(solution)/shard_map/ppermute | solution.py:60
  838.3 110.1 %collective-permute-start.27 = (bf16[512,2048]{1,0:T(8,128)(2,1)}, bf16[512,2048]{1,0:T(8,128)(2,1)}, u32[]{:S(2)}, u32[]{:S(2)}) collective-permute-start(bf16[512,2048]{1,0:T(8,128)(2,1)} %pad_maximum_fusion.8), channel_id=1, source_target_pairs={{0,8},{8,0},{16,24},{24,16},{1,9},{9,1},{17,25},{25,17},{2,10},{10... | collective-permute-start | bytes 6291464 | tf_op jit(solution)/shard_map/ppermute | solution.py:60
  840.3 86.7 %collective-permute-start.34 = (bf16[256,2048]{1,0:T(8,128)(2,1)}, bf16[256,2048]{1,0:T(8,128)(2,1)}, u32[]{:S(2)}, u32[]{:S(2)}) collective-permute-start(bf16[256,2048]{1,0:T(8,128)(2,1)} %reduce-scatter.9.cloned.1.call-done), channel_id=1, source_target_pairs={{0,8},{8,0},{16,24},{24,16},{1,9},{9,1},{17,25},{25,17},{2,10},{10... | collective-permute-start | bytes 3145736 | tf_op jit(solution)/shard_map/ppermute | solution.py:60
  930.0 47.5 %collective-permute-start.35 = (bf16[256,2048]{1,0:T(8,128)(2,1)}, bf16[256,2048]{1,0:T(8,128)(2,1)}, u32[]{:S(2)}, u32[]{:S(2)}) collective-permute-start(bf16[256,2048]{1,0:T(8,128)(2,1)} %add_convert_fusion.2), channel_id=1, source_target_pairs={{0,16},{8,24},{16,0},{24,8},{1,17},{9,25},{17,1},{25,9},{2,18},{10... | collective-permute-start | bytes 3145736 | tf_op jit(solution)/shard_map/ppermute | solution.py:60
  946.8 29.7 %collective-permute-start.30 = (bf16[256,1536]{1,0:T(8,128)(2,1)}, bf16[256,1536]{1,0:T(8,128)(2,1)S(1)}, u32[]{:S(2)}, u32[]{:S(2)}) collective-permute-start(bf16[256,1536]{1,0:T(8,128)(2,1)} %reduce-scatter.11.cloned.1.call-done.refs_0_), channel_id=1, source_target_pairs={{0,8},{8,0},{16,24},{24,16},{1,9},{9,1},{17,25},{25,17},{2,10},{10... | collective-permute-start | bytes 2359304 | tf_op jit(solution)/shard_map/ppermute | solution.py:60
  (124 other events, 1982.1 us)
Sparse Core Ops, SparseCore 0:
  10.2 67.4 all-gather.4
  79.9 82.8 all-gather.6
  164.9 80.4 all-gather.8
  246.9 80.5 all-gather.10
  409.5 92.3 reduce-scatter.4
  533.1 90.5 reduce-scatter.6
  629.0 89.5 reduce-scatter.8
  765.9 69.4 reduce-scatter.10

commit v4 on v3

--- a/solution.py
+++ b/solution.py
@@ -60,26 +60,32 @@
     return lax.ppermute(x, "ctx", [(i, i ^ mask) for i in range(n)])
 
 
+def gather_first(x):
+    count = lax.axis_size("ctx")
+    return [swap(x, j) for j in range(1, 3 if count == 4 else count)]
+
+
+def gather_second(x, arrived):
+    if lax.axis_size("ctx") != 4:
+        return [[x]] + [[p] for p in arrived]
+    one, two = arrived
+    n = x.shape[0] // 2
+    return [[x], [one], [two], [swap(one[:n], 2), swap(two[n:], 1)]]
+
+
 def gather_ctx(x):
-    count = lax.axis_size("ctx")
-    if count != 4:
-        return [[x]] + [[swap(x, j)] for j in range(1, count)]
-    n = x.shape[0] // 2
-    one, two = swap(x, 1), swap(x, 2)
-    lo, hi = swap(one[:n], 2), swap(two[n:], 1)
-    return [[x], [one], [two], [lo, hi]]
+    return gather_second(x, gather_first(x))
 
 
 def scatter_first(far):
     if lax.axis_size("ctx") != 4:
         return None
-    n = far.shape[0] // 2
-    return swap(far[:n], 1), swap(far[n:], 2)
+    return swap(far[0], 1), swap(far[1], 2)
 
 
 def scatter_second(pieces, first):
     if first is None:
-        return [swap(p, j) for j, p in enumerate(pieces) if j]
+        return pieces[1:]
     p1, p2 = pieces[1], pieces[2]
     n = p1.shape[0] // 2
     from_x, from_y = first
@@ -89,7 +95,11 @@
     p2 = jnp.concatenate(
         [(p2[:n].astype(single) + from_x.astype(single)).astype(half), p2[n:]], axis=0
     )
-    return [swap(p1, 1), swap(p2, 2)]
+    return [p1, p2]
+
+
+def scatter_send(sent):
+    return [swap(x, j + 1) for j, x in enumerate(sent)]
 
 
 def total_of(own, arrived):
@@ -182,9 +192,7 @@
         ),
         out_shape=jax.ShapeDtypeStruct((rows, heads * 128), half),
         compiler_params=pltpu.CompilerParams(vmem_limit_bytes=48 * 1024 * 1024),
-        cost_estimate=pl.CostEstimate(
-            flops=20 * 10**9, bytes_accessed=rows * heads * 128 * 8, transcendentals=0
-        ),
+        cost_estimate=hint(20 * 10**9, rows * heads * 128 * 8),
         name="attn_forward",
     )(inv, slopes, *([joined] * 24))
 
@@ -205,42 +213,126 @@
         ),
         out_shape=[shape] * 3,
         compiler_params=pltpu.CompilerParams(vmem_limit_bytes=48 * 1024 * 1024),
-        cost_estimate=pl.CostEstimate(
-            flops=40 * 10**9, bytes_accessed=rows * heads * 128 * 14, transcendentals=0
-        ),
+        cost_estimate=hint(40 * 10**9, rows * heads * 128 * 14),
         name="attn_backward",
     )(inv, slopes, *([joined] * 24), *([grad] * 8))
 
 
-def up_kernel(a_ref, w_ref, b_ref, g_ref, s_ref):
-    u = dot_nn(a_ref[...], w_ref[...]) + b_ref[...]
-    value, slope = gelu_both(u)
-    g_ref[...] = value.astype(half)
-    s_ref[...] = slope.astype(half)
-
-
-def up_gelu(a, w, b):
-    m, k = a.shape
-    n = w.shape[1]
-    t = min(n, 512)
-    col = pl.BlockSpec((m, t), lambda i: (0, i))
-    shape = jax.ShapeDtypeStruct((m, n), half)
+HINT = 0.1
+
+
+def block_of(x):
+    return x if isinstance(x, tuple) else (x, x.shape[0], 0)
+
+
+def hint(flops, bytes_accessed):
+    return pl.CostEstimate(
+        flops=int(HINT * flops), bytes_accessed=int(HINT * bytes_accessed), transcendentals=0
+    )
+
+
+def rows_kernel(dot, epilogue, count, extra, *refs):
+    left, w_ref = refs[:count], refs[count]
+    extras = refs[count + 1 : count + 1 + extra]
+    outs = refs[count + 1 + extra :]
+    for i in range(count):
+        epilogue(i, dot(left[i][...], w_ref[...]), extras, outs)
+
+
+def rows_matmul(blocks, w, transposed, extras, outs, epilogue, name, tile=512):
+    blocks = [block_of(x) for x in blocks]
+    extras = [block_of(x) for x in extras]
+    n = w.shape[0] if transposed else w.shape[1]
+    k = w.shape[1] if transposed else w.shape[0]
+    t = math.gcd(n, tile)
+    w_spec = (
+        pl.BlockSpec((t, k), lambda i: (i, 0)) if transposed else pl.BlockSpec((k, t), lambda i: (0, i))
+    )
+    rows = sum(x[1] for x in blocks)
     return pl.pallas_call(
-        up_kernel,
+        functools.partial(
+            rows_kernel, dot_nt if transposed else dot_nn, epilogue, len(blocks), len(extras)
+        ),
         grid=(n // t,),
-        in_specs=[
-            pl.BlockSpec((m, k), lambda i: (0, 0)),
-            pl.BlockSpec((k, t), lambda i: (0, i)),
-            pl.BlockSpec((1, t), lambda i: (0, i)),
-        ],
-        out_specs=[col, col],
-        out_shape=[shape, shape],
-        compiler_params=pltpu.CompilerParams(vmem_limit_bytes=48 * 1024 * 1024),
-        cost_estimate=pl.CostEstimate(
-            flops=2 * m * n * k, bytes_accessed=2 * (m * k + n * k + 2 * m * n), transcendentals=m * n
-        ),
-        name="up_gelu",
-    )(a, w, b.reshape(1, n))
+        in_specs=[pl.BlockSpec((x[1], k), lambda i, at=x[2]: (at, 0)) for x in blocks]
+        + [w_spec]
+        + [pl.BlockSpec((x[1], t), lambda i, at=x[2]: (at, i)) for x in extras],
+        out_specs=[pl.BlockSpec((r, t), lambda i: (0, i)) for r, _ in outs],
+        out_shape=[jax.ShapeDtypeStruct((r, n), d) for r, d in outs],
+        compiler_params=pltpu.CompilerParams(vmem_limit_bytes=52 * 1024 * 1024),
+        cost_estimate=hint(2 * rows * n * k, 2 * n * k + 4 * rows * (n + k)),
+        name=name,
+    )(*[x[0] for x in blocks], w, *[x[0] for x in extras])
+
+
+def plain(blocks, w, transposed, dtype, name):
+    def epilogue(i, x, extras, outs):
+        outs[i][...] = x.astype(dtype)
+
+    outs = [(block_of(x)[1], dtype) for x in blocks]
+    return rows_matmul(blocks, w, transposed, [], outs, epilogue, name)
+
+
+def joined_rows(blocks, w, bias, name):
+    sizes = [block_of(x)[1] for x in blocks]
+
+    def epilogue(i, x, extras, outs):
+        at = sum(sizes[:i])
+        outs[0][at : at + sizes[i], :] = (x + extras[0][...]).astype(half)
+
+    bias = bias.reshape(1, -1)
+    return rows_matmul(blocks, w, False, [bias], [(sum(sizes), half)], epilogue, name)[0]
+
+
+def up_gelu(blocks, w, bias, name):
+    count = len(blocks)
+
+    def epilogue(i, x, extras, outs):
+        value, slope = gelu_both(x + extras[0][...])
+        outs[i][...] = value.astype(half)
+        outs[count + i][...] = slope.astype(half)
+
+    outs = [(block_of(x)[1], half) for x in blocks] * 2
+    out = rows_matmul(blocks, w, False, [bias.reshape(1, -1)], outs, epilogue, name)
+    return out[:count], out[count:]
+
+
+def hidden_back(blocks, w, slopes, name):
+    def epilogue(i, x, extras, outs):
+        x = x.astype(half).astype(single) * extras[i][...].astype(single)
+        outs[i][...] = x.astype(half)
+
+    outs = [(block_of(x)[1], half) for x in blocks]
+    return rows_matmul(blocks, w, True, slopes, outs, epilogue, name)
+
+
+def outer_kernel(count, *refs):
+    out = refs[-1]
+    total = None
+    for i in range(count):
+        x = dot_tn(refs[i][...], refs[count + i][...])
+        total = x if total is None else total + x
+    out[...] = total.astype(half)
+
+
+def outer(left, right, name):
+    left = [block_of(x) for x in left]
+    right = [block_of(x) for x in right]
+    m, n = left[0][0].shape[1], right[0][0].shape[1]
+    tm = math.gcd(m, 1024)
+    tn = n // 2 if n % 256 == 0 and n > 1024 else n
+    rows = sum(x[1] for x in left)
+    return pl.pallas_call(
+        functools.partial(outer_kernel, len(left)),
+        grid=(m // tm, n // tn),
+        in_specs=[pl.BlockSpec((x[1], tm), lambda i, j, at=x[2]: (at, i)) for x in left]
+        + [pl.BlockSpec((x[1], tn), lambda i, j, at=x[2]: (at, j)) for x in right],
+        out_specs=pl.BlockSpec((tm, tn), lambda i, j: (i, j)),
+        out_shape=jax.ShapeDtypeStruct((m, n), half),
+        compiler_params=pltpu.CompilerParams(vmem_limit_bytes=52 * 1024 * 1024),
+        cost_estimate=hint(2 * rows * m * n, 2 * rows * (m + n) + 2 * m * n),
+        name=name,
+    )(*[x[0] for x in left], *[x[0] for x in right])
 
 
 def lay_out_kernel(axis, layout, c_ref, *refs):
@@ -282,9 +374,7 @@
         ),
         out_shape=jax.ShapeDtypeStruct((out[0], out[1] * groups), single),
         compiler_params=pltpu.CompilerParams(vmem_limit_bytes=48 * 1024 * 1024),
-        cost_estimate=pl.CostEstimate(
-            flops=0, bytes_accessed=6 * r * n * count, transcendentals=0
-        ),
+        cost_estimate=hint(0, 6 * r * n * count),
         name="lay_out",
     )(c.reshape(1), *blocks)
 
@@ -490,65 +580,69 @@
             [lax.dynamic_slice_in_dim(x, place[r] * SPAN, SPAN, axis=0) for r in range(CTX * per)]
         )
 
-    def join(pieces):
-        return jnp.concatenate([x for p in pieces for x in p], axis=0)
-
-    def pieces_of(x):
-        return [x[j * rows : (j + 1) * rows] for j in range(CTX)]
+    def flat(pieces):
+        return [x for p in pieces for x in p]
 
     def scatter_f(x):
         return lax.psum_scatter(x, "fsdp", scatter_dimension=0, tiled=True)
 
-    tok_all = join(gather_ctx(tokens))
-    dz2_own = after(cotangent, tok_all).astype(half)
-    dz2 = [jnp.concatenate(p, axis=0) for p in gather_ctx(dz2_own)]
-    w_up = gather_f(after(up_own.astype(half), tok_all))
-    normed1, _ = norm_parts(tok_all.astype(single))
-    a1 = (normed1 * gain1 + shift1).astype(half)
-    joined = (dot_nn(a1, w_qkv) + bias_qkv).astype(half)
+    far = CTX - 1
+    mid = list(range(1, far))
+
+    tok_near = gather_first(tokens)
+    tok = flat(gather_second(tokens, after(tok_near, small_all)))
+    dz2_own = after(cotangent, tok).astype(half)
+    dz2_near = gather_first(dz2_own)
+    w_up = gather_f(after(up_own.astype(half), tok))
+    a1 = []
+    for x in tok:
+        normed, _ = norm_parts(x.astype(single))
+        a1.append((normed * gain1 + shift1).astype(half))
+    joined = joined_rows(a1, w_qkv, bias_qkv, "qkv")
     w_down = gather_f(after(down_own.astype(half), joined))
     attended = to_rows(attn_forward(joined, inv, slopes, heads, scale))
-    mine = pieces_of(attended)
+    mine = [attended[j * rows : (j + 1) * rows] for j in range(CTX)]
+    mine = after(mine, dz2_near)
     mine = [mine[0]] + [swap(mine[j], j) for j in range(1, CTX)]
     ob = jnp.concatenate(xor_order(mine, c), axis=1)
     y1 = tokens.astype(single) + dot_nn(ob, w_out) + bias_o
 
     normed2, inv2 = norm_parts(y1)
     a2 = gather_ctx((normed2 * gain2 + shift2).astype(half))
-    a2 = [jnp.concatenate(p, axis=0) for p in a2]
-    gb, slope = zip(*[up_gelu(p, w_up, bias_u) for p in a2])
-    dz2_all = jnp.concatenate(dz2, axis=0)
-    down_grad = dot_tn(jnp.concatenate(gb, axis=0), dz2_all).astype(half)
+    gb, slope = [None] * CTX, [None] * CTX
+    last = ()
+    for j in range(CTX):
+        if j == far:
+            dz2 = gather_second(dz2_own, after(dz2_near, a2[far], last))
+        gb[j], slope[j] = up_gelu(after(a2[j], last), w_up, bias_u, f"up_gelu_{j}")
+        last = gb[j]
+    down_grad = outer(flat(gb), flat(dz2), "down_grad")
     down_part = scatter_f(down_grad)
     w_down = after(w_down, down_grad)
 
     du, dh2, mix = [None] * CTX, [None] * CTX, [None] * CTX
-    far = CTX - 1
-
-    def hidden_grad(j, *others):
-        grad = dot_nt(after(dz2[j], *others), w_down).astype(half)
-        return (grad * slope[j].astype(single)).astype(half)
-
-    du[far] = hidden_grad(far)
-    dh2[far] = dot_nt(du[far], w_up).astype(half)
+    du[far] = hidden_back(dz2[far], w_down, slope[far], "du_far")
+    dh2[far] = plain(du[far], w_up, True, half, "dh2_far")
     first = scatter_first(dh2[far])
-    last = dh2[far]
-    for j in reversed(range(1, far)):
-        du[j] = hidden_grad(j, last)
-        last = du[j]
-        if j == 1 and first is not None:
-            du[j] = after(du[j], first)
-        dh2[j] = last = dot_nt(du[j], w_up).astype(half)
-    arrived = scatter_second(dh2, first)
-    du[0] = hidden_grad(0, last)
-    dh2[0] = dot_nt(du[0], w_up)
-    up_grad = dot_tn(
-        jnp.concatenate(a2, axis=0), jnp.concatenate(after(du, dh2[0]), axis=0)
-    ).astype(half)
+    mids = hidden_back(
+        after([dz2[j][0] for j in mid], dh2[far]), w_down, [slope[j][0] for j in mid], "du_mid"
+    )
+    for j, x in zip(mid, mids):
+        du[j] = [x]
+    mids = plain(mids, w_up, True, half, "dh2_mid")
+    for j, x in zip(mid, mids):
+        dh2[j] = x
+    if first is None:
+        dh2[far] = dh2[far][0]
+    sent = scatter_second(dh2, first)
+    arrived = scatter_send(sent)
+    du[0] = hidden_back(after(dz2[0], sent), w_down, slope[0], "du_own")
+    dh2[0] = plain(du[0], w_up, True, single, "dh2_own")[0]
+    up_grad = outer(flat(a2), after(flat(du), dh2[0]), "up_grad")
     up_part = scatter_f(after(up_grad, down_part))
-    mix[far] = dot_nn(after(gb[far], up_grad), w_down).astype(half)
+    mix[far] = plain(after(gb[far], up_grad), w_down, False, half, "mix_far")
     dh2 = total_of(after(dh2[0], mix[far]), arrived)
-    up_bias_grad = jnp.sum(jnp.concatenate(du, axis=0).astype(single), axis=0)
+    up_bias_grad = sum(jnp.sum(x.astype(single), axis=0) for x in flat(du))
     down_bias_grad = jnp.sum(dz2_own.astype(single), axis=0)
     gain2_grad = jnp.sum(dh2 * normed2, axis=0)
     shift2_grad = jnp.sum(dh2, axis=0)
@@ -558,27 +652,52 @@
     dattn = dot_nt(after(dz1, down_part), w_out).astype(half)
     dattn = xor_order([dattn[:, s * part : (s + 1) * part] for s in range(CTX)], c)
     out_bias_grad = jnp.sum(dz1.astype(single), axis=0)
-    out_grad = dot_tn(ob, after(dz1, dattn)).astype(half)
-    for j in range(1, far):
-        mix[j] = dot_nn(after(gb[j], out_grad), w_down).astype(half)
-    dattn = jnp.concatenate([dattn[0]] + [swap(dattn[j], j) for j in range(1, CTX)], axis=0)
-    dqkv = attn_backward(joined, after(dattn, mix[1:far]), inv, slopes, heads, scale)
-    down_out = gather_ctx(after(down_part, dattn))
-    dqkv = to_rows(jnp.concatenate(dqkv, axis=1))
-    dqkv_at = pieces_of(dqkv)
+    out_grad = outer([ob], [after(dz1, dattn)], "out_grad")
+    mids = plain(after([gb[j][0] for j in mid], out_grad), w_down, False, half, "mix_mid")
+    for j, x in zip(mid, mids):
+        mix[j] = x
+    dattn = [dattn[0]] + after([swap(dattn[j], j) for j in range(1, CTX)], mids)
+    dattn = jnp.concatenate(dattn, axis=0)
+    dqkv = attn_backward(joined, dattn, inv, slopes, heads, scale)
+    down_own = after(down_part, dattn)
+    down_near = gather_first(down_own)
+    dqkv = to_rows(jnp.concatenate(after(dqkv, down_near), axis=1))
+    down_out = gather_second(down_own, down_near)
     dh1 = [None] * CTX
-    for j in reversed(range(1, CTX)):
-        dh1[j] = dot_nt(dqkv_at[j], w_qkv).astype(half)
+    if CTX == 4:
+        dh1[far] = [(dqkv, rows // 2, 2 * far), (dqkv, rows // 2, 2 * far + 1)]
+    else:
+        dh1[far] = [(dqkv, rows, far)]
+    dh1[far] = plain(dh1[far], w_qkv, True, half, "dh1_far")
     first = scatter_first(dh1[far])
-    arrived = scatter_second(dh1, first)
-    dh1[0] = dot_nt(after(dqkv_at[0], up_part, dh1[1:]), w_qkv)
-    qkv_grad = dot_tn(a1, after(dqkv, dh1[0])).astype(half)
-    mix[0] = dot_nn(after(gb[0], qkv_grad), w_down)
-    dh1 = total_of(after(dh1[0], mix[0]), arrived)
+    if first is None:
+        dh1[far] = dh1[far][0]
+    dqkv = after(dqkv, dh1[far])
+    mids = plain([(dqkv, rows, j) for j in mid], w_qkv, True, half, "dh1_mid")
+    for j, x in zip(mid, mids):
+        dh1[j] = x
+    dqkv = after(dqkv, up_part, down_out, mids)
+    dh1[0] = plain([(dqkv, rows, 0)], w_qkv, True, single, "dh1_own")[0]
+    mix[0] = plain(after(gb[0], dh1[0]), w_down, False, single, "mix_own")[0]
+    if first is not None:
+        first = after(first, mix[0])
+    sent = scatter_second(dh1, first)
+    arrived = scatter_send(sent)
+    dqkv = after(dqkv, sent)
+    a1_rows = [block_of(x)[1] for x in a1]
+    qkv_grad = outer(
+        a1,
+        [(dqkv, r, sum(a1_rows[:i]) // r) for i, r in enumerate(a1_rows)],
+        "qkv_grad",
+    )
+    dh1 = total_of(after(dh1[0], qkv_grad), arrived)
     out_part = scatter_f(after(out_grad, up_part))
-    qkv_part = scatter_f(after(qkv_grad, out_part, dh1))
+    qkv_part = scatter_f(after(qkv_grad, out_part))
     mix = after(mix, dh1)
-    mixed = total_of(y1 + bias_d + mix[0], scatter_second(mix, scatter_first(mix[far])))
+    first = scatter_first(mix[far])
+    if first is None:
+        mix[far] = mix[far][0]
+    mixed = total_of(y1 + bias_d + mix[0], scatter_send(scatter_second(mix, first)))
     down_out = lay_out(0, down_out, c, width // min(width, 512))
     up_out = lay_out(1, gather_ctx(after(up_part, dh1)), c, nf)
     sums = jnp.sum(dqkv.astype(single), axis=0)
@@ -599,9 +718,6 @@
         x = x.reshape(-1, 1, inner)
         mask = (jnp.arange(CTX) == c)[None, :, None]
         return jnp.where(mask, x, 0.0).reshape(-1)
-
-    early = [out_bias_grad, gain2_grad, shift2_grad, down_bias_grad, spread(up_bias_grad, fpart)]
-    late = [gain1_grad, shift1_grad, spread(sums[:part], part), spread(sums[2 * part :], part)]
 
     def reduced(items, call):
         sizes = [x.shape[0] // nf for x in items]
@@ -614,8 +730,12 @@
             at += n
         return out
 
-    out_bias_out, gain2_out, shift2_out, down_bias_out, up_bias_out = reduced(early, 2)
-    gain1_out, shift1_out, q_bias_out, v_bias_out = reduced(late, 3)
+    sums_in = [out_bias_grad, gain2_grad, shift2_grad, down_bias_grad, spread(up_bias_grad, fpart)]
+    sums_in += [gain1_grad, shift1_grad, spread(sums[:part], part), spread(sums[2 * part :], part)]
+    sums_in[5] = after(sums_in[5], mixed, up_out, down_out)
+    sums_out = reduced(sums_in, 2)
+    out_bias_out, gain2_out, shift2_out, down_bias_out, up_bias_out = sums_out[:5]
+    gain1_out, shift1_out, q_bias_out, v_bias_out = sums_out[5:]
     return (
         mixed,
         input_grad,

time: 1000 us -> 957 us (0.957)
  the two profiles are of different devices: /device:TPU:0 before, /device:TPU:8 now
where the time goes in v4:
time: 957 us; the launch traced here: 946 us
  Pallas kernels  386 us (40%)
  waiting for transfers between devices  326 us (34%)
  other arithmetic  97 us (10%)
  local copies, waits for them, and re-layouts  52.8 us (6%)
  starting transfers between devices  45.3 us (5%)
  between operations  26 us (3%)
  matrix products  12.7 us (1%)
    ppermute x44, waiting for transfers between devices, swap(): return lax.ppermute(x, 'ctx', [(i, i ^ mask) for i in range(n)])  307 us
    pallas_call x17, Pallas kernels, rows_matmul(): pl.pallas_call(functools.partial(rows_kernel, dot_nt if transposed else d...  194 us
    pallas_call x4, Pallas kernels, outer(): pl.pallas_call(functools.partial(outer_kernel, len(left)), grid=(m // tm,...  74.4 us
    ppermute x44, starting transfers between devices, swap(): return lax.ppermute(x, 'ctx', [(i, i ^ mask) for i in range(n)])  44.7 us
    pallas_call x1, Pallas kernels, attn_backward(): pl.pallas_call(functools.partial(attn_bwd_kernel, scale), grid_spec=pltpu...  35.1 us
    pallas_call x1, Pallas kernels, reduce_small(): pl.pallas_call(functools.partial(reduce_small_kernel, nf, nc), out_shape=...  34.7 us
    pallas_call x1, Pallas kernels, attn_forward(): pl.pallas_call(functools.partial(attn_fwd_kernel, scale), grid_spec=pltpu...  23.6 us
    unnamed x175, local copies, waits for them, and re-layouts  22.1 us
  transfers between devices with their start and end apart: 52, of which 26 were waited for; matrix products, arithmetic and copies ran while one was open for 16% of the time, Pallas kernels for 40%

profile of v4, /device:TPU:8, one launch (start us, length us, event | category | flops | bytes accessed | tf_op | source)
XLA Modules:
  0.0 946.0 jit_solution(11750899964588434123)
XLA Ops:
  16.6 10.0 %gather_small.1 = f32[8,24,128]{2,1,0:T(8,128)} custom-call(f32[24,128]{1,0:T(8,128)} %bitcast.100), custom_call_target="tpu_custom_call" | custom-call | tf_op jit(solution)/shard_map/gather_small/pallas_call | solution.py:412
  27.6 32.7 %collective-permute-done.1 = bf16[512,2048]{1,0:T(8,128)(2,1)} collective-permute-done((bf16[512,2048]{1,0:T(8,128)(2,1)S(1)}, bf16[512,2048]{1,0:T(8,128)(2,1)}, u32[]{:S(2)}, u32[]{:S(2)}) %collective-permute-start.1) | collective-permute-done | bytes 2097184 | tf_op jit(solution)/shard_map/ppermute | solution.py:60
  116.5 18.7 %qkv.1.refs_0_.refs_1_.refs_2_.refs_3_.refs_4_.refs_5_.refs_6_.refs_7_.refs_8_.refs_9_.refs_10_.refs_11_.refs_12_.refs_13_.refs_14_.refs_15_.refs_16_.refs_17_.refs_18_.refs_19_.refs_20_.refs_21_.refs_22_.refs_23_ = bf16[2048,1536]{1,0:T(8,128)(2,1)} custom-call(bf16[512,2048]{1,0:T(8,128)(2,1)} %get-tuple-element.237.refs_0_, ...), custom_call_target="tpu_custom_call" | custom-call | flops 1288490240 | bytes 3565158 | tf_op jit(solution)/shard_map/qkv/pallas_call | solution.py:252
  152.6 23.6 %attn_forward.1 = bf16[2048,512]{1,0:T(8,128)(2,1)S(1)} custom-call(s32[16]{0:T(128)S(1)} %select_reduce_fusion.inv_ref, f32[4]{0:T(128)S(1)} %multiply_power_fusion.slope_ref, ...), custom_call_target="tpu_custom_call" | custom-call | flops 2000000000 | bytes 838860 | tf_op jit(solution)/shard_map/attn_forward/pallas_call | solution.py:188
  189.4 12.6 %collective-permute-done.6 = bf16[512,512]{1,0:T(8,128)(2,1)} collective-permute-done((bf16[512,512]{1,0:T(8,128)(2,1)}, bf16[512,512]{1,0:T(8,128)(2,1)}, u32[]{:S(2)}, u32[]{:S(2)}) %collective-permute-start.6) | collective-permute-done | bytes 524320 | tf_op jit(solution)/shard_map/ppermute | solution.py:60
  223.5 45.2 %collective-permute-done.11.refs_0_.refs_2_ = bf16[512,2048]{1,0:T(8,128)(2,1)S(1)} collective-permute-done((bf16[512,2048]{1,0:T(8,128)(2,1)S(1)}, bf16[512,2048]{1,0:T(8,128)(2,1)S(1)}, u32[]{:S(2)}, u32[]{:S(2)}) %collective-permute-start.11) | collective-permute-done | bytes 2097184 | tf_op jit(solution)/shard_map/ppermute | solution.py:60
  273.4 10.9 %up_gelu_0.1 = (bf16[512,2048]{1,0:T(8,128)(2,1)}, bf16[512,2048]{1,0:T(8,128)(2,1)}) custom-call(bf16[512,2048]{1,0:T(8,128)(2,1)} %copy-done.21, bf16[2048,2048]{1,0:T(8,128)(2,1)} %all-gather.9.cloned.1.call-done.refs_1_.refs_2_, f32[1,2048]{1,0:T(1,128)S(1)} %bitcast.77), custom_call_target="tpu_custom_call" | custom-call | flops 429496736 | bytes 1677721 | tf_op jit(solution)/shard_map/up_gelu_0/pallas_call | solution.py:252
  284.3 10.7 %up_gelu_1.1 = (bf16[512,2048]{1,0:T(8,128)(2,1)}, bf16[512,2048]{1,0:T(8,128)(2,1)}) custom-call(bf16[512,2048]{1,0:T(8,128)(2,1)} %copy-done.25, bf16[2048,2048]{1,0:T(8,128)(2,1)} %all-gather.9.cloned.1.call-done.refs_1_.refs_2_, f32[1,2048]{1,0:T(1,128)S(1)} %bitcast.78), custom_call_target="tpu_custom_call" | custom-call | flops 429496736 | bytes 1677721 | tf_op jit(solution)/shard_map/up_gelu_1/pallas_call | solution.py:252
  295.0 10.7 %up_gelu_2.1 = (bf16[512,2048]{1,0:T(8,128)(2,1)}, bf16[512,2048]{1,0:T(8,128)(2,1)}) custom-call(bf16[512,2048]{1,0:T(8,128)(2,1)} %copy-done.24, bf16[2048,2048]{1,0:T(8,128)(2,1)} %all-gather.9.cloned.1.call-done.refs_1_.refs_2_, f32[1,2048]{1,0:T(1,128)S(1)} %bitcast.79), custom_call_target="tpu_custom_call" | custom-call | flops 429496736 | bytes 1677721 | tf_op jit(solution)/shard_map/up_gelu_2/pallas_call | solution.py:252
  311.1 20.6 %up_gelu_3.1 = (bf16[256,2048]{1,0:T(8,128)(2,1)S(1)}, bf16[256,2048]{1,0:T(8,128)(2,1)}, bf16[256,2048]{1,0:T(8,128)(2,1)}, bf16[256,2048]{1,0:T(8,128)(2,1)}) custom-call(bf16[256,2048]{1,0:T(8,128)(2,1)} %copy-done.2, bf16[256,2048]{1,0:T(8,128)(2,1)} %copy-done.29, bf16[2048,2048]{1,0:T(8,128)(2,1)} %all-gather.9.cloned.1.call-done.refs_1_.refs_2_, ...), custom_call_target="tpu_custom_call" | custom-call | flops 429496736 | bytes 1677721 | tf_op jit(solution)/shard_map/up_gelu_3/pallas_call | solution.py:252
  334.3 23.0 %down_grad.1 = bf16[2048,2048]{1,0:T(8,128)(2,1)} custom-call(bf16[512,2048]{1,0:T(8,128)(2,1)} %get-tuple-element.169.refs_0_, bf16[512,2048]{1,0:T(8,128)(2,1)} %get-tuple-element.148.refs_1_.refs_0_, bf16[512,2048]{1,0:T(8,128)(2,1)} %get-tuple-element.149.refs_2_.refs_1_, bf16[256,2048]{1,0:T(8,128)(2,1)S(1)} %get-tuple-element.141.refs_3_.refs_0_, ...), custom_call_target="tpu_custom_call" | custom-call | flops 1717986944 | bytes 2516582 | tf_op jit(solution)/shard_map/down_grad/pallas_call | solution.py:325
  357.5 9.1 du_far.1
  378.6 13.9 %du_mid.1 = (bf16[512,2048]{1,0:T(8,128)(2,1)}, bf16[512,2048]{1,0:T(8,128)(2,1)}) custom-call(bf16[512,2048]{1,0:T(8,128)(2,1)} %collective-permute-done.4.refs_6_.refs_0_, bf16[512,2048]{1,0:T(8,128)(2,1)} %collective-permute-done.5.refs_7_.refs_1_, bf16[2048,2048]{1,0:T(8,128)(2,1)} %all-gather.11.cloned.1.call-done.refs_2_.refs_1_, ...), custom_call_target="tpu_custom_call" | custom-call | flops 858993472 | bytes 2516582 | tf_op jit(solution)/shard_map/du_mid/pallas_call | solution.py:252
  392.6 13.2 %dh2_mid.1 = (bf16[512,2048]{1,0:T(8,128)(2,1)}, bf16[512,2048]{1,0:T(8,128)(2,1)}) custom-call(bf16[512,2048]{1,0:T(8,128)(2,1)} %get-tuple-element.137.refs_0_.refs_6_, bf16[512,2048]{1,0:T(8,128)(2,1)} %get-tuple-element.138.refs_1_.refs_7_, bf16[2048,2048]{1,0:T(8,128)(2,1)} %all-gather.9.cloned.1.call-done.refs_1_.refs_2_), custom_call_target="tpu_custom_call" | custom-call | flops 858993472 | bytes 2516582 | tf_op jit(solution)/shard_map/dh2_mid/pallas_call | solution.py:252
  413.6 9.9 %du_own.1.refs_0_.refs_5_ = bf16[512,2048]{1,0:T(8,128)(2,1)} custom-call(bf16[512,2048]{1,0:T(8,128)(2,1)} %get-tuple-element.134.refs_5_.refs_0_, bf16[2048,2048]{1,0:T(8,128)(2,1)} %all-gather.11.cloned.1.call-done.refs_2_.refs_1_, bf16[512,2048]{1,0:T(8,128)(2,1)} %get-tuple-element.135.refs_2_), custom_call_target="tpu_custom_call" | custom-call | flops 429496736 | bytes 1677721 | tf_op jit(solution)/shard_map/du_own/pallas_call | solution.py:252
  423.5 9.3 dh2_own.1
  432.8 23.4 %up_grad.1 = bf16[2048,2048]{1,0:T(8,128)(2,1)} custom-call(bf16[512,2048]{1,0:T(8,128)(2,1)} %copy-done.21, bf16[512,2048]{1,0:T(8,128)(2,1)} %copy-done.25, bf16[512,2048]{1,0:T(8,128)(2,1)} %copy-done.24, bf16[256,2048]{1,0:T(8,128)(2,1)S(1)} %copy-done.3, bf16[256,2048]{1,0:T(8,128)(2,1)} %copy-done.29, bf16[512,2048]{1,0:T(8,128)(2,1)} %du_own.1.refs_0_.refs_5_, ...), custom_call_target="tpu_custom_call" | custom-call | flops 1717986944 | bytes 2516582 | tf_op jit(solution)/shard_map/up_grad/pallas_call | solution.py:325
  461.0 9.4 mix_far.1
  470.4 31.1 %collective-permute-done.18 = bf16[512,2048]{1,0:T(8,128)(2,1)S(1)} collective-permute-done((bf16[512,2048]{1,0:T(8,128)(2,1)}, bf16[512,2048]{1,0:T(8,128)(2,1)S(1)}, u32[]{:S(2)}, u32[]{:S(2)}) %collective-permute-start.18) | collective-permute-done | bytes 2097184 | tf_op jit(solution)/shard_map/ppermute | solution.py:60
  515.1 9.3 out_grad.1
  524.4 18.7 %reduce-scatter.7.cloned.1.call-done.refs_0_ = bf16[256,2048]{1,0:T(8,128)(2,1)} async-done(((bf16[2048,2048]{1,0:T(8,128)(2,1)}), bf16[256,2048]{1,0:T(8,128)(2,1)}) %reduce-scatter.7.cloned.1.call-update) | async-done | bytes 1048592 | tf_op jit(solution)/shard_map/reduce_scatter | solution.py:587
  546.8 13.6 %mix_mid.1 = (bf16[512,2048]{1,0:T(8,128)(2,1)}, bf16[512,2048]{1,0:T(8,128)(2,1)}) custom-call(bf16[512,2048]{1,0:T(8,128)(2,1)} %get-tuple-element.148.refs_1_.refs_0_, bf16[512,2048]{1,0:T(8,128)(2,1)} %get-tuple-element.149.refs_2_.refs_1_, bf16[2048,2048]{1,0:T(8,128)(2,1)} %all-gather.11.cloned.1.call-done.refs_2_.refs_1_), custom_call_target="tpu_custom_call" | custom-call | flops 858993472 | bytes 2516582 | tf_op jit(solution)/shard_map/mix_mid/pallas_call | solution.py:252
  560.4 10.3 %collective-permute-done.20 = bf16[512,512]{1,0:T(8,128)(2,1)S(1)} collective-permute-done((bf16[512,512]{1,0:T(8,128)(2,1)S(1)}, bf16[512,512]{1,0:T(8,128)(2,1)S(1)}, u32[]{:S(2)}, u32[]{:S(2)}) %collective-permute-start.20) | collective-permute-done | bytes 524320 | tf_op jit(solution)/shard_map/ppermute | solution.py:60
  574.2 35.1 %attn_backward.1 = (bf16[2048,512]{1,0:T(8,128)(2,1)S(1)}, bf16[2048,512]{1,0:T(8,128)(2,1)S(1)}, bf16[2048,512]{1,0:T(8,128)(2,1)}) custom-call(s32[16]{0:T(128)S(1)} %select_reduce_fusion.inv_ref, f32[4]{0:T(128)S(1)} %multiply_power_fusion.slope_ref, ...), custom_call_target="tpu_custom_call" | custom-call | flops 4000000000 | bytes 1468006 | tf_op jit(solution)/shard_map/attn_backward/pallas_call | solution.py:205
  626.1 10.5 %dh1_mid.1 = (bf16[512,2048]{1,0:T(8,128)(2,1)}, bf16[512,2048]{1,0:T(8,128)(2,1)}) custom-call(bf16[2048,1536]{1,0:T(8,128)(2,1)} %copy-done.14, bf16[2048,1536]{1,0:T(8,128)(2,1)} %copy-done.14, bf16[2048,1536]{1,0:T(8,128)(2,1)} %all-gather.5.cloned.1.call-done.refs_5_.refs_2_.refs_1_), custom_call_target="tpu_custom_call" | custom-call | flops 644245120 | bytes 2097152 | tf_op jit(solution)/shard_map/dh1_mid/pallas_call | solution.py:252
  639.3 18.3 %collective-permute-done.25.refs_4_ = bf16[128,2048]{1,0:T(8,128)(2,1)S(1)} collective-permute-done((bf16[128,2048]{1,0:T(8,128)(2,1)S(1)}, bf16[128,2048]{1,0:T(8,128)(2,1)S(1)}, u32[]{:S(2)}, u32[]{:S(2)}) %collective-permute-start.25) | collective-permute-done | bytes 524320 | tf_op jit(solution)/shard_map/ppermute | solution.py:60
  667.0 9.3 mix_own.1
  683.0 18.6 %qkv_grad.1 = bf16[2048,1536]{1,0:T(8,128)(2,1)} custom-call(bf16[512,2048]{1,0:T(8,128)(2,1)} %get-tuple-element.237.refs_0_, bf16[512,2048]{1,0:T(8,128)(2,1)} %get-tuple-element.236.refs_1_, bf16[512,2048]{1,0:T(8,128)(2,1)} %get-tuple-element.235.refs_2_, bf16[256,2048]{1,0:T(8,128)(2,1)S(1)} %get-tuple-element.234.refs_3_, ...), custom_call_target="tpu_custom_call" | custom-call | flops 1288490240 | bytes 2097152 | tf_op jit(solution)/shard_map/qkv_grad/pallas_call | solution.py:325
  708.2 39.7 %collective-permute-done.29 = bf16[512,2048]{1,0:T(8,128)(2,1)} collective-permute-done((bf16[512,2048]{1,0:T(8,128)(2,1)}, bf16[512,2048]{1,0:T(8,128)(2,1)}, u32[]{:S(2)}, u32[]{:S(2)}) %collective-permute-start.29) | collective-permute-done | bytes 2097184 | tf_op jit(solution)/shard_map/ppermute | solution.py:60
  760.0 16.5 %collective-permute-done.32 = bf16[256,2048]{1,0:T(8,128)(2,1)} collective-permute-done((bf16[256,2048]{1,0:T(8,128)(2,1)S(1)}, bf16[256,2048]{1,0:T(8,128)(2,1)}, u32[]{:S(2)}, u32[]{:S(2)}) %collective-permute-start.32) | collective-permute-done | bytes 1048608 | tf_op jit(solution)/shard_map/ppermute | solution.py:60
  792.7 53.5 %collective-permute-done.35.refs_2_ = bf16[256,2048]{1,0:T(8,128)(2,1)S(1)} collective-permute-done((bf16[256,2048]{1,0:T(8,128)(2,1)}, bf16[256,2048]{1,0:T(8,128)(2,1)S(1)}, u32[]{:S(2)}, u32[]{:S(2)}) %collective-permute-start.35) | collective-permute-done | bytes 1048608 | tf_op jit(solution)/shard_map/ppermute | solution.py:60
  889.6 34.7 %reduce_small.1 = f32[24,128]{1,0:T(8,128)} custom-call(f32[8,24,128]{2,1,0:T(8,128)} %bitcast.85), custom_call_target="tpu_custom_call" | custom-call | tf_op jit(solution)/shard_map/reduce_small/pallas_call | solution.py:483
  (417 shorter events, 293.7 us)
Async XLA Ops:
  7.3 109.2 %all-gather.5.cloned.1.call-start = ((), (), s32[]{:S(2)}) async-start(), calls=%async_computation.4 | async-start | bytes 7077888 | tf_op jit(solution)/shard_map/all_gather | solution.py:547
  9.9 202.1 %all-gather.7.cloned.1.call-start = ((), (), s32[]{:S(2)}) async-start(), calls=%async_computation.5 | async-start | bytes 9437184 | tf_op jit(solution)/shard_map/all_gather | solution.py:547
  12.7 260.7 %all-gather.9.cloned.1.call-start = ((), (), s32[]{:S(2)}) async-start(), calls=%async_computation.6 | async-start | bytes 9437184 | tf_op jit(solution)/shard_map/all_gather | solution.py:547
  12.7 47.5 %collective-permute-start.1 = (bf16[512,2048]{1,0:T(8,128)(2,1)S(1)}, bf16[512,2048]{1,0:T(8,128)(2,1)}, u32[]{:S(2)}, u32[]{:S(2)}) collective-permute-start(bf16[512,2048]{1,0:T(8,128)(2,1)S(1)} %copy-done.18), channel_id=1, source_target_pairs={{0,16},{8,24},{16,0},{24,8},{1,17},{9,25},{17,1},{25,9},{2,18},{10... | collective-permute-start | bytes 6291464 | tf_op jit(solution)/shard_map/ppermute | solution.py:60
  14.3 47.2 %collective-permute-start = (bf16[512,2048]{1,0:T(8,128)(2,1)S(1)}, bf16[512,2048]{1,0:T(8,128)(2,1)}, u32[]{:S(2)}, u32[]{:S(2)}) collective-permute-start(bf16[512,2048]{1,0:T(8,128)(2,1)S(1)} %copy-done.18), channel_id=1, source_target_pairs={{0,8},{8,0},{16,24},{24,16},{1,9},{9,1},{17,25},{25,17},{2,10},{10... | collective-permute-start | bytes 6291464 | tf_op jit(solution)/shard_map/ppermute | solution.py:60
  91.4 266.1 %all-gather.11.cloned.1.call-start = ((), (), s32[]{:S(2)}) async-start(), calls=%async_computation.7 | async-start | bytes 9437184 | tf_op jit(solution)/shard_map/all_gather | solution.py:547
  135.2 321.0 %reduce-scatter.5.cloned.1.call-start = ((), (), s32[]{:S(2)}) async-start(), calls=%async_computation.8 | async-start | bytes 9437184 | tf_op jit(solution)/shard_map/reduce_scatter | solution.py:587
  140.0 45.4 %collective-permute-start.5 = (bf16[512,2048]{1,0:T(8,128)(2,1)}, bf16[512,2048]{1,0:T(8,128)(2,1)}, u32[]{:S(2)}, u32[]{:S(2)}) collective-permute-start(bf16[512,2048]{1,0:T(8,128)(2,1)} %get-tuple-element.134.refs_5_.refs_0_), channel_id=1, source_target_pairs={{0,16},{8,24},{16,0},{24,8},{1,17},{9,25},{17,1},{25,9},{2,18},{10... | collective-permute-start | bytes 6291464 | tf_op jit(solution)/shard_map/ppermute | solution.py:60
  140.6 45.3 %collective-permute-start.4 = (bf16[512,2048]{1,0:T(8,128)(2,1)}, bf16[512,2048]{1,0:T(8,128)(2,1)}, u32[]{:S(2)}, u32[]{:S(2)}) collective-permute-start(bf16[512,2048]{1,0:T(8,128)(2,1)} %get-tuple-element.134.refs_5_.refs_0_), channel_id=1, source_target_pairs={{0,8},{8,0},{16,24},{24,16},{1,9},{9,1},{17,25},{25,17},{2,10},{10... | collective-permute-start | bytes 6291464 | tf_op jit(solution)/shard_map/ppermute | solution.py:60
  221.6 47.1 %collective-permute-start.11 = (bf16[512,2048]{1,0:T(8,128)(2,1)S(1)}, bf16[512,2048]{1,0:T(8,128)(2,1)S(1)}, u32[]{:S(2)}, u32[]{:S(2)}) collective-permute-start(bf16[512,2048]{1,0:T(8,128)(2,1)S(1)} %add_convert_fusion.refs_0_), channel_id=1, source_target_pairs={{0,16},{8,24},{16,0},{24,8},{1,17},{9,25},{17,1},{25,9},{2,18},{10... | collective-permute-start | bytes 6291464 | tf_op jit(solution)/shard_map/ppermute | solution.py:60
  222.6 48.6 %collective-permute-start.9 = (bf16[512,2048]{1,0:T(8,128)(2,1)S(1)}, bf16[512,2048]{1,0:T(8,128)(2,1)S(1)}, u32[]{:S(2)}, u32[]{:S(2)}) collective-permute-start(bf16[512,2048]{1,0:T(8,128)(2,1)S(1)} %add_convert_fusion.refs_0_), channel_id=1, source_target_pairs={{0,8},{8,0},{16,24},{24,16},{1,9},{9,1},{17,25},{25,17},{2,10},{10... | collective-permute-start | bytes 6291464 | tf_op jit(solution)/shard_map/ppermute | solution.py:60
  269.9 35.8 %collective-permute-start.12 = (bf16[256,2048]{1,0:T(8,128)(2,1)}, bf16[256,2048]{1,0:T(8,128)(2,1)S(1)}, u32[]{:S(2)}, u32[]{:S(2)}) collective-permute-start(bf16[256,2048]{1,0:T(8,128)(2,1)} %slice.344), channel_id=1, source_target_pairs={{0,8},{8,0},{16,24},{24,16},{1,9},{9,1},{17,25},{25,17},{2,10},{10... | collective-permute-start | bytes 3145736 | tf_op jit(solution)/shard_map/ppermute | solution.py:60
  357.4 185.7 %reduce-scatter.7.cloned.1.call-start = ((), (), s32[]{:S(2)}) async-start(), calls=%async_computation.9 | async-start | bytes 9437184 | tf_op jit(solution)/shard_map/reduce_scatter | solution.py:587
  456.2 245.4 %reduce-scatter.9.cloned.1.call-start = ((), (), s32[]{:S(2)}) async-start(), calls=%async_computation.10 | async-start | bytes 9437184 | tf_op jit(solution)/shard_map/reduce_scatter | solution.py:587
  456.3 45.2 %collective-permute-start.18 = (bf16[512,2048]{1,0:T(8,128)(2,1)}, bf16[512,2048]{1,0:T(8,128)(2,1)S(1)}, u32[]{:S(2)}, u32[]{:S(2)}) collective-permute-start(bf16[512,2048]{1,0:T(8,128)(2,1)} %pad_maximum_fusion.2), channel_id=1, source_target_pairs={{0,16},{8,24},{16,0},{24,8},{1,17},{9,25},{17,1},{25,9},{2,18},{10... | collective-permute-start | bytes 6291464 | tf_op jit(solution)/shard_map/ppermute | solution.py:60
  457.2 44.7 %collective-permute-start.17 = (bf16[512,2048]{1,0:T(8,128)(2,1)S(1)}, bf16[512,2048]{1,0:T(8,128)(2,1)}, u32[]{:S(2)}, u32[]{:S(2)}) collective-permute-start(bf16[512,2048]{1,0:T(8,128)(2,1)S(1)} %pad_maximum_fusion.1), channel_id=1, source_target_pairs={{0,8},{8,0},{16,24},{24,16},{1,9},{9,1},{17,25},{25,17},{2,10},{10... | collective-permute-start | bytes 6291464 | tf_op jit(solution)/shard_map/ppermute | solution.py:60
  543.1 343.8 %reduce-scatter.11.cloned.1.call-start = ((), (), s32[]{:S(2)}) async-start(), calls=%async_computation.11 | async-start | bytes 7077888 | tf_op jit(solution)/shard_map/reduce_scatter | solution.py:587
  572.2 37.1 %collective-permute-start.23 = (bf16[256,2048]{1,0:T(8,128)(2,1)S(1)}, bf16[256,2048]{1,0:T(8,128)(2,1)S(1)}, u32[]{:S(2)}, u32[]{:S(2)}) collective-permute-start(bf16[256,2048]{1,0:T(8,128)(2,1)S(1)} %copy-done.5), channel_id=1, source_target_pairs={{0,16},{8,24},{16,0},{24,8},{1,17},{9,25},{17,1},{25,9},{2,18},{10... | collective-permute-start | bytes 3145736 | tf_op jit(solution)/shard_map/ppermute | solution.py:60
  573.6 35.7 %collective-permute-start.22 = (bf16[256,2048]{1,0:T(8,128)(2,1)S(1)}, bf16[256,2048]{1,0:T(8,128)(2,1)S(1)}, u32[]{:S(2)}, u32[]{:S(2)}) collective-permute-start(bf16[256,2048]{1,0:T(8,128)(2,1)S(1)} %copy-done.5), channel_id=1, source_target_pairs={{0,8},{8,0},{16,24},{24,16},{1,9},{9,1},{17,25},{25,17},{2,10},{10... | collective-permute-start | bytes 3145736 | tf_op jit(solution)/shard_map/ppermute | solution.py:60
  621.8 54.5 %collective-permute-start.26 = (bf16[256,2048]{1,0:T(8,128)(2,1)S(1)}, bf16[256,2048]{1,0:T(8,128)(2,1)}, u32[]{:S(2)}, u32[]{:S(2)}) collective-permute-start(bf16[256,2048]{1,0:T(8,128)(2,1)S(1)} %get-tuple-element.162), channel_id=1, source_target_pairs={{0,8},{8,0},{16,24},{24,16},{1,9},{9,1},{17,25},{25,17},{2,10},{10... | collective-permute-start | bytes 3145736 | tf_op jit(solution)/shard_map/ppermute | solution.py:60
  623.3 53.0 %collective-permute-start.27 = (bf16[256,2048]{1,0:T(8,128)(2,1)}, bf16[256,2048]{1,0:T(8,128)(2,1)}, u32[]{:S(2)}, u32[]{:S(2)}) collective-permute-start(bf16[256,2048]{1,0:T(8,128)(2,1)} %get-tuple-element.163), channel_id=1, source_target_pairs={{0,16},{8,24},{16,0},{24,8},{1,17},{9,25},{17,1},{25,9},{2,18},{10... | collective-permute-start | bytes 3145736 | tf_op jit(solution)/shard_map/ppermute | solution.py:60
  623.9 33.6 %collective-permute-start.25 = (bf16[128,2048]{1,0:T(8,128)(2,1)S(1)}, bf16[128,2048]{1,0:T(8,128)(2,1)S(1)}, u32[]{:S(2)}, u32[]{:S(2)}) collective-permute-start(bf16[128,2048]{1,0:T(8,128)(2,1)S(1)} %slice.350), channel_id=1, source_target_pairs={{0,8},{8,0},{16,24},{24,16},{1,9},{9,1},{17,25},{25,17},{2,10},{10... | collective-permute-start | bytes 1572872 | tf_op jit(solution)/shard_map/ppermute | solution.py:60
  625.0 34.0 %collective-permute-start.24 = (bf16[128,2048]{1,0:T(8,128)(2,1)S(1)}, bf16[128,2048]{1,0:T(8,128)(2,1)S(1)}, u32[]{:S(2)}, u32[]{:S(2)}) collective-permute-start(bf16[128,2048]{1,0:T(8,128)(2,1)S(1)} %slice.349), channel_id=1, source_target_pairs={{0,16},{8,24},{16,0},{24,8},{1,17},{9,25},{17,1},{25,9},{2,18},{10... | collective-permute-start | bytes 1572872 | tf_op jit(solution)/shard_map/ppermute | solution.py:60
  701.7 46.2 %collective-permute-start.29 = (bf16[512,2048]{1,0:T(8,128)(2,1)}, bf16[512,2048]{1,0:T(8,128)(2,1)}, u32[]{:S(2)}, u32[]{:S(2)}) collective-permute-start(bf16[512,2048]{1,0:T(8,128)(2,1)} %pad_maximum_fusion.5), channel_id=1, source_target_pairs={{0,16},{8,24},{16,0},{24,8},{1,17},{9,25},{17,1},{25,9},{2,18},{10... | collective-permute-start | bytes 6291464 | tf_op jit(solution)/shard_map/ppermute | solution.py:60
  702.3 45.8 %collective-permute-start.28 = (bf16[512,2048]{1,0:T(8,128)(2,1)}, bf16[512,2048]{1,0:T(8,128)(2,1)}, u32[]{:S(2)}, u32[]{:S(2)}) collective-permute-start(bf16[512,2048]{1,0:T(8,128)(2,1)} %pad_maximum_fusion.4), channel_id=1, source_target_pairs={{0,8},{8,0},{16,24},{24,16},{1,9},{9,1},{17,25},{25,17},{2,10},{10... | collective-permute-start | bytes 6291464 | tf_op jit(solution)/shard_map/ppermute | solution.py:60
  779.8 94.0 %collective-permute-start.33 = (bf16[512,2048]{1,0:T(8,128)(2,1)}, bf16[512,2048]{1,0:T(8,128)(2,1)}, u32[]{:S(2)}, u32[]{:S(2)}) collective-permute-start(bf16[512,2048]{1,0:T(8,128)(2,1)} %pad_maximum_fusion.7), channel_id=1, source_target_pairs={{0,16},{8,24},{16,0},{24,8},{1,17},{9,25},{17,1},{25,9},{2,18},{10... | collective-permute-start | bytes 6291464 | tf_op jit(solution)/shard_map/ppermute | solution.py:60
  784.5 89.2 %collective-permute-start.31 = (bf16[512,2048]{1,0:T(8,128)(2,1)}, bf16[512,2048]{1,0:T(8,128)(2,1)}, u32[]{:S(2)}, u32[]{:S(2)}) collective-permute-start(bf16[512,2048]{1,0:T(8,128)(2,1)} %pad_maximum_fusion.6), channel_id=1, source_target_pairs={{0,8},{8,0},{16,24},{24,16},{1,9},{9,1},{17,25},{25,17},{2,10},{10... | collective-permute-start | bytes 6291464 | tf_op jit(solution)/shard_map/ppermute | solution.py:60
  789.7 56.5 %collective-permute-start.35 = (bf16[256,2048]{1,0:T(8,128)(2,1)}, bf16[256,2048]{1,0:T(8,128)(2,1)S(1)}, u32[]{:S(2)}, u32[]{:S(2)}) collective-permute-start(bf16[256,2048]{1,0:T(8,128)(2,1)} %reduce-scatter.7.cloned.1.call-done.refs_0_), channel_id=1, source_target_pairs={{0,16},{8,24},{16,0},{24,8},{1,17},{9,25},{17,1},{25,9},{2,18},{10... | collective-permute-start | bytes 3145736 | tf_op jit(solution)/shard_map/ppermute | solution.py:60
  790.5 65.3 %collective-permute-start.34 = (bf16[256,2048]{1,0:T(8,128)(2,1)}, bf16[256,2048]{1,0:T(8,128)(2,1)S(1)}, u32[]{:S(2)}, u32[]{:S(2)}) collective-permute-start(bf16[256,2048]{1,0:T(8,128)(2,1)} %reduce-scatter.7.cloned.1.call-done.refs_0_), channel_id=1, source_target_pairs={{0,8},{8,0},{16,24},{24,16},{1,9},{9,1},{17,25},{25,17},{2,10},{10... | collective-permute-start | bytes 3145736 | tf_op jit(solution)/shard_map/ppermute | solution.py:60
  886.0 43.1 %collective-permute-start.43 = (bf16[256,2048]{1,0:T(8,128)(2,1)S(1)}, bf16[256,2048]{1,0:T(8,128)(2,1)}, u32[]{:S(2)}, u32[]{:S(2)}) collective-permute-start(bf16[256,2048]{1,0:T(8,128)(2,1)S(1)} %add_convert_fusion.1), channel_id=1, source_target_pairs={{0,16},{8,24},{16,0},{24,8},{1,17},{9,25},{17,1},{25,9},{2,18},{10... | collective-permute-start | bytes 3145736 | tf_op jit(solution)/shard_map/ppermute | solution.py:60
  887.0 40.0 %collective-permute-start.39 = (bf16[256,1536]{1,0:T(8,128)(2,1)}, bf16[256,1536]{1,0:T(8,128)(2,1)S(1)}, u32[]{:S(2)}, u32[]{:S(2)}) collective-permute-start(bf16[256,1536]{1,0:T(8,128)(2,1)} %reduce-scatter.11.cloned.1.call-done.refs_0_), channel_id=1, source_target_pairs={{0,16},{8,24},{16,0},{24,8},{1,17},{9,25},{17,1},{25,9},{2,18},{10... | collective-permute-start | bytes 2359304 | tf_op jit(solution)/shard_map/ppermute | solution.py:60
  888.2 39.7 %collective-permute-start.38 = (bf16[256,1536]{1,0:T(8,128)(2,1)}, bf16[256,1536]{1,0:T(8,128)(2,1)S(1)}, u32[]{:S(2)}, u32[]{:S(2)}) collective-permute-start(bf16[256,1536]{1,0:T(8,128)(2,1)} %reduce-scatter.11.cloned.1.call-done.refs_0_), channel_id=1, source_target_pairs={{0,8},{8,0},{16,24},{24,16},{1,9},{9,1},{17,25},{25,17},{2,10},{10... | collective-permute-start | bytes 2359304 | tf_op jit(solution)/shard_map/ppermute | solution.py:60
  (83 other events, 1360.6 us)
Sparse Core Ops, SparseCore 0:
  10.3 64.8 all-gather.4
  77.4 79.7 all-gather.6
  159.4 80.5 all-gather.8
  241.4 80.5 all-gather.10
  357.5 87.7 reduce-scatter.4
  456.4 86.7 reduce-scatter.6
  546.0 87.9 reduce-scatter.8
  701.8 65.3 reduce-scatter.10

commit v5 on v4

--- a/solution.py
+++ b/solution.py
@@ -218,7 +218,7 @@
     )(inv, slopes, *([joined] * 24), *([grad] * 8))
 
 
-HINT = 0.1
+HINT = 0.001
 
 
 def block_of(x):
@@ -333,6 +333,264 @@
         cost_estimate=hint(2 * rows * m * n, 2 * rows * (m + n) + 2 * m * n),
         name=name,
     )(*[x[0] for x in left], *[x[0] for x in right])
+
+
+def partner(mask):
+    c = lax.axis_index("ctx")
+    if mask == 1:
+        return c + 1 - 2 * lax.rem(c, 2)
+    return lax.rem(c + 2, 4) if mask == 2 else 3 - c
+
+
+def greet(masks):
+    barrier = pltpu.get_barrier_semaphore()
+    for mask in masks:
+        pl.semaphore_signal(
+            barrier,
+            inc=1,
+            device_id={"ctx": partner(mask)},
+            device_id_type=pl.DeviceIdType.MESH,
+        )
+    pl.semaphore_wait(barrier, len(masks))
+
+
+class Moves:
+    def __init__(self, send_sem, recv_sem):
+        self.send_sem, self.recv_sem, self.used = send_sem, recv_sem, 0
+
+    def start(self, src, dst, mask):
+        copy = pltpu.make_async_remote_copy(
+            src_ref=src,
+            dst_ref=dst,
+            send_sem=self.send_sem.at[self.used],
+            recv_sem=self.recv_sem.at[self.used],
+            device_id={"ctx": partner(mask)},
+            device_id_type=pl.DeviceIdType.MESH,
+        )
+        self.used += 1
+        copy.start()
+        return copy
+
+
+def multiply(lefts, w, transposed, extras, outs, epilogue, tile=512):
+    k = lefts[0].shape[1]
+    n = w.shape[0] if transposed else w.shape[1]
+    t = math.gcd(n, tile)
+    w_spec = (
+        pl.BlockSpec((t, k), lambda i: (i, 0)) if transposed else pl.BlockSpec((k, t), lambda i: (0, i))
+    )
+    dot = dot_nt if transposed else dot_nn
+
+    def body(*refs):
+        rows_kernel(dot, epilogue, len(lefts), len(extras), *refs)
+
+    pltpu.emit_pipeline(
+        body,
+        grid=(n // t,),
+        in_specs=[pl.BlockSpec((x.shape[0], k), lambda i: (0, 0)) for x in lefts]
+        + [w_spec]
+        + [pl.BlockSpec((x.shape[0], t), lambda i: (0, i)) for x in extras],
+        out_specs=[pl.BlockSpec((x.shape[0], t), lambda i: (0, i)) for x in outs],
+    )(*lefts, w, *extras, *outs)
+
+
+def store(i, x, extras, outs):
+    outs[i][...] = x.astype(outs[i].dtype)
+
+
+def store_sum(i, x, extras, outs):
+    outs[i][...] = (x + extras[i][...].astype(single)).astype(outs[i].dtype)
+
+
+def store_hidden(i, x, extras, outs):
+    outs[i][...] = (x.astype(half).astype(single) * extras[i][...].astype(single)).astype(half)
+
+
+def outer_on(lefts, rights, out):
+    m, n = out.shape
+    tm = math.gcd(m, 1024)
+    tn = n // 2 if n % 256 == 0 and n > 1024 else n
+
+    def body(*refs):
+        outer_kernel(len(lefts), *refs)
+
+    pltpu.emit_pipeline(
+        body,
+        grid=(m // tm, n // tn),
+        in_specs=[pl.BlockSpec((x.shape[0], tm), lambda i, j: (0, i)) for x in lefts]
+        + [pl.BlockSpec((x.shape[0], tn), lambda i, j: (0, j)) for x in rights],
+        out_specs=[pl.BlockSpec((tm, tn), lambda i, j: (i, j))],
+    )(*lefts, *rights, out)
+
+
+def halves(ref):
+    n = ref.shape[0] // 2
+    return ref.at[pl.ds(0, n)], ref.at[pl.ds(n, n)]
+
+
+def moving_call(kernel, operands, outs, moves, call, flops, name):
+    anywhere = pl.BlockSpec(memory_space=pl.ANY)
+    sems = pltpu.SemaphoreType.DMA((moves,))
+    return pl.pallas_call(
+        kernel,
+        in_specs=[anywhere] * len(operands),
+        out_specs=[anywhere] * len(outs),
+        out_shape=[jax.ShapeDtypeStruct(shape, dtype) for shape, dtype in outs],
+        scratch_shapes=[sems, sems],
+        compiler_params=pltpu.CompilerParams(
+            collective_id=call, has_side_effects=True, vmem_limit_bytes=52 * 1024 * 1024
+        ),
+        cost_estimate=hint(flops, 0),
+        name=name,
+    )(*operands)
+
+
+def feed_back_kernel(*refs):
+    dz, slope, a2, gb_far = refs[0:5], refs[5:10], refs[10:15], refs[15:17]
+    w_down, w_up = refs[17:19]
+    du, own, p3, p1, p2 = refs[19:24], refs[24], refs[25:27], refs[27], refs[28]
+    from_x, from_y, land1, land2, up_grad = refs[29:34]
+    mix_far = refs[34:36]
+    moves = Moves(*refs[36:38])
+    greet((1, 2))
+    multiply(dz[3:5], w_down, True, slope[3:5], du[3:5], store_hidden)
+    multiply(du[3:5], w_up, True, [], p3, store)
+    first = [moves.start(p3[0], from_x, 1), moves.start(p3[1], from_y, 2)]
+    multiply(dz[1:3], w_down, True, slope[1:3], du[1:3], store_hidden)
+    (p1_lo, p1_hi), (p2_lo, p2_hi) = halves(p1), halves(p2)
+    (du1_lo, du1_hi), (du2_lo, du2_hi) = halves(du[1]), halves(du[2])
+    (land1_lo, land1_hi), (land2_lo, land2_hi) = halves(land1), halves(land2)
+    multiply([du1_lo, du2_hi], w_up, True, [], [p1_lo, p2_hi], store)
+    second = [moves.start(p1_lo, land1_lo, 1), moves.start(p2_hi, land2_hi, 2)]
+    for copy in first:
+        copy.wait()
+    multiply([du1_hi, du2_lo], w_up, True, [from_y, from_x], [p1_hi, p2_lo], store_sum)
+    second += [moves.start(p1_hi, land1_hi, 1), moves.start(p2_lo, land2_lo, 2)]
+    multiply(dz[0:1], w_down, True, slope[0:1], du[0:1], store_hidden)
+    multiply(du[0:1], w_up, True, [], [own], store)
+    outer_on(a2, du, up_grad)
+    multiply(gb_far, w_down, False, [], mix_far, store)
+    for copy in second:
+        copy.wait()
+
+
+def feed_back(dz, slope, a2, gb_far, w_down, w_up):
+    rows, width = dz[0].shape
+    wide = w_down.shape[0]
+    n = rows // 2
+    sizes = [rows, rows, rows, n, n]
+    outs = [((r, wide), half) for r in sizes]
+    outs += [((rows, width), single)]
+    outs += [((n, width), half)] * 2 + [((rows, width), half)] * 2
+    outs += [((n, width), half)] * 2 + [((rows, width), half)] * 2
+    outs += [((width, wide), half)] + [((n, width), half)] * 2
+    out = moving_call(
+        feed_back_kernel,
+        [*dz, *slope, *a2, *gb_far, w_down, w_up],
+        outs,
+        6,
+        3,
+        26 * rows * width * wide,
+        "feed_back",
+    )
+    du, own, land, up_grad, mix_far = out[0:5], out[5], out[12:14], out[14], out[15:17]
+    return du, own, land, up_grad, mix_far
+
+
+def heads_back_kernel(part, *refs):
+    dattn, ob, dz1, gb1, gb2, w_down = refs[0:6]
+    got, out_grad, mix1, mix2 = refs[6:10]
+    moves = Moves(*refs[10:12])
+    local = refs[12]
+    rows = dattn.shape[0]
+    c = lax.axis_index("ctx")
+
+    def columns(of):
+        return dattn.at[:, pl.ds(pl.multiple_of(of * part, part), part)]
+
+    greet((1, 2, 3))
+    copies = []
+    for mask in (3, 1, 2):
+        at = got.at[pl.ds(mask * rows, rows)]
+        copies.append(moves.start(columns(partner(mask)), at, mask))
+    own = pltpu.make_async_copy(columns(c), got.at[pl.ds(0, rows)], local)
+    own.start()
+    outer_on([ob], [dz1], out_grad)
+    multiply([gb1, gb2], w_down, False, [], [mix1, mix2], store)
+    own.wait()
+    for copy in copies:
+        copy.wait()
+
+
+def heads_back(dattn, ob, dz1, gb1, gb2, w_down, part):
+    rows, width = dattn.shape
+    anywhere = pl.BlockSpec(memory_space=pl.ANY)
+    sems = pltpu.SemaphoreType.DMA((3,))
+    outs = [((4 * rows, part), half), ((width, width), half)] + [((rows, width), half)] * 2
+    return pl.pallas_call(
+        functools.partial(heads_back_kernel, part),
+        in_specs=[anywhere] * 6,
+        out_specs=[anywhere] * 4,
+        out_shape=[jax.ShapeDtypeStruct(shape, dtype) for shape, dtype in outs],
+        scratch_shapes=[sems, sems, pltpu.SemaphoreType.DMA],
+        compiler_params=pltpu.CompilerParams(
+            collective_id=4, has_side_effects=True, vmem_limit_bytes=52 * 1024 * 1024
+        ),
+        cost_estimate=hint(10 * rows * width * width, 0),
+        name="heads_back",
+    )(dattn, ob, dz1, gb1, gb2, w_down)
+
+
+def qkv_back_kernel(*refs):
+    dqkv, w_qkv = refs[0:2]
+    a1, gb_own, w_down = refs[2:7], refs[7], refs[8]
+    own, p3, p1, p2, from_x, from_y, land1, land2, qkv_grad, mix_own = refs[9:19]
+    moves = Moves(*refs[19:21])
+    rows = own.shape[0]
+    n = rows // 2
+
+    def block(k):
+        return dqkv.at[pl.ds(k * n, n)]
+
+    greet((1, 2))
+    (p3_lo, p3_hi), (p1_lo, p1_hi), (p2_lo, p2_hi) = halves(p3), halves(p1), halves(p2)
+    (land1_lo, land1_hi), (land2_lo, land2_hi) = halves(land1), halves(land2)
+    multiply([block(6), block(7)], w_qkv, True, [], [p3_lo, p3_hi], store)
+    first = [moves.start(p3_lo, from_x, 1), moves.start(p3_hi, from_y, 2)]
+    multiply([block(2), block(5)], w_qkv, True, [], [p1_lo, p2_hi], store)
+    second = [moves.start(p1_lo, land1_lo, 1), moves.start(p2_hi, land2_hi, 2)]
+    multiply([dqkv.at[pl.ds(0, rows)]], w_qkv, True, [], [own], store)
+    multiply([gb_own], w_down, False, [], [mix_own], store)
+    for copy in first:
+        copy.wait()
+    multiply([block(3), block(4)], w_qkv, True, [from_y, from_x], [p1_hi, p2_lo], store_sum)
+    second += [moves.start(p1_hi, land1_hi, 1), moves.start(p2_lo, land2_lo, 2)]
+    rights, at = [], 0
+    for x in a1:
+        rights.append(dqkv.at[pl.ds(at, x.shape[0])])
+        at += x.shape[0]
+    outer_on(a1, rights, qkv_grad)
+    for copy in second:
+        copy.wait()
+
+
+def qkv_back(dqkv, w_qkv, a1, gb_own, w_down):
+    rows, width = a1[0].shape
+    wide = gb_own.shape[1]
+    n = rows // 2
+    outs = [((rows, width), single)] + [((rows, width), half)] * 3
+    outs += [((n, width), half)] * 2 + [((rows, width), half)] * 2
+    outs += [((width, dqkv.shape[1]), half), ((rows, width), single)]
+    out = moving_call(
+        qkv_back_kernel,
+        [dqkv, w_qkv, *a1, gb_own, w_down],
+        outs,
+        6,
+        5,
+        16 * rows * width * dqkv.shape[1] + 2 * rows * width * wide,
+        "qkv_back",
+    )
+    return out[0], out[6:8], out[8], out[9]
 
 
 def lay_out_kernel(axis, layout, c_ref, *refs):
@@ -589,15 +847,18 @@
     far = CTX - 1
     mid = list(range(1, far))
 
-    tok_near = gather_first(tokens)
-    tok = flat(gather_second(tokens, after(tok_near, small_all)))
+    def first_norm(x):
+        normed, _ = norm_parts(x.astype(single))
+        return (normed * gain1 + shift1).astype(half)
+
+    tok_near = after(gather_first(tokens), small_all, place, inv, slopes)
+    tok = gather_second(tokens, tok_near)
+    near = [[first_norm(x) for x in p] for p in tok[:far]]
+    tok = after(tok, near)
     dz2_own = after(cotangent, tok).astype(half)
     dz2_near = gather_first(dz2_own)
     w_up = gather_f(after(up_own.astype(half), tok))
-    a1 = []
-    for x in tok:
-        normed, _ = norm_parts(x.astype(single))
-        a1.append((normed * gain1 + shift1).astype(half))
+    a1 = flat(near) + [first_norm(x) for x in tok[far]]
     joined = joined_rows(a1, w_qkv, bias_qkv, "qkv")
     w_down = gather_f(after(down_own.astype(half), joined))
     attended = to_rows(attn_forward(joined, inv, slopes, heads, scale))
@@ -608,12 +869,12 @@
     y1 = tokens.astype(single) + dot_nn(ob, w_out) + bias_o
 
     normed2, inv2 = norm_parts(y1)
-    a2 = gather_ctx((normed2 * gain2 + shift2).astype(half))
+    dz2 = gather_second(dz2_own, after(dz2_near, ob))
+    a2_own = (normed2 * gain2 + shift2).astype(half)
+    a2 = gather_second(a2_own, gather_first(a2_own))
     gb, slope = [None] * CTX, [None] * CTX
     last = ()
     for j in range(CTX):
-        if j == far:
-            dz2 = gather_second(dz2_own, after(dz2_near, a2[far], last))
         gb[j], slope[j] = up_gelu(after(a2[j], last), w_up, bias_u, f"up_gelu_{j}")
         last = gb[j]
     down_grad = outer(flat(gb), flat(dz2), "down_grad")
@@ -621,27 +882,21 @@
     w_down = after(w_down, down_grad)
 
     du, dh2, mix = [None] * CTX, [None] * CTX, [None] * CTX
-    du[far] = hidden_back(dz2[far], w_down, slope[far], "du_far")
-    dh2[far] = plain(du[far], w_up, True, half, "dh2_far")
-    first = scatter_first(dh2[far])
-    mids = hidden_back(
-        after([dz2[j][0] for j in mid], dh2[far]), w_down, [slope[j][0] for j in mid], "du_mid"
-    )
-    for j, x in zip(mid, mids):
-        du[j] = [x]
-    mids = plain(mids, w_up, True, half, "dh2_mid")
-    for j, x in zip(mid, mids):
-        dh2[j] = x
-    if first is None:
-        dh2[far] = dh2[far][0]
-    sent = scatter_second(dh2, first)
-    arrived = scatter_send(sent)
-    du[0] = hidden_back(after(dz2[0], sent), w_down, slope[0], "du_own")
-    dh2[0] = plain(du[0], w_up, True, single, "dh2_own")[0]
-    up_grad = outer(flat(a2), after(flat(du), dh2[0]), "up_grad")
+    if CTX == 4:
+        du, dh2, arrived, up_grad, mix[far] = feed_back(
+            flat(dz2), flat(slope), flat(a2), gb[far], w_down, w_up
+        )
+        du = [du]
+    else:
+        for j in range(CTX):
+            du[j] = hidden_back(dz2[j], w_down, slope[j], f"du_{j}")
+            dh2[j] = plain(du[j], w_up, True, half if j else single, f"dh2_{j}")[0]
+        arrived = scatter_send(dh2[1:])
+        dh2 = dh2[0]
+        up_grad = outer(flat(a2), flat(du), "up_grad")
+        mix[far] = plain(gb[far], w_down, False, half, "mix_far")
     up_part = scatter_f(after(up_grad, down_part))
-    mix[far] = plain(after(gb[far], up_grad), w_down, False, half, "mix_far")
-    dh2 = total_of(after(dh2[0], mix[far]), arrived)
+    dh2 = total_of(dh2, arrived)
     up_bias_grad = sum(jnp.sum(x.astype(single), axis=0) for x in flat(du))
     down_bias_grad = jnp.sum(dz2_own.astype(single), axis=0)
     gain2_grad = jnp.sum(dh2 * normed2, axis=0)
@@ -650,54 +905,42 @@
 
     dz1 = dy1.astype(half)
     dattn = dot_nt(after(dz1, down_part), w_out).astype(half)
-    dattn = xor_order([dattn[:, s * part : (s + 1) * part] for s in range(CTX)], c)
     out_bias_grad = jnp.sum(dz1.astype(single), axis=0)
-    out_grad = outer([ob], [after(dz1, dattn)], "out_grad")
-    mids = plain(after([gb[j][0] for j in mid], out_grad), w_down, False, half, "mix_mid")
-    for j, x in zip(mid, mids):
-        mix[j] = x
-    dattn = [dattn[0]] + after([swap(dattn[j], j) for j in range(1, CTX)], mids)
-    dattn = jnp.concatenate(dattn, axis=0)
+    if CTX == 4:
+        dattn, out_grad, mix[1], mix[2] = heads_back(
+            dattn, ob, dz1, gb[1][0], gb[2][0], w_down, part
+        )
+    else:
+        dattn = xor_order([dattn[:, s * part : (s + 1) * part] for s in range(CTX)], c)
+        dattn = [dattn[0]] + [swap(dattn[j], j) for j in range(1, CTX)]
+        dattn = jnp.concatenate(dattn, axis=0)
+        out_grad = outer([ob], [dz1], "out_grad")
+        for j in mid:
+            mix[j] = plain(gb[j], w_down, False, half, f"mix_{j}")[0]
     dqkv = attn_backward(joined, dattn, inv, slopes, heads, scale)
     down_own = after(down_part, dattn)
     down_near = gather_first(down_own)
     dqkv = to_rows(jnp.concatenate(after(dqkv, down_near), axis=1))
-    down_out = gather_second(down_own, down_near)
-    dh1 = [None] * CTX
     if CTX == 4:
-        dh1[far] = [(dqkv, rows // 2, 2 * far), (dqkv, rows // 2, 2 * far + 1)]
+        dh1, arrived, qkv_grad, mix[0] = qkv_back(dqkv, w_qkv, a1, gb[0][0], w_down)
     else:
-        dh1[far] = [(dqkv, rows, far)]
-    dh1[far] = plain(dh1[far], w_qkv, True, half, "dh1_far")
-    first = scatter_first(dh1[far])
-    if first is None:
-        dh1[far] = dh1[far][0]
-    dqkv = after(dqkv, dh1[far])
-    mids = plain([(dqkv, rows, j) for j in mid], w_qkv, True, half, "dh1_mid")
-    for j, x in zip(mid, mids):
-        dh1[j] = x
-    dqkv = after(dqkv, up_part, down_out, mids)
-    dh1[0] = plain([(dqkv, rows, 0)], w_qkv, True, single, "dh1_own")[0]
-    mix[0] = plain(after(gb[0], dh1[0]), w_down, False, single, "mix_own")[0]
-    if first is not None:
-        first = after(first, mix[0])
-    sent = scatter_second(dh1, first)
-    arrived = scatter_send(sent)
-    dqkv = after(dqkv, sent)
-    a1_rows = [block_of(x)[1] for x in a1]
-    qkv_grad = outer(
-        a1,
-        [(dqkv, r, sum(a1_rows[:i]) // r) for i, r in enumerate(a1_rows)],
-        "qkv_grad",
-    )
-    dh1 = total_of(after(dh1[0], qkv_grad), arrived)
-    out_part = scatter_f(after(out_grad, up_part))
+        dh1 = [
+            plain([(dqkv, rows, j)], w_qkv, True, half if j else single, f"dh1_{j}")[0]
+            for j in range(CTX)
+        ]
+        arrived = scatter_send(dh1[1:])
+        dh1 = dh1[0]
+        qkv_grad = outer(a1, [(dqkv, rows, j) for j in range(CTX)], "qkv_grad")
+        mix[0] = plain(gb[0], w_down, False, single, "mix_0")[0]
+    dh1 = total_of(dh1, arrived)
+    out_part = scatter_f(after(out_grad, up_part, dqkv))
     qkv_part = scatter_f(after(qkv_grad, out_part))
     mix = after(mix, dh1)
     first = scatter_first(mix[far])
     if first is None:
         mix[far] = mix[far][0]
     mixed = total_of(y1 + bias_d + mix[0], scatter_send(scatter_second(mix, first)))
+    down_out = gather_second(down_own, after(down_near, dh1))
     down_out = lay_out(0, down_out, c, width // min(width, 512))
     up_out = lay_out(1, gather_ctx(after(up_part, dh1)), c, nf)
     sums = jnp.sum(dqkv.astype(single), axis=0)

time: 957 us -> 875 us (0.914)
  the two profiles are of different devices: /device:TPU:8 before, /device:TPU:0 now
where the time goes in v5:
time: 875 us; the launch traced here: 864 us
  Pallas kernels  434 us (50%)
  waiting for transfers between devices  202 us (23%)
  other arithmetic  86.2 us (10%)
  local copies, waits for them, and re-layouts  60.9 us (7%)
  starting transfers between devices  41.7 us (5%)
  between operations  25.8 us (3%)
  matrix products  13.6 us (2%)
    pallas_call x2, Pallas kernels, moving_call(): pl.pallas_call(kernel, in_specs=[anywhere] * len(operands), out_specs=[an...  192 us
    ppermute x33, waiting for transfers between devices, swap(): return lax.ppermute(x, 'ctx', [(i, i ^ mask) for i in range(n)])  190 us
    pallas_call x5, Pallas kernels, rows_matmul(): pl.pallas_call(functools.partial(rows_kernel, dot_nt if transposed else d...  74 us
    ppermute x33, starting transfers between devices, swap(): return lax.ppermute(x, 'ctx', [(i, i ^ mask) for i in range(n)])  41.1 us
    unnamed x163, local copies, waits for them, and re-layouts  36.6 us
    pallas_call x1, Pallas kernels, attn_backward(): pl.pallas_call(functools.partial(attn_bwd_kernel, scale), grid_spec=pltpu...  35.2 us
    pallas_call x1, Pallas kernels, reduce_small(): pl.pallas_call(functools.partial(reduce_small_kernel, nf, nc), out_shape=...  34.9 us
    pallas_call x1, Pallas kernels, heads_back(): pl.pallas_call(functools.partial(heads_back_kernel, part), in_specs=[anyw...  26.7 us
  transfers between devices with their start and end apart: 41, of which 18 were waited for; matrix products, arithmetic and copies ran while one was open for 17% of the time, Pallas kernels for 50%

profile of v5, /device:TPU:0, one launch (start us, length us, event | category | flops | bytes accessed | tf_op | source)
XLA Modules:
  0.0 864.3 jit_solution(6757273340301380689)
XLA Ops:
  18.1 9.1 %gather_small.1 = f32[8,24,128]{2,1,0:T(8,128)} custom-call(f32[24,128]{1,0:T(8,128)} %bitcast.98), custom_call_target="tpu_custom_call" | custom-call | tf_op jit(solution)/shard_map/gather_small/pallas_call | solution.py:670
  43.1 18.4 %collective-permute-done = bf16[512,2048]{1,0:T(8,128)(2,1)} collective-permute-done((bf16[512,2048]{1,0:T(8,128)(2,1)S(1)}, bf16[512,2048]{1,0:T(8,128)(2,1)}, u32[]{:S(2)}, u32[]{:S(2)}) %collective-permute-start) | collective-permute-done | bytes 2097184 | tf_op jit(solution)/shard_map/ppermute | solution.py:60
  75.3 5.8 fusion.21
  81.0 8.4 collective-permute-done.3
  99.8 19.1 %qkv.1.refs_0_.refs_1_.refs_2_.refs_3_.refs_4_.refs_5_.refs_6_.refs_7_.refs_8_.refs_9_.refs_10_.refs_11_.refs_12_.refs_13_.refs_14_.refs_15_.refs_16_.refs_17_.refs_18_.refs_19_.refs_20_.refs_21_.refs_22_.refs_23_ = bf16[2048,1536]{1,0:T(8,128)(2,1)} custom-call(bf16[512,2048]{1,0:T(8,128)(2,1)} %get-tuple-element.207.refs_0_.refs_2_, ...), custom_call_target="tpu_custom_call" | custom-call | flops 12884901 | bytes 35651 | tf_op jit(solution)/shard_map/qkv/pallas_call | solution.py:252
  119.2 4.5 convert_reduce_fusion.7
  137.6 23.6 %attn_forward.1 = bf16[2048,512]{1,0:T(8,128)(2,1)S(1)} custom-call(s32[16]{0:T(128)S(1)} %select_reduce_fusion.inv_ref, f32[4]{0:T(128)S(1)} %multiply_power_fusion.slope_ref, ...), custom_call_target="tpu_custom_call" | custom-call | flops 20000000 | bytes 8388 | tf_op jit(solution)/shard_map/attn_forward/pallas_call | solution.py:188
  164.0 5.7 collective-permute-done.5.refs_7_.refs_2_
  174.2 12.5 %collective-permute-done.6 = bf16[512,512]{1,0:T(8,128)(2,1)S(1)} collective-permute-done((bf16[512,512]{1,0:T(8,128)(2,1)}, bf16[512,512]{1,0:T(8,128)(2,1)S(1)}, u32[]{:S(2)}, u32[]{:S(2)}) %collective-permute-start.6) | collective-permute-done | bytes 524320 | tf_op jit(solution)/shard_map/ppermute | solution.py:60
  186.7 6.9 collective-permute-done.7
  196.5 7.9 fusion.53
  208.5 45.3 %collective-permute-done.12.refs_0_.refs_12_ = bf16[512,2048]{1,0:T(8,128)(2,1)S(1)} collective-permute-done((bf16[512,2048]{1,0:T(8,128)(2,1)S(1)}, bf16[512,2048]{1,0:T(8,128)(2,1)S(1)}, u32[]{:S(2)}, u32[]{:S(2)}) %collective-permute-start.12) | collective-permute-done | bytes 2097184 | tf_op jit(solution)/shard_map/ppermute | solution.py:60
  267.1 10.9 %up_gelu_0.1 = (bf16[512,2048]{1,0:T(8,128)(2,1)}, bf16[512,2048]{1,0:T(8,128)(2,1)}) custom-call(bf16[512,2048]{1,0:T(8,128)(2,1)} %copy-done.15, bf16[2048,2048]{1,0:T(8,128)(2,1)} %all-gather.9.cloned.1.call-done.refs_1_.refs_2_.refs_18_, f32[1,2048]{1,0:T(1,128)S(1)} %bitcast.77), custom_call_target="tpu_custom_call" | custom-call | flops 4294967 | bytes 16777 | tf_op jit(solution)/shard_map/up_gelu_0/pallas_call | solution.py:252
  278.0 10.8 %up_gelu_1.1 = (bf16[512,2048]{1,0:T(8,128)(2,1)}, bf16[512,2048]{1,0:T(8,128)(2,1)}) custom-call(bf16[512,2048]{1,0:T(8,128)(2,1)} %copy-done.20, bf16[2048,2048]{1,0:T(8,128)(2,1)} %all-gather.9.cloned.1.call-done.refs_1_.refs_2_.refs_18_, f32[1,2048]{1,0:T(1,128)S(1)} %bitcast.78), custom_call_target="tpu_custom_call" | custom-call | flops 4294967 | bytes 16777 | tf_op jit(solution)/shard_map/up_gelu_1/pallas_call | solution.py:252
  288.7 10.8 %up_gelu_2.1 = (bf16[512,2048]{1,0:T(8,128)(2,1)}, bf16[512,2048]{1,0:T(8,128)(2,1)}) custom-call(bf16[512,2048]{1,0:T(8,128)(2,1)} %copy-done.19, bf16[2048,2048]{1,0:T(8,128)(2,1)} %all-gather.9.cloned.1.call-done.refs_1_.refs_2_.refs_18_, f32[1,2048]{1,0:T(1,128)S(1)} %bitcast.79), custom_call_target="tpu_custom_call" | custom-call | flops 4294967 | bytes 16777 | tf_op jit(solution)/shard_map/up_gelu_2/pallas_call | solution.py:252
  300.6 22.5 %up_gelu_3.1 = (bf16[256,2048]{1,0:T(8,128)(2,1)S(1)}, bf16[256,2048]{1,0:T(8,128)(2,1)}, bf16[256,2048]{1,0:T(8,128)(2,1)}, bf16[256,2048]{1,0:T(8,128)(2,1)}) custom-call(bf16[256,2048]{1,0:T(8,128)(2,1)} %collective-permute-done.13.refs_0_.refs_13_, bf16[256,2048]{1,0:T(8,128)(2,1)} %copy-done.23, ...), custom_call_target="tpu_custom_call" | custom-call | flops 4294967 | bytes 16777 | tf_op jit(solution)/shard_map/up_gelu_3/pallas_call | solution.py:252
  323.1 23.4 %down_grad.1 = bf16[2048,2048]{1,0:T(8,128)(2,1)} custom-call(bf16[512,2048]{1,0:T(8,128)(2,1)} %get-tuple-element.102.refs_0_.refs_7_, bf16[512,2048]{1,0:T(8,128)(2,1)} %get-tuple-element.105.refs_1_.refs_3_, bf16[512,2048]{1,0:T(8,128)(2,1)} %get-tuple-element.108.refs_2_.refs_4_, bf16[256,2048]{1,0:T(8,128)(2,1)S(1)} %get-tuple-element.113.refs_3_.refs_15_, ...), custom_call_target="tpu_custom_call" | custom-call | flops 17179868 | bytes 25165 | tf_op jit(solution)/shard_map/down_grad/pallas_call | solution.py:325
  346.7 114.1 %feed_back.1 = (bf16[512,2048]{1,0:T(8,128)(2,1)}, bf16[512,2048]{1,0:T(8,128)(2,1)}, bf16[512,2048]{1,0:T(8,128)(2,1)}, bf16[256,2048]{1,0:T(8,128)(2,1)S(1)}, ...) custom-call(bf16[512,2048]{1,0:T(8,128)(2,1)} %get-tuple-element.166, ...), custom_call_target="tpu_custom_call" | custom-call | flops 55834576 | tf_op jit(solution)/shard_map/feed_back/pallas_call | solution.py:434
  462.4 6.0 multiply_reduce_fusion
  473.2 5.7 convolution_convert_fusion.refs_0_
  478.9 26.7 %heads_back.1 = (bf16[2048,512]{1,0:T(8,128)(2,1)}, bf16[2048,2048]{1,0:T(8,128)(2,1)}, bf16[512,2048]{1,0:T(8,128)(2,1)}, bf16[512,2048]{1,0:T(8,128)(2,1)}) custom-call(bf16[512,2048]{1,0:T(8,128)(2,1)} %convolution_convert_fusion.refs_0_, bf16[512,2048]{1,0:T(8,128)(2,1)} %pad_maximum_fusion.refs_1_, bf16[512,2048]{1,0:T(8,128)(2,1)} %copy-done.22, ...), custom_call_target="tpu_custom_call" | custom-call | flops 21474836 | tf_op jit(solution)/shard_map/heads_back/pallas_call | solution.py:530
  507.4 35.2 %attn_backward.1 = (bf16[2048,512]{1,0:T(8,128)(2,1)S(1)}, bf16[2048,512]{1,0:T(8,128)(2,1)S(1)}, bf16[2048,512]{1,0:T(8,128)(2,1)}) custom-call(s32[16]{0:T(128)S(1)} %select_reduce_fusion.inv_ref, f32[4]{0:T(128)S(1)} %multiply_power_fusion.slope_ref, ...), custom_call_target="tpu_custom_call" | custom-call | flops 40000000 | bytes 14680 | tf_op jit(solution)/shard_map/attn_backward/pallas_call | solution.py:205
  556.8 78.2 %qkv_back.1 = (f32[512,2048]{1,0:T(8,128)}, bf16[512,2048]{1,0:T(8,128)(2,1)}, bf16[512,2048]{1,0:T(8,128)(2,1)}, bf16[512,2048]{1,0:T(8,128)(2,1)}, bf16[256,20...) custom-call(bf16[2048,1536]{1,0:T(8,128)(2,1)} %dynamic-slice_dynami, ...), custom_call_target="tpu_custom_call" | custom-call | flops 30064772 | tf_op jit(solution)/shard_map/qkv_back/pallas_call | solution.py:434
  635.1 11.8 %reduce-scatter.9.cloned.1.call-done = bf16[256,2048]{1,0:T(8,128)(2,1)} async-done(((bf16[2048,2048]{1,0:T(8,128)(2,1)}), bf16[256,2048]{1,0:T(8,128)(2,1)}) %reduce-scatter.9.cloned.1.call-update) | async-done | bytes 1048592 | tf_op jit(solution)/shard_map/reduce_scatter | solution.py:845
  650.9 5.8 fusion.16
  667.1 16.0 %collective-permute-done.19 = bf16[256,2048]{1,0:T(8,128)(2,1)S(1)} collective-permute-done((bf16[256,2048]{1,0:T(8,128)(2,1)}, bf16[256,2048]{1,0:T(8,128)(2,1)S(1)}, u32[]{:S(2)}, u32[]{:S(2)}) %collective-permute-start.19) | collective-permute-done | bytes 1048608 | tf_op jit(solution)/shard_map/ppermute | solution.py:60
  703.6 41.4 %collective-permute-done.25.refs_3_ = bf16[128,2048]{1,0:T(8,128)(2,1)S(1)} collective-permute-done((bf16[128,2048]{1,0:T(8,128)(2,1)S(1)}, bf16[128,2048]{1,0:T(8,128)(2,1)S(1)}, u32[]{:S(2)}, u32[]{:S(2)}) %collective-permute-start.25) | collective-permute-done | bytes 524320 | tf_op jit(solution)/shard_map/ppermute | solution.py:60
  755.1 8.4 collective-permute-done.22.refs_2_
  766.8 6.0 convert_add_fusion.1
  772.8 19.2 %collective-permute-done.24.refs_4_ = bf16[128,2048]{1,0:T(8,128)(2,1)S(1)} collective-permute-done((bf16[128,2048]{1,0:T(8,128)(2,1)S(1)}, bf16[128,2048]{1,0:T(8,128)(2,1)S(1)}, u32[]{:S(2)}, u32[]{:S(2)}) %collective-permute-start.24) | collective-permute-done | bytes 524320 | tf_op jit(solution)/shard_map/ppermute | solution.py:60
  792.0 6.9 lay_out.3
  806.1 34.9 %reduce_small.1 = f32[24,128]{1,0:T(8,128)} custom-call(f32[8,24,128]{2,1,0:T(8,128)} %bitcast.83), custom_call_target="tpu_custom_call" | custom-call | tf_op jit(solution)/shard_map/reduce_small/pallas_call | solution.py:741
  (356 shorter events, 176.6 us)
Async XLA Ops:
  7.3 92.5 %all-gather.5.cloned.1.call-start = ((), (), s32[]{:S(2)}) async-start(), calls=%async_computation.4 | async-start | bytes 7077888 | tf_op jit(solution)/shard_map/all_gather | solution.py:805
  9.9 186.6 %all-gather.7.cloned.1.call-start = ((), (), s32[]{:S(2)}) async-start(), calls=%async_computation.5 | async-start | bytes 9437184 | tf_op jit(solution)/shard_map/all_gather | solution.py:805
  12.7 254.4 %all-gather.9.cloned.1.call-start = ((), (), s32[]{:S(2)}) async-start(), calls=%async_computation.6 | async-start | bytes 9437184 | tf_op jit(solution)/shard_map/all_gather | solution.py:805
  12.7 48.7 %collective-permute-start = (bf16[512,2048]{1,0:T(8,128)(2,1)S(1)}, bf16[512,2048]{1,0:T(8,128)(2,1)}, u32[]{:S(2)}, u32[]{:S(2)}) collective-permute-start(bf16[512,2048]{1,0:T(8,128)(2,1)S(1)} %copy-done.12), channel_id=1, source_target_pairs={{0,8},{8,0},{16,24},{24,16},{1,9},{9,1},{17,25},{25,17},{2,10},{10... | collective-permute-start | bytes 6291464 | tf_op jit(solution)/shard_map/ppermute | solution.py:60
  15.7 47.2 %collective-permute-start.1 = (bf16[512,2048]{1,0:T(8,128)(2,1)S(1)}, bf16[512,2048]{1,0:T(8,128)(2,1)}, u32[]{:S(2)}, u32[]{:S(2)}) collective-permute-start(bf16[512,2048]{1,0:T(8,128)(2,1)S(1)} %copy-done.12), channel_id=1, source_target_pairs={{0,16},{8,24},{16,0},{24,8},{1,17},{9,25},{17,1},{25,9},{2,18},{10... | collective-permute-start | bytes 6291464 | tf_op jit(solution)/shard_map/ppermute | solution.py:60
  89.9 256.7 %all-gather.11.cloned.1.call-start = ((), (), s32[]{:S(2)}) async-start(), calls=%async_computation.7 | async-start | bytes 9437184 | tf_op jit(solution)/shard_map/all_gather | solution.py:805
  118.9 341.9 %reduce-scatter.5.cloned.1.call-start = ((), (), s32[]{:S(2)}) async-start(), calls=%async_computation.8 | async-start | bytes 9437184 | tf_op jit(solution)/shard_map/reduce_scatter | solution.py:845
  123.7 46.0 %collective-permute-start.5 = (bf16[512,2048]{1,0:T(8,128)(2,1)}, bf16[512,2048]{1,0:T(8,128)(2,1)}, u32[]{:S(2)}, u32[]{:S(2)}) collective-permute-start(bf16[512,2048]{1,0:T(8,128)(2,1)} %get-tuple-element.166.refs_5_.refs_0_), channel_id=1, source_target_pairs={{0,16},{8,24},{16,0},{24,8},{1,17},{9,25},{17,1},{25,9},{2,18},{10... | collective-permute-start | bytes 6291464 | tf_op jit(solution)/shard_map/ppermute | solution.py:60
  125.2 45.5 %collective-permute-start.4 = (bf16[512,2048]{1,0:T(8,128)(2,1)}, bf16[512,2048]{1,0:T(8,128)(2,1)}, u32[]{:S(2)}, u32[]{:S(2)}) collective-permute-start(bf16[512,2048]{1,0:T(8,128)(2,1)} %get-tuple-element.166.refs_5_.refs_0_), channel_id=1, source_target_pairs={{0,8},{8,0},{16,24},{24,16},{1,9},{9,1},{17,25},{25,17},{2,10},{10... | collective-permute-start | bytes 6291464 | tf_op jit(solution)/shard_map/ppermute | solution.py:60
  206.4 47.4 %collective-permute-start.12 = (bf16[512,2048]{1,0:T(8,128)(2,1)S(1)}, bf16[512,2048]{1,0:T(8,128)(2,1)S(1)}, u32[]{:S(2)}, u32[]{:S(2)}) collective-permute-start(bf16[512,2048]{1,0:T(8,128)(2,1)S(1)} %add_convert_fusion.refs_0_.refs_10_), channel_id=1, source_target_pairs={{0,16},{8,24},{16,0},{24,8},{1,17},{9,25},{17,1},{25,9},{2,18},{10... | collective-permute-start | bytes 6291464 | tf_op jit(solution)/shard_map/ppermute | solution.py:60
  207.5 48.7 %collective-permute-start.11 = (bf16[512,2048]{1,0:T(8,128)(2,1)S(1)}, bf16[512,2048]{1,0:T(8,128)(2,1)S(1)}, u32[]{:S(2)}, u32[]{:S(2)}) collective-permute-start(bf16[512,2048]{1,0:T(8,128)(2,1)S(1)} %add_convert_fusion.refs_0_.refs_10_), channel_id=1, source_target_pairs={{0,8},{8,0},{16,24},{24,16},{1,9},{9,1},{17,25},{25,17},{2,10},{10... | collective-permute-start | bytes 6291464 | tf_op jit(solution)/shard_map/ppermute | solution.py:60
  254.9 44.6 %collective-permute-start.14 = (bf16[256,2048]{1,0:T(8,128)(2,1)}, bf16[256,2048]{1,0:T(8,128)(2,1)S(1)}, u32[]{:S(2)}, u32[]{:S(2)}) collective-permute-start(bf16[256,2048]{1,0:T(8,128)(2,1)} %slice.296), channel_id=1, source_target_pairs={{0,8},{8,0},{16,24},{24,16},{1,9},{9,1},{17,25},{25,17},{2,10},{10... | collective-permute-start | bytes 3145736 | tf_op jit(solution)/shard_map/ppermute | solution.py:60
  257.9 41.6 %collective-permute-start.13 = (bf16[256,2048]{1,0:T(8,128)(2,1)}, bf16[256,2048]{1,0:T(8,128)(2,1)}, u32[]{:S(2)}, u32[]{:S(2)}) collective-permute-start(bf16[256,2048]{1,0:T(8,128)(2,1)} %slice.295), channel_id=1, source_target_pairs={{0,16},{8,24},{16,0},{24,8},{1,17},{9,25},{17,1},{25,9},{2,18},{10... | collective-permute-start | bytes 3145736 | tf_op jit(solution)/shard_map/ppermute | solution.py:60
  265.1 58.0 %collective-permute-start.10 = (bf16[256,2048]{1,0:T(8,128)(2,1)}, bf16[256,2048]{1,0:T(8,128)(2,1)}, u32[]{:S(2)}, u32[]{:S(2)}) collective-permute-start(bf16[256,2048]{1,0:T(8,128)(2,1)} %slice.248), channel_id=1, source_target_pairs={{0,8},{8,0},{16,24},{24,16},{1,9},{9,1},{17,25},{25,17},{2,10},{10... | collective-permute-start | bytes 3145736 | tf_op jit(solution)/shard_map/ppermute | solution.py:60
  266.2 56.9 %collective-permute-start.9 = (bf16[256,2048]{1,0:T(8,128)(2,1)}, bf16[256,2048]{1,0:T(8,128)(2,1)}, u32[]{:S(2)}, u32[]{:S(2)}) collective-permute-start(bf16[256,2048]{1,0:T(8,128)(2,1)} %slice.247), channel_id=1, source_target_pairs={{0,16},{8,24},{16,0},{24,8},{1,17},{9,25},{17,1},{25,9},{2,18},{10... | collective-permute-start | bytes 3145736 | tf_op jit(solution)/shard_map/ppermute | solution.py:60
  346.6 210.2 %reduce-scatter.7.cloned.1.call-start = ((), (), s32[]{:S(2)}) async-start(), calls=%async_computation.9 | async-start | bytes 9437184 | tf_op jit(solution)/shard_map/reduce_scatter | solution.py:845
  460.8 186.1 %reduce-scatter.9.cloned.1.call-start = ((), (), s32[]{:S(2)}) async-start(), calls=%async_computation.10 | async-start | bytes 9437184 | tf_op jit(solution)/shard_map/reduce_scatter | solution.py:845
  505.7 37.0 %collective-permute-start.16 = (bf16[256,2048]{1,0:T(8,128)(2,1)S(1)}, bf16[256,2048]{1,0:T(8,128)(2,1)S(1)}, u32[]{:S(2)}, u32[]{:S(2)}) collective-permute-start(bf16[256,2048]{1,0:T(8,128)(2,1)S(1)} %copy-done.2), channel_id=1, source_target_pairs={{0,16},{8,24},{16,0},{24,8},{1,17},{9,25},{17,1},{25,9},{2,18},{10... | collective-permute-start | bytes 3145736 | tf_op jit(solution)/shard_map/ppermute | solution.py:60
  506.5 36.2 %collective-permute-start.15 = (bf16[256,2048]{1,0:T(8,128)(2,1)S(1)}, bf16[256,2048]{1,0:T(8,128)(2,1)S(1)}, u32[]{:S(2)}, u32[]{:S(2)}) collective-permute-start(bf16[256,2048]{1,0:T(8,128)(2,1)S(1)} %copy-done.2), channel_id=1, source_target_pairs={{0,8},{8,0},{16,24},{24,16},{1,9},{9,1},{17,25},{25,17},{2,10},{10... | collective-permute-start | bytes 3145736 | tf_op jit(solution)/shard_map/ppermute | solution.py:60
  556.8 246.6 %reduce-scatter.11.cloned.1.call-start = ((), (), s32[]{:S(2)}) async-start(), calls=%async_computation.11 | async-start | bytes 7077888 | tf_op jit(solution)/shard_map/reduce_scatter | solution.py:845
  663.8 30.5 %collective-permute-start.26 = (bf16[128,2048]{1,0:T(8,128)(2,1)S(1)}, bf16[128,2048]{1,0:T(8,128)(2,1)S(1)}, u32[]{:S(2)}, u32[]{:S(2)}) collective-permute-start(bf16[128,2048]{1,0:T(8,128)(2,1)S(1)} %slice.261), channel_id=1, source_target_pairs={{0,8},{8,0},{16,24},{24,16},{1,9},{9,1},{17,25},{25,17},{2,10},{10... | collective-permute-start | bytes 1572872 | tf_op jit(solution)/shard_map/ppermute | solution.py:60
  685.0 81.8 %collective-permute-start.20 = (bf16[512,2048]{1,0:T(8,128)(2,1)}, bf16[512,2048]{1,0:T(8,128)(2,1)}, u32[]{:S(2)}, u32[]{:S(2)}) collective-permute-start(bf16[512,2048]{1,0:T(8,128)(2,1)} %pad_maximum_fusion.2), channel_id=1, source_target_pairs={{0,16},{8,24},{16,0},{24,8},{1,17},{9,25},{17,1},{25,9},{2,18},{10... | collective-permute-start | bytes 6291464 | tf_op jit(solution)/shard_map/ppermute | solution.py:60
  691.6 75.2 %collective-permute-start.18 = (bf16[512,2048]{1,0:T(8,128)(2,1)}, bf16[512,2048]{1,0:T(8,128)(2,1)}, u32[]{:S(2)}, u32[]{:S(2)}) collective-permute-start(bf16[512,2048]{1,0:T(8,128)(2,1)} %pad_maximum_fusion.1), channel_id=1, source_target_pairs={{0,8},{8,0},{16,24},{24,16},{1,9},{9,1},{17,25},{25,17},{2,10},{10... | collective-permute-start | bytes 6291464 | tf_op jit(solution)/shard_map/ppermute | solution.py:60
  692.0 53.0 %collective-permute-start.25 = (bf16[128,2048]{1,0:T(8,128)(2,1)S(1)}, bf16[128,2048]{1,0:T(8,128)(2,1)S(1)}, u32[]{:S(2)}, u32[]{:S(2)}) collective-permute-start(bf16[128,2048]{1,0:T(8,128)(2,1)S(1)} %slice.260), channel_id=1, source_target_pairs={{0,16},{8,24},{16,0},{24,8},{1,17},{9,25},{17,1},{25,9},{2,18},{10... | collective-permute-start | bytes 1572872 | tf_op jit(solution)/shard_map/ppermute | solution.py:60
  693.6 70.0 %collective-permute-start.22 = (bf16[256,2048]{1,0:T(8,128)(2,1)}, bf16[256,2048]{1,0:T(8,128)(2,1)S(1)}, u32[]{:S(2)}, u32[]{:S(2)}) collective-permute-start(bf16[256,2048]{1,0:T(8,128)(2,1)} %reduce-scatter.7.cloned.1.call-done.refs_0_), channel_id=1, source_target_pairs={{0,16},{8,24},{16,0},{24,8},{1,17},{9,25},{17,1},{25,9},{2,18},{10... | collective-permute-start | bytes 3145736 | tf_op jit(solution)/shard_map/ppermute | solution.py:60
  695.1 69.1 %collective-permute-start.21 = (bf16[256,2048]{1,0:T(8,128)(2,1)}, bf16[256,2048]{1,0:T(8,128)(2,1)}, u32[]{:S(2)}, u32[]{:S(2)}) collective-permute-start(bf16[256,2048]{1,0:T(8,128)(2,1)} %reduce-scatter.7.cloned.1.call-done.refs_0_), channel_id=1, source_target_pairs={{0,8},{8,0},{16,24},{24,16},{1,9},{9,1},{17,25},{25,17},{2,10},{10... | collective-permute-start | bytes 3145736 | tf_op jit(solution)/shard_map/ppermute | solution.py:60
  745.8 53.2 %collective-permute-start.31 = (bf16[256,2048]{1,0:T(8,128)(2,1)}, bf16[256,2048]{1,0:T(8,128)(2,1)}, u32[]{:S(2)}, u32[]{:S(2)}) collective-permute-start(bf16[256,2048]{1,0:T(8,128)(2,1)} %reduce-scatter.9.cloned.1.call-done), channel_id=1, source_target_pairs={{0,8},{8,0},{16,24},{24,16},{1,9},{9,1},{17,25},{25,17},{2,10},{10... | collective-permute-start | bytes 3145736 | tf_op jit(solution)/shard_map/ppermute | solution.py:60
  763.6 28.4 %collective-permute-start.24 = (bf16[128,2048]{1,0:T(8,128)(2,1)S(1)}, bf16[128,2048]{1,0:T(8,128)(2,1)S(1)}, u32[]{:S(2)}, u32[]{:S(2)}) collective-permute-start(bf16[128,2048]{1,0:T(8,128)(2,1)S(1)} %slice.298), channel_id=1, source_target_pairs={{0,8},{8,0},{16,24},{24,16},{1,9},{9,1},{17,25},{25,17},{2,10},{10... | collective-permute-start | bytes 1572872 | tf_op jit(solution)/shard_map/ppermute | solution.py:60
  765.3 26.8 %collective-permute-start.23 = (bf16[128,2048]{1,0:T(8,128)(2,1)S(1)}, bf16[128,2048]{1,0:T(8,128)(2,1)S(1)}, u32[]{:S(2)}, u32[]{:S(2)}) collective-permute-start(bf16[128,2048]{1,0:T(8,128)(2,1)S(1)} %slice.297), channel_id=1, source_target_pairs={{0,16},{8,24},{16,0},{24,8},{1,17},{9,25},{17,1},{25,9},{2,18},{10... | collective-permute-start | bytes 1572872 | tf_op jit(solution)/shard_map/ppermute | solution.py:60
  801.9 46.0 %collective-permute-start.32 = (bf16[256,2048]{1,0:T(8,128)(2,1)}, bf16[256,2048]{1,0:T(8,128)(2,1)}, u32[]{:S(2)}, u32[]{:S(2)}) collective-permute-start(bf16[256,2048]{1,0:T(8,128)(2,1)} %add_convert_fusion.1), channel_id=1, source_target_pairs={{0,16},{8,24},{16,0},{24,8},{1,17},{9,25},{17,1},{25,9},{2,18},{10... | collective-permute-start | bytes 3145736 | tf_op jit(solution)/shard_map/ppermute | solution.py:60
  803.4 40.4 %collective-permute-start.28 = (bf16[256,1536]{1,0:T(8,128)(2,1)}, bf16[256,1536]{1,0:T(8,128)(2,1)S(1)}, u32[]{:S(2)}, u32[]{:S(2)}) collective-permute-start(bf16[256,1536]{1,0:T(8,128)(2,1)} %reduce-scatter.11.cloned.1.call-done.refs_0_), channel_id=1, source_target_pairs={{0,16},{8,24},{16,0},{24,8},{1,17},{9,25},{17,1},{25,9},{2,18},{10... | collective-permute-start | bytes 2359304 | tf_op jit(solution)/shard_map/ppermute | solution.py:60
  804.0 42.3 %collective-permute-start.27 = (bf16[256,1536]{1,0:T(8,128)(2,1)}, bf16[256,1536]{1,0:T(8,128)(2,1)S(1)}, u32[]{:S(2)}, u32[]{:S(2)}) collective-permute-start(bf16[256,1536]{1,0:T(8,128)(2,1)} %reduce-scatter.11.cloned.1.call-done.refs_0_), channel_id=1, source_target_pairs={{0,8},{8,0},{16,24},{24,16},{1,9},{9,1},{17,25},{25,17},{2,10},{10... | collective-permute-start | bytes 2359304 | tf_op jit(solution)/shard_map/ppermute | solution.py:60
  (66 other events, 1038.2 us)
Sparse Core Ops, SparseCore 0:
  10.3 68.1 all-gather.4
  80.7 80.6 all-gather.6
  163.0 80.5 all-gather.8
  245.1 80.5 all-gather.10
  346.7 89.6 reduce-scatter.4
  460.9 89.6 reduce-scatter.6
  556.9 89.9 reduce-scatter.8
  649.2 68.1 reduce-scatter.10
